TPU v7x, 32 devices: a whole 2x2x4 slice. The times are simulated.
32 devices in a mesh: groups: 2 (over y), ep: 4 (over x, core), dp: 4 (over z).
Axes of the slice: x: 2, y: 2, z: 4, core: 2. Of those that a mesh axis runs over, the one named last changes fastest.
Arguments:
- tokens: bfloat16 [1024, 2048], P(('groups', 'ep', 'dp')), parts along dimension 0, may hold values from -6 to 6
- expert_ids: int32 [1024, 8], P(('groups', 'ep', 'dp')), parts along dimension 0, may hold values from 0 to 15, as said below
- route_w: float32 [1024, 8], P(('groups', 'ep', 'dp')), parts along dimension 0, may hold values from 0.1 to 0.5
- hot_list: int32 [8], P('groups'), parts along dimension 0, may hold values from 0 to 15, as said below
- slot_of: int32 [16], replicated, may hold values from 0 to 15, each once
- cold_gate_up: bfloat16 [16, 2048, 1536], P(('ep', 'dp')), may hold values from -0.125 to 0.125
- cold_down: bfloat16 [16, 768, 2048], P(('ep', 'dp')), may hold values from -0.21875 to 0.21875
- hot_weights: bfloat16 [4, 3, 2048, 768], P('dp', None, None, 'ep'), may hold values from -0.125 to 0.125
Outputs:
- mixed: bfloat16 [1024, 2048], P(('groups', 'ep', 'dp')), parts along dimension 0
There are 2 independent parts, one for each index of `groups`. A program takes and returns all parts, laid end to end along the dimension named above; an argument that names none is the same for every part. Nothing has to cross between parts.
Inputs may be any that keep to these rules, and one draw needn't show every extreme that they name: `expert_ids`: each row names 8 different experts. Among the rows of one device, each expert of hot_list is named by exactly 32 rows, every other expert by at most 11 rows, and one expert outside hot_list is named by exactly 11 rows of every device. `hot_list`: 4 different expert numbers.
All inputs are finite; a program needn't handle non-finite values.
Results may differ from a plain program's by a relative error of at most 0.0057.
Values may be sent and summed in bfloat16 or wider, within the bound.
No kernel may reach another device: no remote copies, remote signals or barrier semaphores. Data moves between devices by JAX's collectives and lax.ppermute only.
A program may use at most 64 MiB of HBM per device.

v0:
```python
import jax
import jax.numpy as jnp
from jax import lax
from jax.sharding import PartitionSpec as P


def swiglu_rows(inputs, gate_up, down_proj):
    in_shape = inputs.shape
    flat_in = inputs.reshape(-1, in_shape[-1])
    hidden_width = down_proj.shape[0]
    both_out = jnp.dot(flat_in, gate_up, preferred_element_type=jnp.float32)
    hidden = (jax.nn.silu(both_out[:, :hidden_width]) * both_out[:, hidden_width:]).astype(
        jnp.bfloat16
    )
    result = jnp.dot(hidden, down_proj, preferred_element_type=jnp.float32)
    return result.astype(jnp.bfloat16).reshape(in_shape)


def sliced_rows(inputs, triple):
    in_shape = inputs.shape
    flat_in = inputs.reshape(-1, in_shape[-1])
    gate_out = jnp.dot(flat_in, triple[0], preferred_element_type=jnp.float32)
    up_out = jnp.dot(flat_in, triple[1], preferred_element_type=jnp.float32)
    hidden = (jax.nn.silu(gate_out) * up_out).astype(jnp.bfloat16)
    result = lax.dot_general(
        hidden, triple[2], (((1,), (1,)), ((), ())), preferred_element_type=jnp.float32
    )
    return result.reshape(in_shape)


def body(tokens, expert_ids, route_w, hot_list, slot_of, cold_gate_up, cold_down, hot_weights):
    tok_rows, model_width = tokens.shape
    top_count = expert_ids.shape[1]
    n_hot = hot_list.shape[0]
    n_exp = slot_of.shape[0]
    n_ep = lax.axis_size("ep")
    n_dp = lax.axis_size("dp")
    n_dev = n_ep * n_dp
    most_rows = 2 * tok_rows * top_count // n_exp
    spare_rows = tok_rows * top_count - n_hot * most_rows
    cold_cap = (spare_rows + n_exp - n_hot - 1) // (n_exp - n_hot)
    one_hot = expert_ids[:, :, None] == jnp.arange(n_exp, dtype=jnp.int32)[None, None, :]
    slot_ids = jnp.sum(jnp.where(one_hot, slot_of[None, None, :], 0), axis=2)
    hot_match = expert_ids[:, :, None] == hot_list[None, None, :]
    is_hot = jnp.any(hot_match, axis=2)
    hot_index = jnp.sum(
        jnp.where(hot_match, jnp.arange(n_hot, dtype=jnp.int32)[None, None, :], 0), axis=2
    )
    flat_onehot = one_hot.reshape(tok_rows * top_count, n_exp).astype(jnp.int32)
    earlier = jnp.cumsum(flat_onehot, axis=0) - flat_onehot
    rank_ids = jnp.sum(earlier * flat_onehot, axis=1).reshape(tok_rows, top_count)
    row_ids = jnp.broadcast_to(
        jnp.arange(tok_rows, dtype=jnp.int32)[:, None], (tok_rows, top_count)
    ).reshape(-1)
    cold_size = n_dev * cold_cap
    hot_size = n_hot * most_rows
    cold_target = jnp.where(is_hot, cold_size, slot_ids * cold_cap + rank_ids).reshape(-1)
    hot_target = jnp.where(is_hot, hot_index * most_rows + rank_ids, hot_size).reshape(-1)
    cold_map = jnp.full((cold_size,), tok_rows, jnp.int32).at[cold_target].set(row_ids, mode="drop")
    hot_map = jnp.full((hot_size,), tok_rows, jnp.int32).at[hot_target].set(row_ids, mode="drop")
    padded = jnp.concatenate([tokens, jnp.zeros((1, model_width), tokens.dtype)], axis=0)
    cold_send = jnp.take(padded, cold_map, axis=0).reshape(n_dev, cold_cap, model_width)
    hot_send = jnp.take(padded, hot_map, axis=0).reshape(n_hot, most_rows, model_width)
    gate_up = cold_gate_up[0]
    down_proj = cold_down[0]
    cold_back = lax.all_to_all(
        swiglu_rows(
            lax.all_to_all(cold_send, ("ep", "dp"), split_axis=0, concat_axis=0, tiled=True),
            gate_up,
            down_proj,
        ),
        ("ep", "dp"),
        split_axis=0,
        concat_axis=0,
        tiled=True,
    )
    hot_recv = lax.all_to_all(hot_send, "dp", split_axis=0, concat_axis=0, tiled=True)
    gathered = lax.all_gather(hot_recv, "ep", axis=0, tiled=True)
    own_slice = hot_weights[0]
    hot_sum = lax.psum_scatter(
        sliced_rows(gathered, own_slice), "ep", scatter_dimension=0, tiled=True
    )
    hot_back = lax.all_to_all(
        hot_sum.astype(jnp.bfloat16), "dp", split_axis=0, concat_axis=0, tiled=True
    )
    answers = jnp.concatenate(
        [cold_back.reshape(cold_size, model_width), hot_back.reshape(hot_size, model_width)], axis=0
    )
    positions = jnp.where(
        is_hot, cold_size + hot_index * most_rows + rank_ids, slot_ids * cold_cap + rank_ids
    )
    picked = jnp.take(answers, positions, axis=0)
    mixed = jnp.zeros((tok_rows, model_width), jnp.float32)
    for column in range(top_count):
        mixed = mixed + route_w[:, column, None] * picked[:, column].astype(jnp.float32)
    return mixed.astype(jnp.bfloat16)


def solution(mesh):
    in_specs = (
        P(("groups", "ep", "dp"), None),
        P(("groups", "ep", "dp"), None),
        P(("groups", "ep", "dp"), None),
        P("groups"),
        P(),
        P(("ep", "dp"), None, None),
        P(("ep", "dp"), None, None),
        P("dp", None, None, "ep"),
    )
    out_specs = P(("groups", "ep", "dp"), None)
    return jax.shard_map(body, mesh=mesh, in_specs=in_specs, out_specs=out_specs, check_vma=False)
```

profile of v0, /device:TPU:0, one launch (start us, length us, event | category | flops | bytes accessed | tf_op | source)
XLA Modules:
  0.0 186.6 jit_solution(3161920943817977532)
XLA Ops:
  6.5 0.9 copy.29
  7.6 0.8 fusion.27
  10.0 0.8 select_reduce_fusion
  11.5 1.4 scatter_custom_fusion.1
  13.1 0.9 concatenate.6
  14.0 1.7 gather_fusion.1
  15.7 1.2 broadcast_select_fusion.1
  16.9 20.7 %all_to_all.20 = bf16[4,32,2048]{2,1,0:T(8,128)(2,1)} all-to-all(bf16[4,32,2048]{2,1,0:T(8,128)(2,1)S(1)} %broadcast_select_fusion.1), channel_id=1, replica_groups=mesh['groups'=2,'ep'=4,'dp'=4] {'dp'}, dimensions={0} | all-to-all | bytes 1048576 | tf_op jit(solution)/shard_map/all_to_all | solution.py:77
  37.7 21.8 %all-gather.2.cloned.1.call-done = bf16[16,32,2048]{2,1,0:T(8,128)(2,1)} async-done(((bf16[4,32,2048]{2,1,0:T(8,128)(2,1)}), bf16[16,32,2048]{2,1,0:T(8,128)(2,1)}) %all-gather.2.cloned.1.call-update) | async-done | bytes 2097168 | tf_op jit(solution)/shard_map/all_gather | solution.py:78
  59.5 2.8 %fusion.11 = f32[512,192]{0,1:T(8,128)S(1)} fusion(bf16[512,2048]{1,0:T(8,128)(2,1)} %bitcast.126, bf16[1,3,2048,192]{2,3,1,0:T(8,128)(2,1)} %param.15), kind=kOutput, calls=%fused_computation.18 | convolution fusion | flops 402653184 | bytes 3276800 | tf_op jit(solution)/shard_map/dot_general | solution.py:22
  62.2 2.0 %fusion.7 = bf16[512,192]{0,1:T(8,128)(2,1)S(1)} fusion(bf16[512,2048]{1,0:T(8,128)(2,1)S(1)} %bitcast.127, bf16[1,3,2048,192]{2,3,1,0:T(8,128)(2,1)} %param.15, f32[512,192]{0,1:T(8,128)S(1)} %fusion.11), kind=kOutput, calls=%fused_computation.12 | convolution fusion | flops 403243008 | bytes 3473408 | tf_op jit(solution)/shard_map/dot_general | solution.py:23
  64.2 0.8 copy.37
  65.1 3.8 %fusion.8 = f32[16,32,2048]{2,1,0:T(8,128)} fusion(bf16[16,32,192]{2,1,0:T(8,128)(2,1)} %bitcast.122, bf16[1,3,2048,192]{2,3,1,0:T(8,128)(2,1)} %param.15), kind=kOutput, calls=%fused_computation.15 | convolution fusion | flops 402653184 | bytes 5242880 | tf_op jit(solution)/shard_map/dot_general | solution.py:25
  68.9 1.4 scatter_custom_fusion
  70.4 2.0 %gather_fusion = bf16[176,2048]{1,0:T(8,128)(2,1)} fusion(bf16[33,2048]{1,0:T(8,128)(2,1)S(1)} %concatenate.6, s32[1024]{0:T(1024)S(1)} %pad_clamp_fusion.2), kind=kCustom, calls=%fused_computation | custom fusion | bytes 1442496 | tf_op jit(solution)/shard_map/jit(_take)/gather | solution.py:62
  72.3 2.4 %gather.17 = bf16[16,11,2048]{2,1,0:T(8,128)(2,1)} reshape(bf16[176,2048]{1,0:T(8,128)(2,1)} %gather_fusion) | data formatting | bytes 1441792 | tf_op jit(solution)/shard_map/jit(_take)/gather | solution.py:62
  74.8 1.4 broadcast_select_fusion
  76.2 31.8 %all_to_all.21 = bf16[16,11,2048]{2,1,0:T(8,128)(2,1)} all-to-all(bf16[16,11,2048]{2,1,0:T(8,128)(2,1)S(1)} %broadcast_select_fusion), channel_id=1, replica_groups=mesh['groups'=2,'ep'=4,'dp'=4] {'ep','dp'}, dimensions={0} | all-to-all | bytes 1441792 | tf_op jit(solution)/shard_map/all_to_all | solution.py:68
  108.1 2.4 %reshape.244 = bf16[176,2048]{1,0:T(8,128)(2,1)} reshape(bf16[16,11,2048]{2,1,0:T(8,128)(2,1)} %all_to_all.21) | data formatting | bytes 1441792 | tf_op jit(solution)/shard_map/reshape | solution.py:9
  110.5 4.3 %fusion = f32[176,1536]{1,0:T(8,128)S(1)} fusion(bf16[176,2048]{1,0:T(8,128)(2,1)} %reshape.244, bf16[1,2048,1536]{2,1,0:T(8,128)(2,1)} %param.13), kind=kOutput, calls=%fused_computation.5 | convolution fusion | flops 1107296256 | bytes 8093696 | tf_op jit(solution)/shard_map/dot_general | solution.py:11
  114.8 1.7 fusion.4
  116.5 2.4 %reshape.245 = bf16[16,11,2048]{2,1,0:T(8,128)(2,1)} reshape(bf16[176,2048]{1,0:T(8,128)(2,1)} %fusion.4) | data formatting | bytes 1441792 | tf_op jit(solution)/shard_map/reshape | solution.py:16
  118.8 4.5 %all-to-all-start.1 = ((bf16[16,11,2048]{2,1,0:T(8,128)(2,1)}), bf16[16,11,2048]{2,1,0:T(8,128)(2,1)}, u32[]{:S(2)}, u32[]{:S(2)}) async-start(bf16[16,11,2048]{2,1,0:T(8,128)(2,1)} %reshape.245), calls=%async_computation.1 | async-start | bytes 2097152 | tf_op jit(solution)/shard_map/all_to_all | solution.py:66
  123.3 2.1 %convert_element_type.75 = bf16[4,32,2048]{2,1,0:T(8,128)(2,1)} convert(f32[4,32,2048]{2,1,0:T(8,128)} %reduce-scatter.2.cloned.1.call-done) | non-fusion elementwise | flops 262144 | bytes 1572864 | tf_op jit(solution)/shard_map/convert_element_type | solution.py:84
  125.4 24.9 %all-to-all-done.1 = bf16[16,11,2048]{2,1,0:T(8,128)(2,1)} async-done(((bf16[16,11,2048]{2,1,0:T(8,128)(2,1)}), bf16[16,11,2048]{2,1,0:T(8,128)(2,1)}, u32[]{:S(2)}, u32[]{:S(2)}) %all-to-all-start.1) | async-done | bytes 720928 | tf_op jit(solution)/shard_map/all_to_all | solution.py:66
  150.3 4.3 %all-to-all-start.3 = ((bf16[4,32,2048]{2,1,0:T(8,128)(2,1)}), bf16[4,32,2048]{2,1,0:T(8,128)(2,1)}, u32[]{:S(2)}, u32[]{:S(2)}) async-start(bf16[4,32,2048]{2,1,0:T(8,128)(2,1)} %convert_element_type.75), calls=%async_computation.4 | async-start | bytes 1048576 | tf_op jit(solution)/shard_map/all_to_all | solution.py:83
  155.2 2.4 %reshape.246 = bf16[176,2048]{1,0:T(8,128)(2,1)} reshape(bf16[16,11,2048]{2,1,0:T(8,128)(2,1)} %all-to-all-done.1) | data formatting | bytes 1441792 | tf_op jit(solution)/shard_map/reshape | solution.py:87
  157.5 11.5 %all-to-all-done.3 = bf16[4,32,2048]{2,1,0:T(8,128)(2,1)} async-done(((bf16[4,32,2048]{2,1,0:T(8,128)(2,1)}), bf16[4,32,2048]{2,1,0:T(8,128)(2,1)}, u32[]{:S(2)}, u32[]{:S(2)}) %all-to-all-start.3) | async-done | bytes 524320 | tf_op jit(solution)/shard_map/all_to_all | solution.py:83
  169.1 2.4 %pad_maximum_fusion = bf16[304,2048]{1,0:T(8,128)(2,1)} fusion(bf16[128,2048]{1,0:T(8,128)(2,1)} %bitcast.14, bf16[176,2048]{1,0:T(8,128)(2,1)} %reshape.246), kind=kLoop, calls=%fused_computation.10 | loop fusion | flops 2490368 | bytes 2490368 | tf_op jit(solution)/shard_map/concatenate | solution.py:86
  171.5 4.8 %gather_fusion.2 = bf16[256,2048]{1,0:T(8,128)(2,1)} fusion(bf16[304,2048]{1,0:T(8,128)(2,1)} %pad_maximum_fusion, s32[1024]{0:T(1024)S(1)} %pad_clamp_fusion), kind=kCustom, calls=%fused_computation.2 | custom fusion | bytes 2098176 | tf_op jit(solution)/shard_map/jit(_take)/gather | solution.py:92
  176.3 2.4 %copy_select_fusion = bf16[32,8,2048]{2,0,1:T(8,128)(2,1)S(1)} fusion(bf16[32,8,2048]{2,1,0:T(8,128)(2,1)} %bitcast.120, pred[32,8]{0,1:T(8,128)(4,1)S(1)} %compare_and_fusion), kind=kLoop, calls=%fused_computation.13 | loop fusion | flops 524288 | bytes 2097408 | tf_op jit(solution)/shard_map/jit(_take)/select_n | solution.py:92
  178.8 1.0 fusion.20
  (49 shorter events, 3.3 us)
Async XLA Ops:
  6.5 108.2 %copy-start = (bf16[1,768,2048]{2,1,0:T(8,128)(2,1)S(1)}, bf16[1,768,2048]{2,1,0:T(8,128)(2,1)}, u32[]{:S(2)}) copy-start(bf16[1,768,2048]{2,1,0:T(8,128)(2,1)} %param.14) | copy-start | bytes 9437188
  6.5 52.9 %all-gather.2.cloned.1.call-start = ((), (), s32[]{:S(2)}) async-start(), calls=%async_computation.5 | async-start | bytes 2621440 | tf_op jit(solution)/shard_map/all_gather | solution.py:78
  37.6 85.7 %reduce-scatter.2.cloned.1.call-start = ((), (), s32[]{:S(2)}) async-start(), calls=%async_computation.6 | async-start | bytes 5242880 | tf_op jit(solution)/shard_map/reduce_scatter | solution.py:80
  59.5 2.8 %copy-start.2 = (bf16[16,32,2048]{2,1,0:T(8,128)(2,1)S(1)}, bf16[16,32,2048]{2,1,0:T(8,128)(2,1)}, u32[]{:S(2)}) copy-start(bf16[16,32,2048]{2,1,0:T(8,128)(2,1)} %all-gather.2.cloned.1.call-done) | copy-start | bytes 6291460
  118.8 36.3 %copy-start.1 = (f32[32,8]{0,1:T(8,128)S(1)}, f32[32,8]{0,1:T(8,128)}, u32[]{:S(2)}) copy-start(f32[32,8]{0,1:T(8,128)} %param.10) | copy-start | bytes 3076
  118.8 31.4 %all-to-all-start.1 = ((bf16[16,11,2048]{2,1,0:T(8,128)(2,1)}), bf16[16,11,2048]{2,1,0:T(8,128)(2,1)}, u32[]{:S(2)}, u32[]{:S(2)}) async-start(bf16[16,11,2048]{2,1,0:T(8,128)(2,1)} %reshape.245), calls=%async_computation.1 | async-start | bytes 2097152 | tf_op jit(solution)/shard_map/all_to_all | solution.py:66
  150.3 18.8 %all-to-all-start.3 = ((bf16[4,32,2048]{2,1,0:T(8,128)(2,1)}), bf16[4,32,2048]{2,1,0:T(8,128)(2,1)}, u32[]{:S(2)}, u32[]{:S(2)}) async-start(bf16[4,32,2048]{2,1,0:T(8,128)(2,1)} %convert_element_type.75), calls=%async_computation.4 | async-start | bytes 1048576 | tf_op jit(solution)/shard_map/all_to_all | solution.py:83
Sparse Core Ops, SparseCore 0:
  37.7 21.6 all-gather.1
  69.1 50.1 reduce-scatter.1
where the time goes:
time: 187 us
  waiting for transfers between devices  58.2 us (31%)
  blocking collectives  52.6 us (28%)
  local copies, waits for them, and re-layouts  25.1 us (13%)
  matrix products  14.6 us (8%)
  other arithmetic  13.6 us (7%)
  between operations  13.6 us (7%)
  starting transfers between devices  8.84 us (5%)
    all_to_all x1, blocking collectives, body(): lax.all_to_all(cold_send, ('ep', 'dp'), split_axis=0, concat_axis=0, tile...  31.8 us
    all_to_all x1, waiting for transfers between devices, body(): lax.all_to_all(swiglu_rows(lax.all_to_all(cold_send, ('ep', 'dp'), split_...  24.9 us
    all_gather x1, waiting for transfers between devices, body(): gathered = lax.all_gather(hot_recv, 'ep', axis=0, tiled=True)  21.8 us
    all_to_all x1, blocking collectives, body(): lax.all_to_all(hot_send, 'dp', split_axis=0, concat_axis=0, tiled=True)  20.7 us
    all_to_all x1, waiting for transfers between devices, body(): lax.all_to_all(hot_sum.astype(jnp.bfloat16), 'dp', split_axis=0, concat_a...  11.5 us
    gather x1, local copies, waits for them, and re-layouts, body(): picked = jnp.take(answers, positions, axis=0)  4.81 us
    all_to_all x1, starting transfers between devices, body(): lax.all_to_all(swiglu_rows(lax.all_to_all(cold_send, ('ep', 'dp'), split_...  4.47 us
    gather x2, local copies, waits for them, and re-layouts, body(): jnp.take(padded, cold_map, axis=0).reshape(n_dev, cold_cap, model_width)  4.35 us
  transfers between devices with their start and end apart: 4, of which 3 were waited for; matrix products, arithmetic and copies ran while one was open for 12% of the time, Pallas kernels for 0%

commit v1 on v0

--- a/solution.py
+++ b/solution.py
@@ -1,6 +1,10 @@
+import functools
+
 import jax
 import jax.numpy as jnp
 from jax import lax
+from jax.experimental import pallas as pl
+from jax.experimental.pallas import tpu as pltpu
 from jax.sharding import PartitionSpec as P
 
 
@@ -28,7 +32,7 @@
     return result.reshape(in_shape)
 
 
-def body(tokens, expert_ids, route_w, hot_list, slot_of, cold_gate_up, cold_down, hot_weights):
+def routed_body(tokens, expert_ids, route_w, hot_list, slot_of, cold_gate_up, cold_down, hot_weights):
     tok_rows, model_width = tokens.shape
     top_count = expert_ids.shape[1]
     n_hot = hot_list.shape[0]
@@ -96,6 +100,189 @@
     return mixed.astype(jnp.bfloat16)
 
 
+def pin(array):
+    return pltpu.with_memory_space_constraint(array, pltpu.VMEM)
+
+
+def expert_kernel(n_blocks, halves, cap, key_ref, *refs):
+    rows_in = refs[:n_blocks]
+    meta_in = refs[n_blocks : 2 * n_blocks]
+    gate_up_ref, down_ref, hot_ref, out_ref, x_ref, hid_ref = refs[2 * n_blocks :]
+    height = rows_in[0].shape[0]
+    total = n_blocks * height
+    width = rows_in[0].shape[1]
+    hidden_width = down_ref.shape[1]
+    top = meta_in[0].shape[1] // 2
+    for index, block in enumerate(rows_in):
+        x_ref[pl.ds(index * height, height), :] = block[...]
+    meta = jnp.concatenate(
+        [m[pl.ds(half * height, height), :] for m, half in zip(meta_in, halves)], axis=0
+    )
+    ids, gains = meta[:, :top], meta[:, top:]
+    is_cold = ids == key_ref[0:1, :top]
+    is_hot = ids == key_ref[1:2, :top]
+    cold_gain = jnp.sum(jnp.where(is_cold, gains, 0.0), axis=1, keepdims=True)
+    hot_gain = jnp.sum(jnp.where(is_hot, gains, 0.0), axis=1, keepdims=True)
+    mark = jnp.sum(jnp.where(is_cold, 1.0, 0.0), axis=1, keepdims=True)
+    marks = jnp.broadcast_to(mark, (total, 128))
+    below = lax.broadcasted_iota(jnp.int32, (total, total), 0) > lax.broadcasted_iota(
+        jnp.int32, (total, total), 1
+    )
+    rank = jnp.dot(
+        jnp.where(below, 1.0, 0.0).astype(jnp.bfloat16),
+        marks.astype(jnp.bfloat16),
+        preferred_element_type=jnp.float32,
+    )
+    lane = lax.broadcasted_iota(jnp.int32, (total, 128), 1).astype(jnp.float32)
+    spread = jnp.where((marks > 0.5) & (rank == lane), 1.0, 0.0).astype(jnp.bfloat16)
+    x = x_ref[...]
+    picked = lax.dot_general(
+        spread, x, (((0,), (0,)), ((), ())), preferred_element_type=jnp.float32
+    )[:cap].astype(jnp.bfloat16)
+    step = 256
+    for start in range(0, hidden_width, step):
+        gate = jnp.dot(
+            picked, gate_up_ref[0, :, start : start + step], preferred_element_type=jnp.float32
+        )
+        up = jnp.dot(
+            picked,
+            gate_up_ref[0, :, hidden_width + start : hidden_width + start + step],
+            preferred_element_type=jnp.float32,
+        )
+        hid_ref[:, start : start + step] = (gate / (1.0 + jnp.exp(-gate)) * up).astype(jnp.bfloat16)
+    gate = jnp.dot(x, hot_ref[0, 0], preferred_element_type=jnp.float32)
+    up = jnp.dot(x, hot_ref[0, 1], preferred_element_type=jnp.float32)
+    hot_hidden = (gate / (1.0 + jnp.exp(-gate)) * up).astype(jnp.bfloat16)
+    cold_hidden = hid_ref[...]
+    spread_cap = spread[:, :cap]
+
+    @pl.loop(0, width // step)
+    def _(chunk):
+        at = pl.ds(pl.multiple_of(chunk * step, step), step)
+        hot_part = lax.dot_general(
+            hot_hidden,
+            hot_ref[0, 2, at, :],
+            (((1,), (1,)), ((), ())),
+            preferred_element_type=jnp.float32,
+        )
+        cold_part = jnp.dot(
+            cold_hidden, down_ref[0, :, at], preferred_element_type=jnp.float32
+        ).astype(jnp.bfloat16)
+        cold_rows = jnp.dot(spread_cap, cold_part, preferred_element_type=jnp.float32)
+        out_ref[:, at] = (hot_gain * hot_part + cold_gain * cold_rows).astype(jnp.bfloat16)
+
+
+def expert_rows(key, blocks, metas, halves, cap, weights):
+    n_blocks = len(blocks)
+    height, width = blocks[0].shape
+    total = n_blocks * height
+    hidden_width = weights[1].shape[1]
+    slice_width = weights[2].shape[3]
+    flops = 2 * 3 * width * (total * slice_width + cap * hidden_width) + 4 * 128 * total * width
+    vmem = pl.BlockSpec(memory_space=pltpu.VMEM)
+    return pl.pallas_call(
+        functools.partial(expert_kernel, n_blocks, halves, cap),
+        out_shape=jax.ShapeDtypeStruct((total, width), jnp.bfloat16),
+        in_specs=[vmem] * (1 + 2 * n_blocks + 3),
+        out_specs=vmem,
+        scratch_shapes=[
+            pltpu.VMEM((total, width), jnp.bfloat16),
+            pltpu.VMEM((cap, hidden_width), jnp.bfloat16),
+        ],
+        compiler_params=pltpu.CompilerParams(vmem_limit_bytes=24 * 2**20),
+        cost_estimate=pl.CostEstimate(
+            flops=flops, bytes_accessed=total * width * 4, transcendentals=total * slice_width
+        ),
+    )(key, *blocks, *metas, *[pin(w) for w in weights])
+
+
+def ring_perms(n_ep, n_dp):
+    chips = [(0, z) for z in range(n_dp)] + [(1, z) for z in reversed(range(n_dp))]
+
+    def device(place, core):
+        x, z = chips[place % len(chips)]
+        return (2 * x + core) * n_dp + z
+
+    def hop(by0, by1):
+        return [
+            (device(i, core), device(i + (by1 if core else by0), core))
+            for i in range(len(chips))
+            for core in range(2)
+        ]
+
+    swap = [(device(i, c), device(i, 1 - c)) for i in range(len(chips)) for c in range(2)]
+    return hop, swap
+
+
+def dense_body(tokens, expert_ids, route_w, hot_list, slot_of, cold_gate_up, cold_down, hot_weights):
+    tok_rows, width = tokens.shape
+    top = expert_ids.shape[1]
+    n_hot, n_exp = hot_list.shape[0], slot_of.shape[0]
+    n_ep, n_dp = lax.axis_size("ep"), lax.axis_size("dp")
+    cold_cap = -(-(tok_rows * top - n_hot * tok_rows) // (n_exp - n_hot))
+    hop, swap_pairs = ring_perms(n_ep, n_dp)
+    axes = ("ep", "dp")
+    move = lambda a, by0, by1=None: lax.ppermute(a, axes, hop(by0, by0 if by1 is None else by1))
+    swap = lambda a: lax.ppermute(a, axes, swap_pairs)
+    weights = (cold_gate_up, cold_down, hot_weights)
+    core = lax.axis_index("ep") % 2
+
+    me = lax.axis_index("ep") * n_dp + lax.axis_index("dp")
+    my_expert = jnp.sum(jnp.where(slot_of == me, jnp.arange(n_exp, dtype=jnp.int32), 0))
+    my_cold = jnp.where(jnp.any(hot_list == my_expert), -1, my_expert)
+    my_hot = jnp.sum(jnp.where(jnp.arange(n_hot) == lax.axis_index("dp"), hot_list, 0))
+    key = jnp.broadcast_to(
+        jnp.stack([my_cold, my_hot]).astype(jnp.float32)[:, None], (2, 128)
+    )
+
+    plus = {0: tokens}
+    meta = jnp.concatenate([expert_ids.astype(jnp.float32), route_w], axis=1)
+    meta = jnp.concatenate([meta, swap(meta)], axis=0)
+    metas = {0: meta}
+    for far in (1, 2, 3):
+        plus[far] = move(plus[far - 1], 1)
+        plus[-far] = move(plus[1 - far], -1)
+        metas[far] = move(metas[far - 1], 1)
+        metas[-far] = move(metas[1 - far], -1)
+    plus[4] = move(jnp.where(core == 0, plus[3], plus[-3]), 1, -1)
+    metas[4] = move(jnp.where(core == 0, metas[3], metas[-3]), 1, -1)
+    other = {far: swap(plus[far]) for far in plus}
+
+    def batch(fars, pool, half):
+        cap = -(-cold_cap * len(fars) // 16) * 16
+        rows = expert_rows(
+            key, [pool[f] for f in fars], [metas[f] for f in fars], [half] * len(fars), cap, weights
+        )
+        return rows
+
+    parts, theirs = {}, {}
+    for fars in ((0, 1, -1), (2, -2), (3, -3, 4)):
+        back = swap(batch(fars, other, 1))
+        mine = batch(fars, plus, 0)
+        for index, far in enumerate(fars):
+            at = slice(index * tok_rows, (index + 1) * tok_rows)
+            parts[far] = (mine[at], back[at])
+
+    f32 = jnp.float32
+    full = lambda far: parts[far][0].astype(f32) + parts[far][1].astype(f32)
+    low = lambda a: a.astype(jnp.bfloat16)
+    last = move(low(full(4)), -1, 1)
+    ahead = move(low(full(-3) + jnp.where(core == 1, last, 0).astype(f32)), 1)
+    behind = move(low(full(3) + jnp.where(core == 0, last, 0).astype(f32)), -1)
+    for far in (2, 1):
+        ahead = move(low(full(-far) + ahead.astype(f32)), 1)
+        behind = move(low(full(far) + behind.astype(f32)), -1)
+    return low(full(0) + ahead.astype(f32) + behind.astype(f32))
+
+
+def body(tokens, expert_ids, *rest):
+    hot_list, slot_of = rest[1], rest[2]
+    every_row_hot = 2 * expert_ids.shape[1] == slot_of.shape[0]
+    two_columns = lax.axis_size("ep") == 4 and lax.axis_size("dp") == 4
+    chosen = dense_body if every_row_hot and two_columns else routed_body
+    return chosen(tokens, expert_ids, *rest)
+
+
 def solution(mesh):
     in_specs = (
         P(("groups", "ep", "dp"), None),

time: 187 us -> 97.8 us (0.52)
  blocking collectives: 52.6 us -> 0 us
  waiting for transfers between devices: 58.2 us -> 10.5 us
  Pallas kernels: 0 us -> 31.7 us
  starting transfers between devices: 8.84 us -> 26.6 us
  matrix products: 14.6 us -> 0 us
  between operations: 13.6 us -> 1.46 us
  local copies, waits for them, and re-layouts: 25.1 us -> 18.6 us
  other arithmetic: 13.6 us -> 8.44 us
    all_to_all x2 -> x0, blocking collectives: 52.6 us -> none  [the longest x1 31.8 us: body(): lax.all_to_all(cold_send, ('ep', 'dp'), split_axis=0, concat_axis=0, tile...]
    all_to_all x2 -> x0, waiting for transfers between devices: 36.4 us -> none  [the longest x1 24.9 us: body(): lax.all_to_all(swiglu_rows(lax.all_to_all(cold_send, ('ep', 'dp'), split_...]
    pallas_call x0 -> x6, Pallas kernels: none -> 31.7 us  [expert_rows(): pl.pallas_call(functools.partial(expert_kernel, n_blocks, halves, cap), o...]
    ppermute x0 -> x33, starting transfers between devices: none -> 26.6 us  [the longest x21 23.4 us: dense_body(): lax.ppermute(a, axes, hop(by0, by0 if by1 is None else by1))]
    all_gather x1 -> x0, waiting for transfers between devices: 21.8 us -> none  [body(): gathered = lax.all_gather(hot_recv, 'ep', axis=0, tiled=True)]
    unnamed x7 -> x25, local copies, waits for them, and re-layouts: 0.92 us -> 18.5 us
    dot_general x5 -> x0, matrix products: 14.6 us -> none  [the longest x1 4.31 us: swiglu_rows(): both_out = jnp.dot(flat_in, gate_up, preferred_element_type=jnp.float32)]
    gather x4 -> x0, local copies, waits for them, and re-layouts: 10.9 us -> none  [the longest x1 4.81 us: body(): picked = jnp.take(answers, positions, axis=0)]
  transfers between devices with their start and end apart: 4 -> 33, of which waited for: 3 -> 5; matrix products, arithmetic and copies ran while one was open for 12% -> 13% of each run, Pallas kernels for 0% -> 27%
where the time goes in v1:
time: 97.8 us; the launch traced here: 97.3 us
  Pallas kernels  31.7 us (32%)
  starting transfers between devices  26.6 us (27%)
  local copies, waits for them, and re-layouts  18.6 us (19%)
  waiting for transfers between devices  10.5 us (11%)
  other arithmetic  8.44 us (9%)
  between operations  1.46 us (1%)
    pallas_call x6, Pallas kernels, expert_rows(): pl.pallas_call(functools.partial(expert_kernel, n_blocks, halves, cap), o...  31.7 us
    ppermute x21, starting transfers between devices, dense_body(): lax.ppermute(a, axes, hop(by0, by0 if by1 is None else by1))  23.4 us
    unnamed x25, local copies, waits for them, and re-layouts  18.5 us
    ppermute x21, waiting for transfers between devices, dense_body(): lax.ppermute(a, axes, hop(by0, by0 if by1 is None else by1))  10.4 us
    ppermute x12, starting transfers between devices, dense_body(): swap = lambda a: lax.ppermute(a, axes, swap_pairs)  3.2 us
  transfers between devices with their start and end apart: 33, of which 5 were waited for; matrix products, arithmetic and copies ran while one was open for 13% of the time, Pallas kernels for 27%

profile of v1, /device:TPU:0, one launch (start us, length us, event | category | flops | bytes accessed | tf_op | source)
XLA Modules:
  0.0 97.3 jit_solution(12452636793471856434)
XLA Ops:
  0.0 3.0 %collective-permute-start = (bf16[32,2048]{1,0:T(8,128)(2,1)}, bf16[32,2048]{1,0:T(8,128)(2,1)S(1)}, u32[]{:S(2)}, u32[]{:S(2)}) collective-permute-start(bf16[32,2048]{1,0:T(8,128)(2,1)} %refs_0_.1), channel_id=1, source_target_pairs={{0,1},{4,5},{1,2},{5,6},{2,3},{6,7},{3,11},{7,15},{11,10},{15,14},... | collective-permute-start | bytes 393224 | tf_op jit(solution)/shard_map/ppermute | solution.py:225
  3.0 3.6 %collective-permute-done.refs_1_ = bf16[32,2048]{1,0:T(8,128)(2,1)S(1)} collective-permute-done((bf16[32,2048]{1,0:T(8,128)(2,1)}, bf16[32,2048]{1,0:T(8,128)(2,1)S(1)}, u32[]{:S(2)}, u32[]{:S(2)}) %collective-permute-start) | collective-permute-done | bytes 131104 | tf_op jit(solution)/shard_map/ppermute | solution.py:225
  6.6 1.8 %collective-permute-start.9 = (bf16[32,2048]{1,0:T(8,128)(2,1)S(1)}, bf16[32,2048]{1,0:T(8,128)(2,1)}, u32[]{:S(2)}, u32[]{:S(2)}) collective-permute-start(bf16[32,2048]{1,0:T(8,128)(2,1)S(1)} %collective-permute-done.refs_1_), channel_id=1, source_target_pairs={{0,1},{4,5},{1,2},{5,6},{2,3},{6,7},{3,11},{7,15},{11,10},{15,14},... | collective-permute-start | bytes 393224 | tf_op jit(solution)/shard_map/ppermute | solution.py:225
  10.1 1.7 %collective-permute-done.9.refs_0_ = bf16[32,2048]{1,0:T(8,128)(2,1)} collective-permute-done((bf16[32,2048]{1,0:T(8,128)(2,1)S(1)}, bf16[32,2048]{1,0:T(8,128)(2,1)}, u32[]{:S(2)}, u32[]{:S(2)}) %collective-permute-start.9) | collective-permute-done | bytes 131104 | tf_op jit(solution)/shard_map/ppermute | solution.py:225
  11.7 1.8 %collective-permute-start.16 = (bf16[32,2048]{1,0:T(8,128)(2,1)}, bf16[32,2048]{1,0:T(8,128)(2,1)S(1)}, u32[]{:S(2)}, u32[]{:S(2)}) collective-permute-start(bf16[32,2048]{1,0:T(8,128)(2,1)} %collective-permute-done.9.refs_0_), channel_id=1, source_target_pairs={{0,1},{4,5},{1,2},{5,6},{2,3},{6,7},{3,11},{7,15},{11,10},{15,14},... | collective-permute-start | bytes 393224 | tf_op jit(solution)/shard_map/ppermute | solution.py:225
  14.6 1.8 %collective-permute-start.3 = (f32[64,16]{1,0:T(8,128)S(1)}, f32[64,16]{1,0:T(8,128)S(1)}, u32[]{:S(2)}, u32[]{:S(2)}) collective-permute-start(f32[64,16]{1,0:T(8,128)S(1)} %copy.19.refs_3_), channel_id=1, source_target_pairs={{0,1},{4,5},{1,2},{5,6},{2,3},{6,7},{3,11},{7,15},{11,10},{15,14},... | collective-permute-start | bytes 12296 | tf_op jit(solution)/shard_map/ppermute | solution.py:225
  16.6 1.3 %fusion.1 = s32[]{:T(128)} fusion(s32[4]{0:T(128)} %param.11, s32[]{:T(128)S(6)} %axis_index.33), kind=kLoop, calls=%fused_computation.16 | loop fusion | flops 11 | bytes 24 | tf_op jit(solution)/shard_map/reduce_sum | solution.py:233
  18.5 1.8 %collective-permute-start.11 = (f32[64,16]{1,0:T(8,128)S(1)}, f32[64,16]{1,0:T(8,128)S(1)}, u32[]{:S(2)}, u32[]{:S(2)}) collective-permute-start(f32[64,16]{1,0:T(8,128)S(1)} %collective-permute-done.3.refs_4_), channel_id=1, source_target_pairs={{0,1},{4,5},{1,2},{5,6},{2,3},{6,7},{3,11},{7,15},{11,10},{15,14},... | collective-permute-start | bytes 12296 | tf_op jit(solution)/shard_map/ppermute | solution.py:225
  20.6 1.9 %collective-permute-start.18 = (bf16[32,2048]{1,0:T(8,128)(2,1)S(1)}, bf16[32,2048]{1,0:T(8,128)(2,1)S(1)}, u32[]{:S(2)}, u32[]{:S(2)}) collective-permute-start(bf16[32,2048]{1,0:T(8,128)(2,1)S(1)} %broadcast_select_fusion), channel_id=1, source_target_pairs={{0,1},{4,12},{1,2},{5,4},{2,3},{6,5},{3,11},{7,6},{11,10},{15,7},{... | collective-permute-start | bytes 393224 | tf_op jit(solution)/shard_map/ppermute | solution.py:225
  22.5 1.3 %fusion = s32[]{:T(128)} fusion(s32[16]{0:T(128)} %param.12, s32[]{:T(128)S(6)} %add.55), kind=kLoop, calls=%fused_computation.15 | loop fusion | flops 47 | bytes 72 | tf_op jit(solution)/shard_map/reduce_sum | solution.py:231
  23.8 1.6 %collective-permute-start.19 = (f32[64,16]{1,0:T(8,128)S(1)}, f32[64,16]{1,0:T(8,128)S(1)}, u32[]{:S(2)}, u32[]{:S(2)}) collective-permute-start(f32[64,16]{1,0:T(8,128)S(1)} %collective-permute-done.11.refs_2_), channel_id=1, source_target_pairs={{0,1},{4,5},{1,2},{5,6},{2,3},{6,7},{3,11},{7,15},{11,10},{15,14},... | collective-permute-start | bytes 12296 | tf_op jit(solution)/shard_map/ppermute | solution.py:225
  25.8 1.9 %compare_reduce_fusion = pred[]{:T(512)} fusion(s32[4]{0:T(128)} %param.11, s32[]{:T(128)} %fusion), kind=kLoop, calls=%fused_computation.13 | loop fusion | flops 7 | bytes 21 | tf_op jit(solution)/shard_map/reduce_or | solution.py:232
  29.6 1.6 %collective-permute-start.21 = (f32[64,16]{1,0:T(8,128)S(1)}, f32[64,16]{1,0:T(8,128)S(1)}, u32[]{:S(2)}, u32[]{:S(2)}) collective-permute-start(f32[64,16]{1,0:T(8,128)S(1)} %broadcast_select_fusion.1), channel_id=1, source_target_pairs={{0,1},{4,12},{1,2},{5,4},{2,3},{6,5},{3,11},{7,6},{11,10},{15,7},{... | collective-permute-start | bytes 12296 | tf_op jit(solution)/shard_map/ppermute | solution.py:225
  31.9 4.6 %copy.20.refs_8_.refs_6_ = bf16[1,3,2048,192]{3,2,1,0:T(8,128)(2,1)} copy(bf16[1,3,2048,192]{2,3,1,0:T(8,128)(2,1)} %param.15) | data formatting | bytes 4718592 | tf_op args[7]
  36.7 2.8 %copy-done = bf16[1,2048,1536]{2,1,0:T(8,128)(2,1)S(1)} copy-done((bf16[1,2048,1536]{2,1,0:T(8,128)(2,1)S(1)}, bf16[1,2048,1536]{2,1,0:T(8,128)(2,1)}, u32[]{:S(2)}) %copy-start) | copy-done | bytes 6291480
  39.5 1.9 %copy-done.2 = bf16[1,3,2048,192]{3,2,1,0:T(8,128)(2,1)S(1)} copy-done((bf16[1,3,2048,192]{3,2,1,0:T(8,128)(2,1)S(1)}, bf16[1,3,2048,192]{3,2,1,0:T(8,128)(2,1)}, u32[]{:S(2)}) %copy-start.2) | copy-done | bytes 2359320
  41.3 1.9 %copy-done.5 = bf16[1,768,2048]{2,1,0:T(8,128)(2,1)S(1)} copy-done((bf16[1,768,2048]{2,1,0:T(8,128)(2,1)S(1)}, bf16[1,768,2048]{2,1,0:T(8,128)(2,1)}, u32[]{:S(2)}) %copy-start.5) | copy-done | bytes 3145752
  43.2 5.0 %shard_map.87 = bf16[96,2048]{1,0:T(8,128)(2,1)S(1)} custom-call(f32[2,128]{1,0:T(2,128)S(1)} %broadcast_in_dim.21.key_ref, bf16[32,2048]{1,0:T(8,128)(2,1)S(1)} %collective-permute-done.22.refs_0_, bf16[32,2048]{1,0:T(8,128)(2,1)S(1)} %collective-permute-done.23.refs_1_, bf16[32,2048]{1,0:T(8,128)(2,1)S(1)} %collective-permute-done.24.refs_2_, ...), custom_call_target="tpu_custom_call" | custom-call | flops 780140544 | bytes 786432 | tf_op jit(solution)/shard_map/pallas_call | solution.py:183
  48.9 5.0 %shard_map.86 = bf16[96,2048]{1,0:T(8,128)(2,1)S(1)} custom-call(f32[2,128]{1,0:T(2,128)S(1)} %broadcast_in_dim.21.key_ref, bf16[32,2048]{1,0:T(8,128)(2,1)S(1)} %collective-permute-done.16.refs_0_, bf16[32,2048]{1,0:T(8,128)(2,1)S(1)} %collective-permute-done.17.refs_1_, bf16[32,2048]{1,0:T(8,128)(2,1)S(1)} %collective-permute-done.18.refs_2_, ...), custom_call_target="tpu_custom_call" | custom-call | flops 780140544 | bytes 786432 | tf_op jit(solution)/shard_map/pallas_call | solution.py:183
  55.2 1.2 %collective-permute-start.5 = (bf16[32,2048]{1,0:T(8,128)(2,1)S(1)}, bf16[32,2048]{1,0:T(8,128)(2,1)S(1)}, u32[]{:S(2)}, u32[]{:S(2)}) collective-permute-start(bf16[32,2048]{1,0:T(8,128)(2,1)S(1)} %copy-done.7), channel_id=1, source_target_pairs={{0,4},{4,0},{1,5},{5,1},{2,6},{6,2},{3,7},{7,3},{11,15},{15,11},{1... | collective-permute-start | bytes 393224 | tf_op jit(solution)/shard_map/ppermute | solution.py:226
  57.0 2.8 %copy-done.1 = bf16[1,2048,1536]{2,1,0:T(8,128)(2,1)S(1)} copy-done((bf16[1,2048,1536]{2,1,0:T(8,128)(2,1)S(1)}, bf16[1,2048,1536]{2,1,0:T(8,128)(2,1)}, u32[]{:S(2)}) %copy-start.1) | copy-done | bytes 6291480
  59.8 1.9 %copy-done.4 = bf16[1,3,2048,192]{3,2,1,0:T(8,128)(2,1)S(1)} copy-done((bf16[1,3,2048,192]{3,2,1,0:T(8,128)(2,1)S(1)}, bf16[1,3,2048,192]{3,2,1,0:T(8,128)(2,1)}, u32[]{:S(2)}) %copy-start.4) | copy-done | bytes 2359320
  61.6 1.9 %copy-done.6 = bf16[1,768,2048]{2,1,0:T(8,128)(2,1)S(1)} copy-done((bf16[1,768,2048]{2,1,0:T(8,128)(2,1)S(1)}, bf16[1,768,2048]{2,1,0:T(8,128)(2,1)}, u32[]{:S(2)}) %copy-start.6) | copy-done | bytes 3145752
  63.5 5.8 %shard_map.85 = bf16[64,2048]{1,0:T(8,128)(2,1)S(1)} custom-call(f32[2,128]{1,0:T(2,128)S(1)} %broadcast_in_dim.21.key_ref, bf16[32,2048]{1,0:T(8,128)(2,1)} %collective-permute-done.13.refs_0_, bf16[32,2048]{1,0:T(8,128)(2,1)} %collective-permute-done.14.refs_1_, f32[64,16]{1,0:T(8,128)S(1)} %collective-permute-done.11.refs_2_, ...), custom_call_target="tpu_custom_call" | custom-call | flops 520093696 | bytes 524288 | tf_op jit(solution)/shard_map/pallas_call | solution.py:183
  69.6 1.5 %collective-permute-start.27 = (bf16[32,2048]{1,0:T(8,128)(2,1)S(1)}, bf16[32,2048]{1,0:T(8,128)(2,1)S(1)}, u32[]{:S(2)}, u32[]{:S(2)}) collective-permute-start(bf16[32,2048]{1,0:T(8,128)(2,1)S(1)} %get-tuple-element.5), channel_id=1, source_target_pairs={{0,1},{4,5},{1,2},{5,6},{2,3},{6,7},{3,11},{7,15},{11,10},{15,14},... | collective-permute-start | bytes 393224 | tf_op jit(solution)/shard_map/ppermute | solution.py:225
  71.7 5.0 %shard_map.83 = bf16[96,2048]{1,0:T(8,128)(2,1)S(1)} custom-call(f32[2,128]{1,0:T(2,128)S(1)} %broadcast_in_dim.21.key_ref, bf16[32,2048]{1,0:T(8,128)(2,1)S(1)} %collective-permute-done.5.refs_0_, bf16[32,2048]{1,0:T(8,128)(2,1)S(1)} %collective-permute-done.6.refs_1_, bf16[32,2048]{1,0:T(8,128)(2,1)S(1)} %collective-permute-done.7.refs_2_, ...), custom_call_target="tpu_custom_call" | custom-call | flops 780140544 | bytes 786432 | tf_op jit(solution)/shard_map/pallas_call | solution.py:183
  76.8 5.8 %shard_map.84 = bf16[64,2048]{1,0:T(8,128)(2,1)S(1)} custom-call(f32[2,128]{1,0:T(2,128)S(1)} %broadcast_in_dim.21.key_ref, bf16[32,2048]{1,0:T(8,128)(2,1)} %collective-permute-done.9.refs_0_, bf16[32,2048]{1,0:T(8,128)(2,1)} %collective-permute-done.10.refs_1_, f32[64,16]{1,0:T(8,128)S(1)} %collective-permute-done.11.refs_2_, ...), custom_call_target="tpu_custom_call" | custom-call | flops 520093696 | bytes 524288 | tf_op jit(solution)/shard_map/pallas_call | solution.py:183
  82.7 1.5 %collective-permute-start.28 = (bf16[32,2048]{1,0:T(8,128)(2,1)S(1)}, bf16[32,2048]{1,0:T(8,128)(2,1)S(1)}, u32[]{:S(2)}, u32[]{:S(2)}) collective-permute-start(bf16[32,2048]{1,0:T(8,128)(2,1)S(1)} %get-tuple-element.9), channel_id=1, source_target_pairs={{0,1},{4,5},{1,2},{5,6},{2,3},{6,7},{3,11},{7,15},{11,10},{15,14},... | collective-permute-start | bytes 393224 | tf_op jit(solution)/shard_map/ppermute | solution.py:225
  84.8 5.0 %shard_map.82 = bf16[96,2048]{1,0:T(8,128)(2,1)S(1)} custom-call(f32[2,128]{1,0:T(2,128)S(1)} %broadcast_in_dim.21.key_ref, bf16[32,2048]{1,0:T(8,128)(2,1)S(1)} %copy-done.7, bf16[32,2048]{1,0:T(8,128)(2,1)S(1)} %collective-permute-done.refs_1_, bf16[32,2048]{1,0:T(8,128)(2,1)S(1)} %collective-permute-done.1.refs_2_, f32[64,16]{1,0:T(8,128)S(1)} %copy.19.refs_3_, ...), custom_call_target="tpu_custom_call" | custom-call | flops 780140544 | bytes 786432 | tf_op jit(solution)/shard_map/pallas_call | solution.py:183
  90.0 1.5 %collective-permute-start.29 = (bf16[32,2048]{1,0:T(8,128)(2,1)S(1)}, bf16[32,2048]{1,0:T(8,128)(2,1)S(1)}, u32[]{:S(2)}, u32[]{:S(2)}) collective-permute-start(bf16[32,2048]{1,0:T(8,128)(2,1)S(1)} %get-tuple-element.7), channel_id=1, source_target_pairs={{0,1},{4,5},{1,2},{5,6},{2,3},{6,7},{3,11},{7,15},{11,10},{15,14},... | collective-permute-start | bytes 393224 | tf_op jit(solution)/shard_map/ppermute | solution.py:225
  92.1 3.3 %collective-permute-done.29 = bf16[32,2048]{1,0:T(8,128)(2,1)S(1)} collective-permute-done((bf16[32,2048]{1,0:T(8,128)(2,1)S(1)}, bf16[32,2048]{1,0:T(8,128)(2,1)S(1)}, u32[]{:S(2)}, u32[]{:S(2)}) %collective-permute-start.29) | collective-permute-done | bytes 131104 | tf_op jit(solution)/shard_map/ppermute | solution.py:225
  95.3 1.2 %collective-permute-done.32 = bf16[32,2048]{1,0:T(8,128)(2,1)S(1)} collective-permute-done((bf16[32,2048]{1,0:T(8,128)(2,1)S(1)}, bf16[32,2048]{1,0:T(8,128)(2,1)S(1)}, u32[]{:S(2)}, u32[]{:S(2)}) %collective-permute-start.32) | collective-permute-done | bytes 131104 | tf_op jit(solution)/shard_map/ppermute | solution.py:225
  (82 shorter events, 10.9 us)
Async XLA Ops:
  0.0 6.6 %collective-permute-start = (bf16[32,2048]{1,0:T(8,128)(2,1)}, bf16[32,2048]{1,0:T(8,128)(2,1)S(1)}, u32[]{:S(2)}, u32[]{:S(2)}) collective-permute-start(bf16[32,2048]{1,0:T(8,128)(2,1)} %refs_0_.1), channel_id=1, source_target_pairs={{0,1},{4,5},{1,2},{5,6},{2,3},{6,7},{3,11},{7,15},{11,10},{15,14},... | collective-permute-start | bytes 393224 | tf_op jit(solution)/shard_map/ppermute | solution.py:225
  3.0 5.5 %collective-permute-start.1 = (bf16[32,2048]{1,0:T(8,128)(2,1)}, bf16[32,2048]{1,0:T(8,128)(2,1)S(1)}, u32[]{:S(2)}, u32[]{:S(2)}) collective-permute-start(bf16[32,2048]{1,0:T(8,128)(2,1)} %refs_0_.1), channel_id=1, source_target_pairs={{0,8},{4,12},{1,0},{5,4},{2,1},{6,5},{3,2},{7,6},{11,3},{15,7},{10... | collective-permute-start | bytes 393224 | tf_op jit(solution)/shard_map/ppermute | solution.py:225
  6.6 5.1 %collective-permute-start.9 = (bf16[32,2048]{1,0:T(8,128)(2,1)S(1)}, bf16[32,2048]{1,0:T(8,128)(2,1)}, u32[]{:S(2)}, u32[]{:S(2)}) collective-permute-start(bf16[32,2048]{1,0:T(8,128)(2,1)S(1)} %collective-permute-done.refs_1_), channel_id=1, source_target_pairs={{0,1},{4,5},{1,2},{5,6},{2,3},{6,7},{3,11},{7,15},{11,10},{15,14},... | collective-permute-start | bytes 393224 | tf_op jit(solution)/shard_map/ppermute | solution.py:225
  8.5 5.1 %collective-permute-start.10 = (bf16[32,2048]{1,0:T(8,128)(2,1)S(1)}, bf16[32,2048]{1,0:T(8,128)(2,1)}, u32[]{:S(2)}, u32[]{:S(2)}) collective-permute-start(bf16[32,2048]{1,0:T(8,128)(2,1)S(1)} %collective-permute-done.1.refs_2_), channel_id=1, source_target_pairs={{0,8},{4,12},{1,0},{5,4},{2,1},{6,5},{3,2},{7,6},{11,3},{15,7},{10... | collective-permute-start | bytes 393224 | tf_op jit(solution)/shard_map/ppermute | solution.py:225
  11.7 8.8 %collective-permute-start.16 = (bf16[32,2048]{1,0:T(8,128)(2,1)}, bf16[32,2048]{1,0:T(8,128)(2,1)S(1)}, u32[]{:S(2)}, u32[]{:S(2)}) collective-permute-start(bf16[32,2048]{1,0:T(8,128)(2,1)} %collective-permute-done.9.refs_0_), channel_id=1, source_target_pairs={{0,1},{4,5},{1,2},{5,6},{2,3},{6,7},{3,11},{7,15},{11,10},{15,14},... | collective-permute-start | bytes 393224 | tf_op jit(solution)/shard_map/ppermute | solution.py:225
  13.6 7.0 %collective-permute-start.17 = (bf16[32,2048]{1,0:T(8,128)(2,1)}, bf16[32,2048]{1,0:T(8,128)(2,1)S(1)}, u32[]{:S(2)}, u32[]{:S(2)}) collective-permute-start(bf16[32,2048]{1,0:T(8,128)(2,1)} %collective-permute-done.10.refs_1_), channel_id=1, source_target_pairs={{0,8},{4,12},{1,0},{5,4},{2,1},{6,5},{3,2},{7,6},{11,3},{15,7},{10... | collective-permute-start | bytes 393224 | tf_op jit(solution)/shard_map/ppermute | solution.py:225
  14.6 3.9 %collective-permute-start.3 = (f32[64,16]{1,0:T(8,128)S(1)}, f32[64,16]{1,0:T(8,128)S(1)}, u32[]{:S(2)}, u32[]{:S(2)}) collective-permute-start(f32[64,16]{1,0:T(8,128)S(1)} %copy.19.refs_3_), channel_id=1, source_target_pairs={{0,1},{4,5},{1,2},{5,6},{2,3},{6,7},{3,11},{7,15},{11,10},{15,14},... | collective-permute-start | bytes 12296 | tf_op jit(solution)/shard_map/ppermute | solution.py:225
  16.4 3.9 %collective-permute-start.4 = (f32[64,16]{1,0:T(8,128)S(1)}, f32[64,16]{1,0:T(8,128)S(1)}, u32[]{:S(2)}, u32[]{:S(2)}) collective-permute-start(f32[64,16]{1,0:T(8,128)S(1)} %copy.19.refs_3_), channel_id=1, source_target_pairs={{0,8},{4,12},{1,0},{5,4},{2,1},{6,5},{3,2},{7,6},{11,3},{15,7},{10... | collective-permute-start | bytes 12296 | tf_op jit(solution)/shard_map/ppermute | solution.py:225
  18.5 5.3 %collective-permute-start.11 = (f32[64,16]{1,0:T(8,128)S(1)}, f32[64,16]{1,0:T(8,128)S(1)}, u32[]{:S(2)}, u32[]{:S(2)}) collective-permute-start(f32[64,16]{1,0:T(8,128)S(1)} %collective-permute-done.3.refs_4_), channel_id=1, source_target_pairs={{0,1},{4,5},{1,2},{5,6},{2,3},{6,7},{3,11},{7,15},{11,10},{15,14},... | collective-permute-start | bytes 12296 | tf_op jit(solution)/shard_map/ppermute | solution.py:225
  20.4 5.0 %collective-permute-start.12 = (f32[64,16]{1,0:T(8,128)S(1)}, f32[64,16]{1,0:T(8,128)S(1)}, u32[]{:S(2)}, u32[]{:S(2)}) collective-permute-start(f32[64,16]{1,0:T(8,128)S(1)} %collective-permute-done.4.refs_5_), channel_id=1, source_target_pairs={{0,8},{4,12},{1,0},{5,4},{2,1},{6,5},{3,2},{7,6},{11,3},{15,7},{10... | collective-permute-start | bytes 12296 | tf_op jit(solution)/shard_map/ppermute | solution.py:225
  20.6 8.9 %collective-permute-start.18 = (bf16[32,2048]{1,0:T(8,128)(2,1)S(1)}, bf16[32,2048]{1,0:T(8,128)(2,1)S(1)}, u32[]{:S(2)}, u32[]{:S(2)}) collective-permute-start(bf16[32,2048]{1,0:T(8,128)(2,1)S(1)} %broadcast_select_fusion), channel_id=1, source_target_pairs={{0,1},{4,12},{1,2},{5,4},{2,3},{6,5},{3,11},{7,6},{11,10},{15,7},{... | collective-permute-start | bytes 393224 | tf_op jit(solution)/shard_map/ppermute | solution.py:225
  23.8 5.8 %collective-permute-start.19 = (f32[64,16]{1,0:T(8,128)S(1)}, f32[64,16]{1,0:T(8,128)S(1)}, u32[]{:S(2)}, u32[]{:S(2)}) collective-permute-start(f32[64,16]{1,0:T(8,128)S(1)} %collective-permute-done.11.refs_2_), channel_id=1, source_target_pairs={{0,1},{4,5},{1,2},{5,6},{2,3},{6,7},{3,11},{7,15},{11,10},{15,14},... | collective-permute-start | bytes 12296 | tf_op jit(solution)/shard_map/ppermute | solution.py:225
  25.3 4.2 %collective-permute-start.20 = (f32[64,16]{1,0:T(8,128)S(1)}, f32[64,16]{1,0:T(8,128)S(1)}, u32[]{:S(2)}, u32[]{:S(2)}) collective-permute-start(f32[64,16]{1,0:T(8,128)S(1)} %collective-permute-done.12.refs_3_), channel_id=1, source_target_pairs={{0,8},{4,12},{1,0},{5,4},{2,1},{6,5},{3,2},{7,6},{11,3},{15,7},{10... | collective-permute-start | bytes 12296 | tf_op jit(solution)/shard_map/ppermute | solution.py:225
  28.9 7.7 %collective-permute-start.22 = (bf16[32,2048]{1,0:T(8,128)(2,1)S(1)}, bf16[32,2048]{1,0:T(8,128)(2,1)S(1)}, u32[]{:S(2)}, u32[]{:S(2)}) collective-permute-start(bf16[32,2048]{1,0:T(8,128)(2,1)S(1)} %collective-permute-done.16.refs_0_), channel_id=1, source_target_pairs={{0,4},{4,0},{1,5},{5,1},{2,6},{6,2},{3,7},{7,3},{11,15},{15,11},{1... | collective-permute-start | bytes 393224 | tf_op jit(solution)/shard_map/ppermute | solution.py:226
  29.0 7.6 %collective-permute-start.23 = (bf16[32,2048]{1,0:T(8,128)(2,1)S(1)}, bf16[32,2048]{1,0:T(8,128)(2,1)S(1)}, u32[]{:S(2)}, u32[]{:S(2)}) collective-permute-start(bf16[32,2048]{1,0:T(8,128)(2,1)S(1)} %collective-permute-done.17.refs_1_), channel_id=1, source_target_pairs={{0,4},{4,0},{1,5},{5,1},{2,6},{6,2},{3,7},{7,3},{11,15},{15,11},{1... | collective-permute-start | bytes 393224 | tf_op jit(solution)/shard_map/ppermute | solution.py:226
  29.5 7.1 %collective-permute-start.24 = (bf16[32,2048]{1,0:T(8,128)(2,1)S(1)}, bf16[32,2048]{1,0:T(8,128)(2,1)S(1)}, u32[]{:S(2)}, u32[]{:S(2)}) collective-permute-start(bf16[32,2048]{1,0:T(8,128)(2,1)S(1)} %collective-permute-done.18.refs_2_), channel_id=1, source_target_pairs={{0,4},{4,0},{1,5},{5,1},{2,6},{6,2},{3,7},{7,3},{11,15},{15,11},{1... | collective-permute-start | bytes 393224 | tf_op jit(solution)/shard_map/ppermute | solution.py:226
  29.6 7.0 %collective-permute-start.21 = (f32[64,16]{1,0:T(8,128)S(1)}, f32[64,16]{1,0:T(8,128)S(1)}, u32[]{:S(2)}, u32[]{:S(2)}) collective-permute-start(f32[64,16]{1,0:T(8,128)S(1)} %broadcast_select_fusion.1), channel_id=1, source_target_pairs={{0,1},{4,12},{1,2},{5,4},{2,3},{6,5},{3,11},{7,6},{11,10},{15,7},{... | collective-permute-start | bytes 12296 | tf_op jit(solution)/shard_map/ppermute | solution.py:225
  48.3 5.7 %collective-permute-start.25 = (bf16[96,2048]{1,0:T(8,128)(2,1)S(1)}, bf16[96,2048]{1,0:T(8,128)(2,1)S(1)}, u32[]{:S(2)}, u32[]{:S(2)}) collective-permute-start(bf16[96,2048]{1,0:T(8,128)(2,1)S(1)} %shard_map.87), channel_id=1, source_target_pairs={{0,4},{4,0},{1,5},{5,1},{2,6},{6,2},{3,7},{7,3},{11,15},{15,11},{1... | collective-permute-start | bytes 1179656 | tf_op jit(solution)/shard_map/ppermute | solution.py:226
  48.3 8.1 %collective-permute-start.13 = (bf16[32,2048]{1,0:T(8,128)(2,1)}, bf16[32,2048]{1,0:T(8,128)(2,1)}, u32[]{:S(2)}, u32[]{:S(2)}) collective-permute-start(bf16[32,2048]{1,0:T(8,128)(2,1)} %collective-permute-done.9.refs_0_), channel_id=1, source_target_pairs={{0,4},{4,0},{1,5},{5,1},{2,6},{6,2},{3,7},{7,3},{11,15},{15,11},{1... | collective-permute-start | bytes 393224 | tf_op jit(solution)/shard_map/ppermute | solution.py:226
  48.8 8.1 %collective-permute-start.14 = (bf16[32,2048]{1,0:T(8,128)(2,1)}, bf16[32,2048]{1,0:T(8,128)(2,1)}, u32[]{:S(2)}, u32[]{:S(2)}) collective-permute-start(bf16[32,2048]{1,0:T(8,128)(2,1)} %collective-permute-done.10.refs_1_), channel_id=1, source_target_pairs={{0,4},{4,0},{1,5},{5,1},{2,6},{6,2},{3,7},{7,3},{11,15},{15,11},{1... | collective-permute-start | bytes 393224 | tf_op jit(solution)/shard_map/ppermute | solution.py:226
  54.7 14.8 %collective-permute-start.26 = (bf16[32,2048]{1,0:T(8,128)(2,1)S(1)}, bf16[32,2048]{1,0:T(8,128)(2,1)S(1)}, u32[]{:S(2)}, u32[]{:S(2)}) collective-permute-start(bf16[32,2048]{1,0:T(8,128)(2,1)S(1)} %add_convert_fusion.7), channel_id=1, source_target_pairs={{0,8},{4,5},{1,0},{5,6},{2,1},{6,7},{3,2},{7,15},{11,3},{15,14},{1... | collective-permute-start | bytes 393224 | tf_op jit(solution)/shard_map/ppermute | solution.py:225
  55.2 15.9 %collective-permute-start.5 = (bf16[32,2048]{1,0:T(8,128)(2,1)S(1)}, bf16[32,2048]{1,0:T(8,128)(2,1)S(1)}, u32[]{:S(2)}, u32[]{:S(2)}) collective-permute-start(bf16[32,2048]{1,0:T(8,128)(2,1)S(1)} %copy-done.7), channel_id=1, source_target_pairs={{0,4},{4,0},{1,5},{5,1},{2,6},{6,2},{3,7},{7,3},{11,15},{15,11},{1... | collective-permute-start | bytes 393224 | tf_op jit(solution)/shard_map/ppermute | solution.py:226
  56.4 15.2 %collective-permute-start.6 = (bf16[32,2048]{1,0:T(8,128)(2,1)S(1)}, bf16[32,2048]{1,0:T(8,128)(2,1)S(1)}, u32[]{:S(2)}, u32[]{:S(2)}) collective-permute-start(bf16[32,2048]{1,0:T(8,128)(2,1)S(1)} %collective-permute-done.refs_1_), channel_id=1, source_target_pairs={{0,4},{4,0},{1,5},{5,1},{2,6},{6,2},{3,7},{7,3},{11,15},{15,11},{1... | collective-permute-start | bytes 393224 | tf_op jit(solution)/shard_map/ppermute | solution.py:226
  56.5 15.2 %collective-permute-start.7 = (bf16[32,2048]{1,0:T(8,128)(2,1)S(1)}, bf16[32,2048]{1,0:T(8,128)(2,1)S(1)}, u32[]{:S(2)}, u32[]{:S(2)}) collective-permute-start(bf16[32,2048]{1,0:T(8,128)(2,1)S(1)} %collective-permute-done.1.refs_2_), channel_id=1, source_target_pairs={{0,4},{4,0},{1,5},{5,1},{2,6},{6,2},{3,7},{7,3},{11,15},{15,11},{1... | collective-permute-start | bytes 393224 | tf_op jit(solution)/shard_map/ppermute | solution.py:226
  69.4 13.2 %collective-permute-start.15 = (bf16[64,2048]{1,0:T(8,128)(2,1)S(1)}, bf16[64,2048]{1,0:T(8,128)(2,1)S(1)}, u32[]{:S(2)}, u32[]{:S(2)}) collective-permute-start(bf16[64,2048]{1,0:T(8,128)(2,1)S(1)} %shard_map.85), channel_id=1, source_target_pairs={{0,4},{4,0},{1,5},{5,1},{2,6},{6,2},{3,7},{7,3},{11,15},{15,11},{1... | collective-permute-start | bytes 786440 | tf_op jit(solution)/shard_map/ppermute | solution.py:226
  69.6 13.0 %collective-permute-start.27 = (bf16[32,2048]{1,0:T(8,128)(2,1)S(1)}, bf16[32,2048]{1,0:T(8,128)(2,1)S(1)}, u32[]{:S(2)}, u32[]{:S(2)}) collective-permute-start(bf16[32,2048]{1,0:T(8,128)(2,1)S(1)} %get-tuple-element.5), channel_id=1, source_target_pairs={{0,1},{4,5},{1,2},{5,6},{2,3},{6,7},{3,11},{7,15},{11,10},{15,14},... | collective-permute-start | bytes 393224 | tf_op jit(solution)/shard_map/ppermute | solution.py:225
  71.1 11.5 %collective-permute-start.30 = (bf16[32,2048]{1,0:T(8,128)(2,1)S(1)}, bf16[32,2048]{1,0:T(8,128)(2,1)S(1)}, u32[]{:S(2)}, u32[]{:S(2)}) collective-permute-start(bf16[32,2048]{1,0:T(8,128)(2,1)S(1)} %get-tuple-element.6), channel_id=1, source_target_pairs={{0,8},{4,12},{1,0},{5,4},{2,1},{6,5},{3,2},{7,6},{11,3},{15,7},{10... | collective-permute-start | bytes 393224 | tf_op jit(solution)/shard_map/ppermute | solution.py:225
  76.7 13.1 %collective-permute-start.8 = (bf16[96,2048]{1,0:T(8,128)(2,1)S(1)}, bf16[96,2048]{1,0:T(8,128)(2,1)S(1)}, u32[]{:S(2)}, u32[]{:S(2)}) collective-permute-start(bf16[96,2048]{1,0:T(8,128)(2,1)S(1)} %shard_map.83), channel_id=1, source_target_pairs={{0,4},{4,0},{1,5},{5,1},{2,6},{6,2},{3,7},{7,3},{11,15},{15,11},{1... | collective-permute-start | bytes 1179656 | tf_op jit(solution)/shard_map/ppermute | solution.py:226
  82.7 7.1 %collective-permute-start.28 = (bf16[32,2048]{1,0:T(8,128)(2,1)S(1)}, bf16[32,2048]{1,0:T(8,128)(2,1)S(1)}, u32[]{:S(2)}, u32[]{:S(2)}) collective-permute-start(bf16[32,2048]{1,0:T(8,128)(2,1)S(1)} %get-tuple-element.9), channel_id=1, source_target_pairs={{0,1},{4,5},{1,2},{5,6},{2,3},{6,7},{3,11},{7,15},{11,10},{15,14},... | collective-permute-start | bytes 393224 | tf_op jit(solution)/shard_map/ppermute | solution.py:225
  84.3 5.6 %collective-permute-start.31 = (bf16[32,2048]{1,0:T(8,128)(2,1)S(1)}, bf16[32,2048]{1,0:T(8,128)(2,1)S(1)}, u32[]{:S(2)}, u32[]{:S(2)}) collective-permute-start(bf16[32,2048]{1,0:T(8,128)(2,1)S(1)} %get-tuple-element.10), channel_id=1, source_target_pairs={{0,8},{4,12},{1,0},{5,4},{2,1},{6,5},{3,2},{7,6},{11,3},{15,7},{10... | collective-permute-start | bytes 393224 | tf_op jit(solution)/shard_map/ppermute | solution.py:225
  90.0 5.4 %collective-permute-start.29 = (bf16[32,2048]{1,0:T(8,128)(2,1)S(1)}, bf16[32,2048]{1,0:T(8,128)(2,1)S(1)}, u32[]{:S(2)}, u32[]{:S(2)}) collective-permute-start(bf16[32,2048]{1,0:T(8,128)(2,1)S(1)} %get-tuple-element.7), channel_id=1, source_target_pairs={{0,1},{4,5},{1,2},{5,6},{2,3},{6,7},{3,11},{7,15},{11,10},{15,14},... | collective-permute-start | bytes 393224 | tf_op jit(solution)/shard_map/ppermute | solution.py:225
  91.5 5.1 %collective-permute-start.32 = (bf16[32,2048]{1,0:T(8,128)(2,1)S(1)}, bf16[32,2048]{1,0:T(8,128)(2,1)S(1)}, u32[]{:S(2)}, u32[]{:S(2)}) collective-permute-start(bf16[32,2048]{1,0:T(8,128)(2,1)S(1)} %get-tuple-element.8), channel_id=1, source_target_pairs={{0,8},{4,12},{1,0},{5,4},{2,1},{6,5},{3,2},{7,6},{11,3},{15,7},{10... | collective-permute-start | bytes 393224 | tf_op jit(solution)/shard_map/ppermute | solution.py:225
  (13 other events, 58.8 us)

commit v2 on v0

--- a/solution.py
+++ b/solution.py
@@ -1,6 +1,10 @@
+import functools
+
 import jax
 import jax.numpy as jnp
 from jax import lax
+from jax.experimental import pallas as pl
+from jax.experimental.pallas import tpu as pltpu
 from jax.sharding import PartitionSpec as P
 
 
@@ -28,7 +32,7 @@
     return result.reshape(in_shape)
 
 
-def body(tokens, expert_ids, route_w, hot_list, slot_of, cold_gate_up, cold_down, hot_weights):
+def routed_body(tokens, expert_ids, route_w, hot_list, slot_of, cold_gate_up, cold_down, hot_weights):
     tok_rows, model_width = tokens.shape
     top_count = expert_ids.shape[1]
     n_hot = hot_list.shape[0]
@@ -96,6 +100,367 @@
     return mixed.astype(jnp.bfloat16)
 
 
+def pin(array):
+    return pltpu.with_memory_space_constraint(array, pltpu.VMEM)
+
+
+NN = (((1,), (0,)), ((), ()))
+NT = (((1,), (1,)), ((), ()))
+TN = (((0,), (0,)), ((), ()))
+STEP = 256
+LANES = 128
+
+
+def mm(a, b, dims=NN):
+    return lax.dot_general(a, b, dims, preferred_element_type=jnp.float32)
+
+
+def swish(gate, up):
+    return (gate / (1.0 + jnp.exp(-gate)) * up).astype(jnp.bfloat16)
+
+
+def message_kernel(hot_list_ref, slot_ref, tok_ref, ids_ref, gain_ref, out_ref, key_ref):
+    width = tok_ref.shape[1]
+    out_ref[:, :width] = tok_ref[...]
+    top = ids_ref.shape[0]
+    bf16, f32 = jnp.bfloat16, jnp.float32
+    gains = gain_ref[...]
+    terms = [ids_ref[...].astype(f32)]
+    for _ in range(3):
+        term = gains.astype(bf16).astype(f32)
+        terms.append(term)
+        gains = gains - term
+    stacked = jnp.concatenate(terms, axis=0).astype(bf16)
+    shape = (4 * top, LANES)
+    place = lax.broadcasted_iota(jnp.int32, shape, 0) == lax.broadcasted_iota(jnp.int32, shape, 1)
+    out_ref[:, width:] = mm(stacked, jnp.where(place, 1.0, 0.0).astype(bf16), TN).astype(bf16)
+    along = lax.axis_index("dp")
+    me = lax.axis_index("ep") * lax.axis_size("dp") + along
+    my_cold, my_hot = jnp.int32(0), jnp.int32(0)
+    for expert in range(slot_ref.shape[0]):
+        my_cold = jnp.where(slot_ref[expert] == me, expert, my_cold)
+    held = my_cold
+    for place in range(hot_list_ref.shape[0]):
+        my_cold = jnp.where(hot_list_ref[place] == held, -1, my_cold)
+        my_hot = jnp.where(along == place, hot_list_ref[place], my_hot)
+    row = lax.broadcasted_iota(jnp.int32, key_ref.shape, 0)
+    key_ref[...] = jnp.where(row == 0, my_cold, my_hot).astype(f32)
+
+
+def load_kernel(n, *refs):
+    copies = []
+    sems = refs[2 * n + 1]
+    for index in range(n):
+        src, dst = refs[index], refs[n + 1 + index]
+        rows = src.shape[-2]
+        parts = 4
+        for part in range(parts):
+            at = pl.ds(part * (rows // parts), rows // parts)
+            lead = (0,) * (len(src.shape) - 2)
+            if len(src.shape) == 4:
+                for third in range(src.shape[1]):
+                    copies.append((src.at[0, third, at], dst.at[0, third, at]))
+            else:
+                copies.append((src.at[lead + (at,)], dst.at[lead + (at,)]))
+    started = []
+    for number, (src, dst) in enumerate(copies):
+        copy = pltpu.make_async_copy(src, dst, sems.at[number])
+        copy.start()
+        started.append(copy)
+    for copy in started:
+        copy.wait()
+
+
+def routing(key_ref, metas, top, lanes):
+    meta = jnp.concatenate([m[...] for m in metas], axis=0).astype(jnp.float32)
+    total = meta.shape[0]
+    ids = meta[:, :top]
+    gains = meta[:, top : 2 * top] + meta[:, 2 * top : 3 * top] + meta[:, 3 * top : 4 * top]
+    is_cold = ids == key_ref[0:1, :top]
+    is_hot = ids == key_ref[1:2, :top]
+    cold_gain = jnp.sum(jnp.where(is_cold, gains, 0.0), axis=1, keepdims=True)
+    hot_gain = jnp.sum(jnp.where(is_hot, gains, 0.0), axis=1, keepdims=True)
+    mark = jnp.sum(jnp.where(is_cold, 1.0, 0.0), axis=1, keepdims=True)
+    marks = jnp.broadcast_to(mark, (total, lanes))
+    shape = (total, total)
+    below = lax.broadcasted_iota(jnp.int32, shape, 0) > lax.broadcasted_iota(jnp.int32, shape, 1)
+    rank = mm(jnp.where(below, 1.0, 0.0).astype(jnp.bfloat16), marks.astype(jnp.bfloat16))
+    lane = lax.broadcasted_iota(jnp.int32, (total, lanes), 1).astype(jnp.float32)
+    spread = jnp.where((marks > 0.5) & (rank == lane), 1.0, 0.0).astype(jnp.bfloat16)
+    return cold_gain, hot_gain, spread
+
+
+def load_rows(blocks, x_ref):
+    height, width = blocks[0].shape[0], x_ref.shape[1]
+    for index, block in enumerate(blocks):
+        x_ref[index * height : (index + 1) * height, :] = block[:, :width]
+
+
+def tails(blocks, width):
+    return [block.at[:, width : width + LANES] for block in blocks]
+
+
+def weigh(hidden, packed_ref, spread, hot_ref, cold_gain, hot_gain, out_ref, first=0):
+    width = out_ref.shape[1]
+    rows = slice(first, first + hidden.shape[0])
+    for start in range(0, width, STEP):
+        at = slice(start, start + STEP)
+        hot_part = mm(hidden, hot_ref[0, 2, :, at])
+        cold_part = mm(spread, packed_ref[:, at])
+        out_ref[rows, at] = (hot_gain * hot_part + cold_gain * cold_part).astype(out_ref.dtype)
+
+
+def keep_gains(cold_gain, hot_gain, gain_ref):
+    lane = lax.broadcasted_iota(jnp.int32, gain_ref.shape, 1)
+    gain_ref[...] = jnp.where(lane == 0, cold_gain, hot_gain)
+
+
+def early_kernel(n, top, cap, key_ref, *refs):
+    blocks, (hot_ref, hid_ref, pick_ref, spread_ref, gain_ref, x_ref) = refs[:n], refs[n:]
+    load_rows(blocks, x_ref)
+    metas = tails(blocks, x_ref.shape[1])
+    cold_gain, hot_gain, spread = routing(key_ref, metas, top, spread_ref.shape[1])
+    spread_ref[...] = spread
+    keep_gains(cold_gain, hot_gain, gain_ref)
+    x = x_ref[...]
+    hid_ref[...] = swish(mm(x, hot_ref[0, 0], NT), mm(x, hot_ref[0, 1], NT))
+    pick_ref[...] = mm(spread[:, :cap], x, TN).astype(jnp.bfloat16)
+
+
+def late_kernel(n, top, cap, key_ref, *refs):
+    blocks, (early_ref, gate_up_ref, down_ref, hot_ref), rest = refs[:n], refs[n : n + 4], refs[n + 4 :]
+    sib_ref, hid_ref, near_ref, far_ref, spread_ref, gain_ref, x_ref, c_ref, h_ref = rest
+    width = x_ref.shape[1]
+    units = down_ref.shape[1]
+    load_rows(blocks, x_ref)
+    cold_gain, hot_gain, spread = routing(key_ref, tails(blocks, width), top, spread_ref.shape[1])
+    spread_ref[...] = spread
+    keep_gains(cold_gain, hot_gain, gain_ref)
+    spread = spread[:, :cap]
+    x = x_ref[...]
+    n_early = early_ref.shape[0]
+    c_ref[:n_early, :] = early_ref[...]
+    c_ref[n_early:, :] = mm(spread, x, TN).astype(jnp.bfloat16)
+    cold = c_ref[...]
+    for start in range(0, units, STEP):
+        gate = mm(cold, gate_up_ref[0, :, start : start + STEP])
+        up = mm(cold, gate_up_ref[0, :, units + start : units + start + STEP])
+        h_ref[:, start : start + STEP] = swish(gate, up)
+    hidden = swish(mm(x, hot_ref[0, 0], NT), mm(x, hot_ref[0, 1], NT))
+    hid_ref[...] = hidden
+    half = hidden.shape[0] // 2
+    cold_hidden = h_ref[...]
+    for start in range(0, width, STEP):
+        at = slice(start, start + STEP)
+        packed = mm(cold_hidden, down_ref[0, :, at]).astype(jnp.bfloat16)
+        near_ref[:, at] = packed[:n_early]
+        far_ref[:, at] = packed[n_early:]
+    weigh(hidden[half:], far_ref, spread[half:], hot_ref, cold_gain[half:], hot_gain[half:], sib_ref)
+
+
+def result_kernel(own_rows, sib_rows, after, hid_ref, packed_ref, spread_ref, gain_ref, hot_ref, *refs):
+    outs = refs[after:]
+    cap = packed_ref.shape[0]
+    spans = ([sib_rows] if sib_rows else []) + [own_rows]
+    for (first, size), out_ref in zip(spans, outs):
+        at = slice(first, first + size)
+        weigh(
+            hid_ref[at, :],
+            packed_ref,
+            spread_ref[at, :cap],
+            hot_ref,
+            gain_ref[at, 0:1],
+            gain_ref[at, 1:2],
+            out_ref,
+        )
+
+
+def run_kernel(kernel, operands, outs, scratch, flops, moved, limit=12):
+    vmem = pl.BlockSpec(memory_space=pltpu.VMEM)
+    return pl.pallas_call(
+        kernel,
+        out_shape=[pltpu.VMEM(shape, dtype) for shape, dtype in outs],
+        in_specs=[vmem] * len(operands),
+        out_specs=[vmem] * len(outs),
+        scratch_shapes=[pltpu.VMEM(shape, dtype) for shape, dtype in scratch],
+        compiler_params=pltpu.CompilerParams(vmem_limit_bytes=limit * 2**20),
+        cost_estimate=pl.CostEstimate(flops=flops, bytes_accessed=moved, transcendentals=0),
+    )(*[pin(a) for a in operands])
+
+
+def load_weights(weights, after):
+    n = len(weights)
+    hbm = lambda a: pltpu.with_memory_space_constraint(a, pltpu.HBM)
+    return pl.pallas_call(
+        functools.partial(load_kernel, n),
+        out_shape=[pltpu.VMEM(w.shape, w.dtype) for w in weights],
+        in_specs=[pl.BlockSpec(memory_space=pltpu.HBM)] * n + [pl.BlockSpec(memory_space=pl.ANY)],
+        out_specs=[pl.BlockSpec(memory_space=pltpu.VMEM)] * n,
+        scratch_shapes=[pltpu.SemaphoreType.DMA((4 * n + 8,))],
+        compiler_params=pltpu.CompilerParams(vmem_limit_bytes=2**20),
+        cost_estimate=pl.CostEstimate(
+            flops=0, bytes_accessed=sum(w.size * 2 for w in weights), transcendentals=0
+        ),
+    )(*[hbm(w) for w in weights], after)
+
+
+def make_message(tokens, ids, gains, hot_list, slot_of):
+    rows, width = tokens.shape
+    vmem, smem = pl.BlockSpec(memory_space=pltpu.VMEM), pl.BlockSpec(memory_space=pltpu.SMEM)
+    hbm = lambda a: pltpu.with_memory_space_constraint(a, pltpu.HBM)
+    return pl.pallas_call(
+        message_kernel,
+        out_shape=[
+            pltpu.VMEM((rows, width + LANES), tokens.dtype),
+            pltpu.VMEM((8, LANES), jnp.float32),
+        ],
+        in_specs=[smem] * 2 + [vmem] * 3,
+        out_specs=[vmem] * 2,
+        compiler_params=pltpu.CompilerParams(vmem_limit_bytes=2**21),
+    )(*[hbm(a) for a in (hot_list, slot_of, tokens, ids, gains)])
+
+
+def ring_perms(n_dp):
+    chips = [(0, z) for z in range(n_dp)] + [(1, z) for z in reversed(range(n_dp))]
+    size = len(chips)
+
+    def device(place, core):
+        x, z = chips[place % size]
+        return (2 * x + core) * n_dp + z
+
+    def hop(by):
+        return [
+            (device(i, core), device(i + (-by if core else by), core))
+            for i in range(size)
+            for core in range(2)
+        ]
+
+    swap = [(device(i, core), device(i, 1 - core)) for i in range(size) for core in range(2)]
+    return hop, swap
+
+
+def dense_body(tokens, expert_ids, route_w, hot_list, slot_of, cold_gate_up, cold_down, hot_weights):
+    tok_rows, width = tokens.shape
+    top = expert_ids.shape[1]
+    n_hot, n_exp = hot_list.shape[0], slot_of.shape[0]
+    n_dp = lax.axis_size("dp")
+    units, hot_units = cold_down.shape[1], hot_weights.shape[3]
+    cold_cap = -(-(tok_rows * top - n_hot * tok_rows) // (n_exp - n_hot))
+    f32, bf16 = jnp.float32, jnp.bfloat16
+    hop, swap_pairs = ring_perms(n_dp)
+    axes = ("ep", "dp")
+    move = lambda a, by: lax.ppermute(a, axes, hop(by))
+    swap = lambda a: lax.ppermute(a, axes, swap_pairs)
+
+    message, key = make_message(tokens, expert_ids.T, route_w.T, hot_list, slot_of)
+    weights = (cold_gate_up, cold_down, jnp.swapaxes(hot_weights, 2, 3))
+    gate_up, down, hot = load_weights(weights, message)
+
+    tie = lambda *arrays: lax.optimization_barrier(arrays)
+    own = {0: message}
+    own[1], own[-1], hot = tie(move(message, 1), move(message, -1), hot)
+    for far in (2, 3):
+        own[far], own[-far] = tie(move(own[far - 1], 1), move(own[1 - far], -1))
+    own[4] = move(own[3], 1)
+    sib = {far: swap(own[far]) for far in own}
+
+    near, late = (3, -3, 2, -2, 1, -1, 0), (4,)
+    pad = lambda n: -(-n * cold_cap // 16) * 16
+    lanes = lambda cap: -(-cap // LANES) * LANES
+    n_near, n_late = 2 * len(near), 2 * len(late)
+    cap_near, cap_late = pad(n_near), pad(n_late)
+    rows_near, rows_late = n_near * tok_rows, n_late * tok_rows
+    gather = lambda fars: [own[f] for f in fars] + [sib[f] for f in fars]
+    hid_near, picked, spread_near, gain_near = run_kernel(
+        functools.partial(early_kernel, n_near, top, cap_near),
+        (key, *gather(near), hot),
+        [
+            ((rows_near, hot_units), bf16),
+            ((cap_near, width), bf16),
+            ((rows_near, lanes(cap_near)), bf16),
+            ((rows_near, LANES), f32),
+        ],
+        [((rows_near, width), bf16)],
+        2 * rows_near * width * (2 * hot_units + cap_near),
+        4 * rows_near * width,
+    )
+    back_late, hid_late, packed_near, packed_late, spread_late, gain_late = run_kernel(
+        functools.partial(late_kernel, n_late, top, cap_late),
+        (key, *gather(late), picked, gate_up, down, hot),
+        [
+            ((rows_late // 2, width), bf16),
+            ((rows_late, hot_units), bf16),
+            ((cap_near, width), bf16),
+            ((cap_late, width), bf16),
+            ((rows_late, lanes(cap_late)), bf16),
+            ((rows_late, LANES), f32),
+        ],
+        [
+            ((rows_late, width), bf16),
+            ((cap_near + cap_late, width), bf16),
+            ((cap_near + cap_late, units), bf16),
+        ],
+        2 * (cap_near + cap_late) * 3 * units * width,
+        4 * rows_late * width,
+    )
+
+    def results(fars, pool, sides, after=()):
+        hid, packed, spread, gain = sides
+        first, size = pool.index(fars[0]) * tok_rows, len(fars) * tok_rows
+        shift = len(pool) * tok_rows
+        outs = [((size, width), f32)]
+        if pool is near:
+            outs = [((size, width), bf16)] + outs
+        return run_kernel(
+            functools.partial(
+                result_kernel,
+                (first, size),
+                (first + shift, size) if pool is near else None,
+                len(after),
+            ),
+            (hid, packed, spread, gain, hot, *after),
+            outs,
+            [],
+            4 * size * width * (hot_units + packed.shape[0]),
+            8 * size * width,
+        )
+
+    total = {}
+
+    def add_up(fars, mine, other):
+        for index, far in enumerate(fars):
+            at = slice(index * tok_rows, (index + 1) * tok_rows)
+            total[far] = mine[at] + other[at].astype(f32)
+
+    low = lambda a: a.astype(bf16)
+    sides = (hid_near, packed_near, spread_near, gain_near)
+    from_late = swap(back_late)
+    (own_late,) = results(late, late, (hid_late, packed_late, spread_late, gain_late))
+    add_up(late, own_late, from_late)
+    first = low(total[4])
+    behind = move(first, -1)
+    back, mine = results((3, -3), near, sides, (first,))
+    add_up((3, -3), mine, swap(back))
+    ahead, behind = tie(low(total[-3]), low(total[3] + behind.astype(f32)))
+    rest = (2, -2, 1, -1, 0)
+    back, mine = results(rest, near, sides, (behind,))
+    ahead, behind = move(ahead, 1), move(behind, -1)
+    add_up(rest, mine, swap(back))
+    for far in (2, 1):
+        ahead, behind = tie(ahead, behind)
+        ahead, behind = tie(low(total[-far] + ahead.astype(f32)), low(total[far] + behind.astype(f32)))
+        ahead, behind = move(ahead, 1), move(behind, -1)
+    return low(total[0] + ahead.astype(f32) + behind.astype(f32))
+
+
+def body(tokens, expert_ids, *rest):
+    hot_list, slot_of = rest[1], rest[2]
+    every_row_hot = 2 * expert_ids.shape[1] == slot_of.shape[0]
+    two_columns = lax.axis_size("ep") == 4 and lax.axis_size("dp") == 4
+    chosen = dense_body if every_row_hot and two_columns else routed_body
+    return chosen(tokens, expert_ids, *rest)
+
+
 def solution(mesh):
     in_specs = (
         P(("groups", "ep", "dp"), None),

time: 187 us -> 61.9 us (0.33)
  blocking collectives: 52.6 us -> 0 us
  waiting for transfers between devices: 58.2 us -> 30.2 us
  local copies, waits for them, and re-layouts: 25.1 us -> 0 us
  matrix products: 14.6 us -> 0 us
  between operations: 13.6 us -> 0.12 us
  other arithmetic: 13.6 us -> 0.98 us
  Pallas kernels: 0 us -> 12.1 us
  starting transfers between devices: 8.84 us -> 18.4 us
    all_to_all x2 -> x0, blocking collectives: 52.6 us -> none  [the longest x1 31.8 us: body(): lax.all_to_all(cold_send, ('ep', 'dp'), split_axis=0, concat_axis=0, tile...]
    all_to_all x2 -> x0, waiting for transfers between devices: 36.4 us -> none  [the longest x1 24.9 us: body(): lax.all_to_all(swiglu_rows(lax.all_to_all(cold_send, ('ep', 'dp'), split_...]
    ppermute x0 -> x25, waiting for transfers between devices: none -> 30.2 us  [the longest x14 29.4 us: dense_body(): move = lambda a, by: lax.ppermute(a, axes, hop(by))]
    all_gather x1 -> x0, waiting for transfers between devices: 21.8 us -> none  [body(): gathered = lax.all_gather(hot_recv, 'ep', axis=0, tiled=True)]
    ppermute x0 -> x25, starting transfers between devices: none -> 18.4 us  [the longest x14 15.8 us: dense_body(): move = lambda a, by: lax.ppermute(a, axes, hop(by))]
    dot_general x5 -> x0, matrix products: 14.6 us -> none  [the longest x1 4.31 us: swiglu_rows(): both_out = jnp.dot(flat_in, gate_up, preferred_element_type=jnp.float32)]
    pallas_call x0 -> x7, Pallas kernels: none -> 12.1 us  [the longest x5 6.52 us: run_kernel(): pl.pallas_call(kernel, out_shape=[pltpu.VMEM(shape, dtype) for shape, dty...]
    gather x4 -> x0, local copies, waits for them, and re-layouts: 10.9 us -> none  [the longest x1 4.81 us: body(): picked = jnp.take(answers, positions, axis=0)]
  transfers between devices with their start and end apart: 4 -> 25, of which waited for: 3 -> 14; matrix products, arithmetic and copies ran while one was open for 12% -> 0% of each run, Pallas kernels for 0% -> 11%
where the time goes in v2:
time: 61.9 us; the launch traced here: 61.8 us
  waiting for transfers between devices  30.2 us (49%)
  starting transfers between devices  18.4 us (30%)
  Pallas kernels  12.1 us (20%)
  other arithmetic  0.98 us (2%)
    ppermute x14, waiting for transfers between devices, dense_body(): move = lambda a, by: lax.ppermute(a, axes, hop(by))  29.4 us
    ppermute x14, starting transfers between devices, dense_body(): move = lambda a, by: lax.ppermute(a, axes, hop(by))  15.8 us
    pallas_call x5, Pallas kernels, run_kernel(): pl.pallas_call(kernel, out_shape=[pltpu.VMEM(shape, dtype) for shape, dty...  6.52 us
    pallas_call x1, Pallas kernels, load_weights(): pl.pallas_call(functools.partial(load_kernel, n), out_shape=[pltpu.VMEM(w...  4.48 us
    ppermute x11, starting transfers between devices, dense_body(): swap = lambda a: lax.ppermute(a, axes, swap_pairs)  2.59 us
  transfers between devices with their start and end apart: 25, of which 14 were waited for; matrix products, arithmetic and copies ran while one was open for 0% of the time, Pallas kernels for 11%

profile of v2, /device:TPU:0, one launch (start us, length us, event | category | flops | bytes accessed | tf_op | source)
XLA Modules:
  0.0 61.8 jit_solution(13455910142696796467)
XLA Ops:
  0.0 1.1 %shard_map.82 = (bf16[32,2176]{1,0:T(8,128)(2,1)S(1)}, f32[8,128]{1,0:T(8,128)S(1)}) custom-call(s32[4]{0:T(128)} %hot_list_ref.1, s32[16]{0:T(128)} %slot_ref.1, bf16[32,2048]{1,0:T(8,128)(2,1)} %tok_ref.1, s32[8,32]{1,0:T(8,128)} %bitcast.4, f32[8,32]{1,0:T(8,128)} %bitcast.5), custom_call_target="tpu_custom_call" | custom-call | tf_op jit(solution)/shard_map/pallas_call | solution.py:311
  1.1 3.0 %collective-permute-start = (bf16[32,2176]{1,0:T(8,128)(2,1)S(1)}, bf16[32,2176]{1,0:T(8,128)(2,1)S(1)}, u32[]{:S(2)}, u32[]{:S(2)}) collective-permute-start(bf16[32,2176]{1,0:T(8,128)(2,1)S(1)} %get-tuple-element.42.refs_3_.refs_6_), channel_id=1, source_target_pairs={{0,1},{4,12},{1,2},{5,4},{2,3},{6,5},{3,11},{7,6},{11,10},{15,7},{... | collective-permute-start | bytes 417800 | tf_op jit(solution)/shard_map/ppermute | solution.py:352
  4.1 4.5 %shard_map.83 = (bf16[1,2048,1536]{2,1,0:T(8,128)(2,1)S(1)}, bf16[1,768,2048]{2,1,0:T(8,128)(2,1)S(1)}, bf16[1,3,192,2048]{3,2,1,0:T(8,128)(2,1)S(1)}) custom-call(bf16[1,2048,1536]{2,1,0:T(8,128)(2,1)} %refs_0_.1, bf16[1,768,2048]{2,1,0:T(8,128)(2,1)} %refs_1_.1, bf16[1,3,192,2048]{3,2,1,0:T(8,128)(2,1)} %bitcast.3, ...), custom_call_target="tpu_custom_call" | custom-call | bytes 11796480 | tf_op jit(solution)/shard_map/pallas_call | solution.py:294
  8.6 0.6 collective-permute-done.1.refs_5_
  9.2 1.6 %collective-permute-start.2 = (bf16[32,2176]{1,0:T(8,128)(2,1)S(1)}, bf16[32,2176]{1,0:T(8,128)(2,1)S(1)}, u32[]{:S(2)}, u32[]{:S(2)}) collective-permute-start(bf16[32,2176]{1,0:T(8,128)(2,1)S(1)} %collective-permute-done.refs_4_), channel_id=1, source_target_pairs={{0,1},{4,12},{1,2},{5,4},{2,3},{6,5},{3,11},{7,6},{11,10},{15,7},{... | collective-permute-start | bytes 417800 | tf_op jit(solution)/shard_map/ppermute | solution.py:352
  11.2 4.4 %collective-permute-done.2.refs_2_ = bf16[32,2176]{1,0:T(8,128)(2,1)S(1)} collective-permute-done((bf16[32,2176]{1,0:T(8,128)(2,1)S(1)}, bf16[32,2176]{1,0:T(8,128)(2,1)S(1)}, u32[]{:S(2)}, u32[]{:S(2)}) %collective-permute-start.2) | collective-permute-done | bytes 139296 | tf_op jit(solution)/shard_map/ppermute | solution.py:352
  15.8 1.6 %collective-permute-start.4 = (bf16[32,2176]{1,0:T(8,128)(2,1)S(1)}, bf16[32,2176]{1,0:T(8,128)(2,1)S(1)}, u32[]{:S(2)}, u32[]{:S(2)}) collective-permute-start(bf16[32,2176]{1,0:T(8,128)(2,1)S(1)} %collective-permute-done.2.refs_2_), channel_id=1, source_target_pairs={{0,1},{4,12},{1,2},{5,4},{2,3},{6,5},{3,11},{7,6},{11,10},{15,7},{... | collective-permute-start | bytes 417800 | tf_op jit(solution)/shard_map/ppermute | solution.py:352
  17.9 0.5 collective-permute-start.10
  18.4 4.0 %collective-permute-done.4.refs_0_ = bf16[32,2176]{1,0:T(8,128)(2,1)S(1)} collective-permute-done((bf16[32,2176]{1,0:T(8,128)(2,1)S(1)}, bf16[32,2176]{1,0:T(8,128)(2,1)S(1)}, u32[]{:S(2)}, u32[]{:S(2)}) %collective-permute-start.4) | collective-permute-done | bytes 139296 | tf_op jit(solution)/shard_map/ppermute | solution.py:352
  22.7 2.0 %collective-permute-start.13 = (bf16[32,2176]{1,0:T(8,128)(2,1)S(1)}, bf16[32,2176]{1,0:T(8,128)(2,1)S(1)}, u32[]{:S(2)}, u32[]{:S(2)}) collective-permute-start(bf16[32,2176]{1,0:T(8,128)(2,1)S(1)} %collective-permute-done.4.refs_0_), channel_id=1, source_target_pairs={{0,1},{4,12},{1,2},{5,4},{2,3},{6,5},{3,11},{7,6},{11,10},{15,7},{... | collective-permute-start | bytes 417800 | tf_op jit(solution)/shard_map/ppermute | solution.py:352
  24.7 0.5 collective-permute-start.9
  25.7 2.0 %collective-permute-done.13.refs_0_ = bf16[32,2176]{1,0:T(8,128)(2,1)S(1)} collective-permute-done((bf16[32,2176]{1,0:T(8,128)(2,1)S(1)}, bf16[32,2176]{1,0:T(8,128)(2,1)S(1)}, u32[]{:S(2)}, u32[]{:S(2)}) %collective-permute-start.13) | collective-permute-done | bytes 139296 | tf_op jit(solution)/shard_map/ppermute | solution.py:352
  27.8 1.7 %shard_map.84 = (bf16[448,192]{1,0:T(8,128)(2,1)S(1)}, bf16[160,2048]{1,0:T(8,128)(2,1)S(1)}, bf16[448,256]{1,0:T(8,128)(2,1)S(1)}, f32[448,128]{1,0:T(8,128)S(1)}) custom-call(f32[8,128]{1,0:T(8,128)S(1)} %get-tuple-element.41.key_ref, bf16[32,2176]{1,0:T(8,128)(2,1)S(1)} %collective-permute-done.4.refs_0_, ...), custom_call_target="tpu_custom_call" | custom-call | flops 998244352 | bytes 3670016 | tf_op jit(solution)/shard_map/pallas_call | solution.py:280
  29.5 3.0 %shard_map.85 = (bf16[32,2048]{1,0:T(8,128)(2,1)S(1)}, bf16[64,192]{1,0:T(8,128)(2,1)S(1)}, bf16[160,2048]{1,0:T(8,128)(2,1)S(1)}, bf16[32,2048]{1,0:T(8,128)(2,...) custom-call(f32[8,128]{1,0:T(8,128)S(1)} %get-tuple-element.41.key_ref, ...), custom_call_target="tpu_custom_call" | custom-call | flops 1811939328 | bytes 524288 | tf_op jit(solution)/shard_map/pallas_call | solution.py:280
  32.5 0.6 collective-permute-start.15
  33.4 0.7 %collective-permute-done.15 = bf16[32,2048]{1,0:T(8,128)(2,1)S(1)} collective-permute-done((bf16[32,2048]{1,0:T(8,128)(2,1)S(1)}, bf16[32,2048]{1,0:T(8,128)(2,1)S(1)}, u32[]{:S(2)}, u32[]{:S(2)}) %collective-permute-start.15) | collective-permute-done | bytes 131104 | tf_op jit(solution)/shard_map/ppermute | solution.py:353
  34.1 0.6 %shard_map.87 = (bf16[64,2048]{1,0:T(8,128)(2,1)S(1)}, f32[64,2048]{1,0:T(8,128)S(1)}) custom-call(bf16[448,192]{1,0:T(8,128)(2,1)S(1)} %get-tuple-element.51.hid_ref, bf16[160,2048]{1,0:T(8,128)(2,1)S(1)} %get-tuple-element.55.packed_ref, bf16[448,256]{1,0:T(8,128)(2,1)S(1)} %get-tuple-element.56.spread_ref, f32[448,128]{1,0:T(8,128)S(1)} %get-tuple-element.57.gain_ref, ...), custom_call_target="tpu_custom_call" | custom-call | flops 184549376 | bytes 1048576 | tf_op jit(solution)/shard_map/pallas_call | solution.py:280
  35.2 0.5 collective-permute-start.17
  35.6 4.5 %collective-permute-done.17 = bf16[32,2048]{1,0:T(8,128)(2,1)S(1)} collective-permute-done((bf16[32,2048]{1,0:T(8,128)(2,1)S(1)}, bf16[32,2048]{1,0:T(8,128)(2,1)S(1)}, u32[]{:S(2)}, u32[]{:S(2)}) %collective-permute-start.17) | collective-permute-done | bytes 131104 | tf_op jit(solution)/shard_map/ppermute | solution.py:352
  40.2 0.9 %shard_map.88 = (bf16[160,2048]{1,0:T(8,128)(2,1)S(1)}, f32[160,2048]{1,0:T(8,128)S(1)}) custom-call(bf16[448,192]{1,0:T(8,128)(2,1)S(1)} %get-tuple-element.51.hid_ref, bf16[160,2048]{1,0:T(8,128)(2,1)S(1)} %get-tuple-element.55.packed_ref, bf16[448,256]{1,0:T(8,128)(2,1)S(1)} %get-tuple-element.56.spread_ref, f32[448,128]{1,0:T(8,128)S(1)} %get-tuple-element.57.gain_ref, ...), custom_call_target="tpu_custom_call" | custom-call | flops 461373440 | bytes 2621440 | tf_op jit(solution)/shard_map/pallas_call | solution.py:280
  41.2 2.1 %collective-permute-start.19 = (bf16[32,2048]{1,0:T(8,128)(2,1)S(1)}, bf16[32,2048]{1,0:T(8,128)(2,1)S(1)}, u32[]{:S(2)}, u32[]{:S(2)}) collective-permute-start(bf16[32,2048]{1,0:T(8,128)(2,1)S(1)} %get-tuple-element.68), channel_id=1, source_target_pairs={{0,1},{4,12},{1,2},{5,4},{2,3},{6,5},{3,11},{7,6},{11,10},{15,7},{... | collective-permute-start | bytes 393224 | tf_op jit(solution)/shard_map/ppermute | solution.py:352
  43.3 4.2 %collective-permute-done.19 = bf16[32,2048]{1,0:T(8,128)(2,1)S(1)} collective-permute-done((bf16[32,2048]{1,0:T(8,128)(2,1)S(1)}, bf16[32,2048]{1,0:T(8,128)(2,1)S(1)}, u32[]{:S(2)}, u32[]{:S(2)}) %collective-permute-start.19) | collective-permute-done | bytes 131104 | tf_op jit(solution)/shard_map/ppermute | solution.py:352
  47.4 0.8 %collective-permute-done.20 = bf16[32,2048]{1,0:T(8,128)(2,1)S(1)} collective-permute-done((bf16[32,2048]{1,0:T(8,128)(2,1)S(1)}, bf16[32,2048]{1,0:T(8,128)(2,1)S(1)}, u32[]{:S(2)}, u32[]{:S(2)}) %collective-permute-start.20) | collective-permute-done | bytes 131104 | tf_op jit(solution)/shard_map/ppermute | solution.py:352
  48.3 1.5 %collective-permute-start.21 = (bf16[32,2048]{1,0:T(8,128)(2,1)S(1)}, bf16[32,2048]{1,0:T(8,128)(2,1)S(1)}, u32[]{:S(2)}, u32[]{:S(2)}) collective-permute-start(bf16[32,2048]{1,0:T(8,128)(2,1)S(1)} %get-tuple-element.71), channel_id=1, source_target_pairs={{0,1},{4,12},{1,2},{5,4},{2,3},{6,5},{3,11},{7,6},{11,10},{15,7},{... | collective-permute-start | bytes 393224 | tf_op jit(solution)/shard_map/ppermute | solution.py:352
  49.8 0.6 collective-permute-start.22
  50.4 3.1 %collective-permute-done.21 = bf16[32,2048]{1,0:T(8,128)(2,1)S(1)} collective-permute-done((bf16[32,2048]{1,0:T(8,128)(2,1)S(1)}, bf16[32,2048]{1,0:T(8,128)(2,1)S(1)}, u32[]{:S(2)}, u32[]{:S(2)}) %collective-permute-start.21) | collective-permute-done | bytes 131104 | tf_op jit(solution)/shard_map/ppermute | solution.py:352
  53.5 1.3 %collective-permute-done.22 = bf16[32,2048]{1,0:T(8,128)(2,1)S(1)} collective-permute-done((bf16[32,2048]{1,0:T(8,128)(2,1)S(1)}, bf16[32,2048]{1,0:T(8,128)(2,1)S(1)}, u32[]{:S(2)}, u32[]{:S(2)}) %collective-permute-start.22) | collective-permute-done | bytes 131104 | tf_op jit(solution)/shard_map/ppermute | solution.py:352
  54.9 1.2 %collective-permute-start.23 = (bf16[32,2048]{1,0:T(8,128)(2,1)S(1)}, bf16[32,2048]{1,0:T(8,128)(2,1)S(1)}, u32[]{:S(2)}, u32[]{:S(2)}) collective-permute-start(bf16[32,2048]{1,0:T(8,128)(2,1)S(1)} %get-tuple-element.75), channel_id=1, source_target_pairs={{0,1},{4,12},{1,2},{5,4},{2,3},{6,5},{3,11},{7,6},{11,10},{15,7},{... | collective-permute-start | bytes 393224 | tf_op jit(solution)/shard_map/ppermute | solution.py:352
  56.1 0.9 %collective-permute-start.24 = (bf16[32,2048]{1,0:T(8,128)(2,1)S(1)}, bf16[32,2048]{1,0:T(8,128)(2,1)S(1)}, u32[]{:S(2)}, u32[]{:S(2)}) collective-permute-start(bf16[32,2048]{1,0:T(8,128)(2,1)S(1)} %get-tuple-element.76), channel_id=1, source_target_pairs={{0,8},{4,5},{1,0},{5,6},{2,1},{6,7},{3,2},{7,15},{11,3},{15,14},{1... | collective-permute-start | bytes 393224 | tf_op jit(solution)/shard_map/ppermute | solution.py:352
  57.0 3.2 %collective-permute-done.23 = bf16[32,2048]{1,0:T(8,128)(2,1)S(1)} collective-permute-done((bf16[32,2048]{1,0:T(8,128)(2,1)S(1)}, bf16[32,2048]{1,0:T(8,128)(2,1)S(1)}, u32[]{:S(2)}, u32[]{:S(2)}) %collective-permute-start.23) | collective-permute-done | bytes 131104 | tf_op jit(solution)/shard_map/ppermute | solution.py:352
  60.1 1.0 %collective-permute-done.24 = bf16[32,2048]{1,0:T(8,128)(2,1)S(1)} collective-permute-done((bf16[32,2048]{1,0:T(8,128)(2,1)S(1)}, bf16[32,2048]{1,0:T(8,128)(2,1)S(1)}, u32[]{:S(2)}, u32[]{:S(2)}) %collective-permute-start.24) | collective-permute-done | bytes 131104 | tf_op jit(solution)/shard_map/ppermute | solution.py:352
  61.1 0.7 %add_convert_fusion = bf16[32,2048]{1,0:T(8,128)(2,1)} fusion(bf16[32,2048]{1,0:T(8,128)(2,1)S(1)} %collective-permute-done.24, bf16[32,2048]{1,0:T(8,128)(2,1)S(1)} %collective-permute-done.23, f32[160,2048]{1,0:T(8,128)S(1)} %get-tuple-element.66, bf16[160,2048]{1,0:T(8,128)(2,1)S(1)} %collective-permute-done.18), kind=kLoop, calls=%fused_computation | loop fusion | flops 458752 | bytes 786432 | tf_op jit(solution)/shard_map/convert_element_type | solution.py:435
  (30 shorter events, 3.0 us)
Async XLA Ops:
  1.1 7.5 %collective-permute-start = (bf16[32,2176]{1,0:T(8,128)(2,1)S(1)}, bf16[32,2176]{1,0:T(8,128)(2,1)S(1)}, u32[]{:S(2)}, u32[]{:S(2)}) collective-permute-start(bf16[32,2176]{1,0:T(8,128)(2,1)S(1)} %get-tuple-element.42.refs_3_.refs_6_), channel_id=1, source_target_pairs={{0,1},{4,12},{1,2},{5,4},{2,3},{6,5},{3,11},{7,6},{11,10},{15,7},{... | collective-permute-start | bytes 417800 | tf_op jit(solution)/shard_map/ppermute | solution.py:352
  4.1 5.1 %collective-permute-start.1 = (bf16[32,2176]{1,0:T(8,128)(2,1)S(1)}, bf16[32,2176]{1,0:T(8,128)(2,1)S(1)}, u32[]{:S(2)}, u32[]{:S(2)}) collective-permute-start(bf16[32,2176]{1,0:T(8,128)(2,1)S(1)} %get-tuple-element.42.refs_3_.refs_6_), channel_id=1, source_target_pairs={{0,8},{4,5},{1,0},{5,6},{2,1},{6,7},{3,2},{7,15},{11,3},{15,14},{1... | collective-permute-start | bytes 417800 | tf_op jit(solution)/shard_map/ppermute | solution.py:352
  9.2 6.4 %collective-permute-start.2 = (bf16[32,2176]{1,0:T(8,128)(2,1)S(1)}, bf16[32,2176]{1,0:T(8,128)(2,1)S(1)}, u32[]{:S(2)}, u32[]{:S(2)}) collective-permute-start(bf16[32,2176]{1,0:T(8,128)(2,1)S(1)} %collective-permute-done.refs_4_), channel_id=1, source_target_pairs={{0,1},{4,12},{1,2},{5,4},{2,3},{6,5},{3,11},{7,6},{11,10},{15,7},{... | collective-permute-start | bytes 417800 | tf_op jit(solution)/shard_map/ppermute | solution.py:352
  10.8 5.1 %collective-permute-start.3 = (bf16[32,2176]{1,0:T(8,128)(2,1)S(1)}, bf16[32,2176]{1,0:T(8,128)(2,1)S(1)}, u32[]{:S(2)}, u32[]{:S(2)}) collective-permute-start(bf16[32,2176]{1,0:T(8,128)(2,1)S(1)} %collective-permute-done.1.refs_5_), channel_id=1, source_target_pairs={{0,8},{4,5},{1,0},{5,6},{2,1},{6,7},{3,2},{7,15},{11,3},{15,14},{1... | collective-permute-start | bytes 417800 | tf_op jit(solution)/shard_map/ppermute | solution.py:352
  15.8 6.5 %collective-permute-start.4 = (bf16[32,2176]{1,0:T(8,128)(2,1)S(1)}, bf16[32,2176]{1,0:T(8,128)(2,1)S(1)}, u32[]{:S(2)}, u32[]{:S(2)}) collective-permute-start(bf16[32,2176]{1,0:T(8,128)(2,1)S(1)} %collective-permute-done.2.refs_2_), channel_id=1, source_target_pairs={{0,1},{4,12},{1,2},{5,4},{2,3},{6,5},{3,11},{7,6},{11,10},{15,7},{... | collective-permute-start | bytes 417800 | tf_op jit(solution)/shard_map/ppermute | solution.py:352
  17.4 5.3 %collective-permute-start.5 = (bf16[32,2176]{1,0:T(8,128)(2,1)S(1)}, bf16[32,2176]{1,0:T(8,128)(2,1)S(1)}, u32[]{:S(2)}, u32[]{:S(2)}) collective-permute-start(bf16[32,2176]{1,0:T(8,128)(2,1)S(1)} %collective-permute-done.3.refs_3_), channel_id=1, source_target_pairs={{0,8},{4,5},{1,0},{5,6},{2,1},{6,7},{3,2},{7,15},{11,3},{15,14},{1... | collective-permute-start | bytes 417800 | tf_op jit(solution)/shard_map/ppermute | solution.py:352
  17.9 6.9 %collective-permute-start.12 = (bf16[32,2176]{1,0:T(8,128)(2,1)S(1)}, bf16[32,2176]{1,0:T(8,128)(2,1)S(1)}, u32[]{:S(2)}, u32[]{:S(2)}) collective-permute-start(bf16[32,2176]{1,0:T(8,128)(2,1)S(1)} %get-tuple-element.42.refs_3_.refs_6_), channel_id=1, source_target_pairs={{0,4},{4,0},{1,5},{5,1},{2,6},{6,2},{3,7},{7,3},{11,15},{15,11},{1... | collective-permute-start | bytes 417800 | tf_op jit(solution)/shard_map/ppermute | solution.py:353
  17.9 7.4 %collective-permute-start.10 = (bf16[32,2176]{1,0:T(8,128)(2,1)S(1)}, bf16[32,2176]{1,0:T(8,128)(2,1)S(1)}, u32[]{:S(2)}, u32[]{:S(2)}) collective-permute-start(bf16[32,2176]{1,0:T(8,128)(2,1)S(1)} %collective-permute-done.refs_4_), channel_id=1, source_target_pairs={{0,4},{4,0},{1,5},{5,1},{2,6},{6,2},{3,7},{7,3},{11,15},{15,11},{1... | collective-permute-start | bytes 417800 | tf_op jit(solution)/shard_map/ppermute | solution.py:353
  18.4 6.9 %collective-permute-start.11 = (bf16[32,2176]{1,0:T(8,128)(2,1)S(1)}, bf16[32,2176]{1,0:T(8,128)(2,1)S(1)}, u32[]{:S(2)}, u32[]{:S(2)}) collective-permute-start(bf16[32,2176]{1,0:T(8,128)(2,1)S(1)} %collective-permute-done.1.refs_5_), channel_id=1, source_target_pairs={{0,4},{4,0},{1,5},{5,1},{2,6},{6,2},{3,7},{7,3},{11,15},{15,11},{1... | collective-permute-start | bytes 417800 | tf_op jit(solution)/shard_map/ppermute | solution.py:353
  22.7 5.1 %collective-permute-start.13 = (bf16[32,2176]{1,0:T(8,128)(2,1)S(1)}, bf16[32,2176]{1,0:T(8,128)(2,1)S(1)}, u32[]{:S(2)}, u32[]{:S(2)}) collective-permute-start(bf16[32,2176]{1,0:T(8,128)(2,1)S(1)} %collective-permute-done.4.refs_0_), channel_id=1, source_target_pairs={{0,1},{4,12},{1,2},{5,4},{2,3},{6,5},{3,11},{7,6},{11,10},{15,7},{... | collective-permute-start | bytes 417800 | tf_op jit(solution)/shard_map/ppermute | solution.py:352
  24.7 3.0 %collective-permute-start.8 = (bf16[32,2176]{1,0:T(8,128)(2,1)S(1)}, bf16[32,2176]{1,0:T(8,128)(2,1)S(1)}, u32[]{:S(2)}, u32[]{:S(2)}) collective-permute-start(bf16[32,2176]{1,0:T(8,128)(2,1)S(1)} %collective-permute-done.2.refs_2_), channel_id=1, source_target_pairs={{0,4},{4,0},{1,5},{5,1},{2,6},{6,2},{3,7},{7,3},{11,15},{15,11},{1... | collective-permute-start | bytes 417800 | tf_op jit(solution)/shard_map/ppermute | solution.py:353
  24.7 3.0 %collective-permute-start.9 = (bf16[32,2176]{1,0:T(8,128)(2,1)S(1)}, bf16[32,2176]{1,0:T(8,128)(2,1)S(1)}, u32[]{:S(2)}, u32[]{:S(2)}) collective-permute-start(bf16[32,2176]{1,0:T(8,128)(2,1)S(1)} %collective-permute-done.3.refs_3_), channel_id=1, source_target_pairs={{0,4},{4,0},{1,5},{5,1},{2,6},{6,2},{3,7},{7,3},{11,15},{15,11},{1... | collective-permute-start | bytes 417800 | tf_op jit(solution)/shard_map/ppermute | solution.py:353
  25.2 2.5 %collective-permute-start.6 = (bf16[32,2176]{1,0:T(8,128)(2,1)S(1)}, bf16[32,2176]{1,0:T(8,128)(2,1)S(1)}, u32[]{:S(2)}, u32[]{:S(2)}) collective-permute-start(bf16[32,2176]{1,0:T(8,128)(2,1)S(1)} %collective-permute-done.4.refs_0_), channel_id=1, source_target_pairs={{0,4},{4,0},{1,5},{5,1},{2,6},{6,2},{3,7},{7,3},{11,15},{15,11},{1... | collective-permute-start | bytes 417800 | tf_op jit(solution)/shard_map/ppermute | solution.py:353
  25.3 2.5 %collective-permute-start.7 = (bf16[32,2176]{1,0:T(8,128)(2,1)S(1)}, bf16[32,2176]{1,0:T(8,128)(2,1)S(1)}, u32[]{:S(2)}, u32[]{:S(2)}) collective-permute-start(bf16[32,2176]{1,0:T(8,128)(2,1)S(1)} %collective-permute-done.5.refs_1_), channel_id=1, source_target_pairs={{0,4},{4,0},{1,5},{5,1},{2,6},{6,2},{3,7},{7,3},{11,15},{15,11},{1... | collective-permute-start | bytes 417800 | tf_op jit(solution)/shard_map/ppermute | solution.py:353
  27.7 1.8 %collective-permute-start.14 = (bf16[32,2176]{1,0:T(8,128)(2,1)S(1)}, bf16[32,2176]{1,0:T(8,128)(2,1)S(1)}, u32[]{:S(2)}, u32[]{:S(2)}) collective-permute-start(bf16[32,2176]{1,0:T(8,128)(2,1)S(1)} %collective-permute-done.13.refs_0_), channel_id=1, source_target_pairs={{0,4},{4,0},{1,5},{5,1},{2,6},{6,2},{3,7},{7,3},{11,15},{15,11},{1... | collective-permute-start | bytes 417800 | tf_op jit(solution)/shard_map/ppermute | solution.py:353
  32.5 1.5 %collective-permute-start.15 = (bf16[32,2048]{1,0:T(8,128)(2,1)S(1)}, bf16[32,2048]{1,0:T(8,128)(2,1)S(1)}, u32[]{:S(2)}, u32[]{:S(2)}) collective-permute-start(bf16[32,2048]{1,0:T(8,128)(2,1)S(1)} %get-tuple-element.62), channel_id=1, source_target_pairs={{0,4},{4,0},{1,5},{5,1},{2,6},{6,2},{3,7},{7,3},{11,15},{15,11},{1... | collective-permute-start | bytes 393224 | tf_op jit(solution)/shard_map/ppermute | solution.py:353
  34.7 5.4 %collective-permute-start.16 = (bf16[64,2048]{1,0:T(8,128)(2,1)S(1)}, bf16[64,2048]{1,0:T(8,128)(2,1)S(1)}, u32[]{:S(2)}, u32[]{:S(2)}) collective-permute-start(bf16[64,2048]{1,0:T(8,128)(2,1)S(1)} %get-tuple-element.64), channel_id=1, source_target_pairs={{0,4},{4,0},{1,5},{5,1},{2,6},{6,2},{3,7},{7,3},{11,15},{15,11},{1... | collective-permute-start | bytes 786440 | tf_op jit(solution)/shard_map/ppermute | solution.py:353
  35.2 5.0 %collective-permute-start.17 = (bf16[32,2048]{1,0:T(8,128)(2,1)S(1)}, bf16[32,2048]{1,0:T(8,128)(2,1)S(1)}, u32[]{:S(2)}, u32[]{:S(2)}) collective-permute-start(bf16[32,2048]{1,0:T(8,128)(2,1)S(1)} %add_convert_fusion.7.refs_0_), channel_id=1, source_target_pairs={{0,8},{4,5},{1,0},{5,6},{2,1},{6,7},{3,2},{7,15},{11,3},{15,14},{1... | collective-permute-start | bytes 393224 | tf_op jit(solution)/shard_map/ppermute | solution.py:352
  41.1 7.1 %collective-permute-start.18 = (bf16[160,2048]{1,0:T(8,128)(2,1)S(1)}, bf16[160,2048]{1,0:T(8,128)(2,1)S(1)}, u32[]{:S(2)}, u32[]{:S(2)}) collective-permute-start(bf16[160,2048]{1,0:T(8,128)(2,1)S(1)} %get-tuple-element.67), channel_id=1, source_target_pairs={{0,4},{4,0},{1,5},{5,1},{2,6},{6,2},{3,7},{7,3},{11,15},{15,11},{1... | collective-permute-start | bytes 1966088 | tf_op jit(solution)/shard_map/ppermute | solution.py:353
  41.2 6.2 %collective-permute-start.19 = (bf16[32,2048]{1,0:T(8,128)(2,1)S(1)}, bf16[32,2048]{1,0:T(8,128)(2,1)S(1)}, u32[]{:S(2)}, u32[]{:S(2)}) collective-permute-start(bf16[32,2048]{1,0:T(8,128)(2,1)S(1)} %get-tuple-element.68), channel_id=1, source_target_pairs={{0,1},{4,12},{1,2},{5,4},{2,3},{6,5},{3,11},{7,6},{11,10},{15,7},{... | collective-permute-start | bytes 393224 | tf_op jit(solution)/shard_map/ppermute | solution.py:352
  43.3 5.0 %collective-permute-start.20 = (bf16[32,2048]{1,0:T(8,128)(2,1)S(1)}, bf16[32,2048]{1,0:T(8,128)(2,1)S(1)}, u32[]{:S(2)}, u32[]{:S(2)}) collective-permute-start(bf16[32,2048]{1,0:T(8,128)(2,1)S(1)} %get-tuple-element.65.refs_0_), channel_id=1, source_target_pairs={{0,8},{4,5},{1,0},{5,6},{2,1},{6,7},{3,2},{7,15},{11,3},{15,14},{1... | collective-permute-start | bytes 393224 | tf_op jit(solution)/shard_map/ppermute | solution.py:352
  48.3 5.1 %collective-permute-start.21 = (bf16[32,2048]{1,0:T(8,128)(2,1)S(1)}, bf16[32,2048]{1,0:T(8,128)(2,1)S(1)}, u32[]{:S(2)}, u32[]{:S(2)}) collective-permute-start(bf16[32,2048]{1,0:T(8,128)(2,1)S(1)} %get-tuple-element.71), channel_id=1, source_target_pairs={{0,1},{4,12},{1,2},{5,4},{2,3},{6,5},{3,11},{7,6},{11,10},{15,7},{... | collective-permute-start | bytes 393224 | tf_op jit(solution)/shard_map/ppermute | solution.py:352
  49.8 5.0 %collective-permute-start.22 = (bf16[32,2048]{1,0:T(8,128)(2,1)S(1)}, bf16[32,2048]{1,0:T(8,128)(2,1)S(1)}, u32[]{:S(2)}, u32[]{:S(2)}) collective-permute-start(bf16[32,2048]{1,0:T(8,128)(2,1)S(1)} %get-tuple-element.72), channel_id=1, source_target_pairs={{0,8},{4,5},{1,0},{5,6},{2,1},{6,7},{3,2},{7,15},{11,3},{15,14},{1... | collective-permute-start | bytes 393224 | tf_op jit(solution)/shard_map/ppermute | solution.py:352
  54.9 5.2 %collective-permute-start.23 = (bf16[32,2048]{1,0:T(8,128)(2,1)S(1)}, bf16[32,2048]{1,0:T(8,128)(2,1)S(1)}, u32[]{:S(2)}, u32[]{:S(2)}) collective-permute-start(bf16[32,2048]{1,0:T(8,128)(2,1)S(1)} %get-tuple-element.75), channel_id=1, source_target_pairs={{0,1},{4,12},{1,2},{5,4},{2,3},{6,5},{3,11},{7,6},{11,10},{15,7},{... | collective-permute-start | bytes 393224 | tf_op jit(solution)/shard_map/ppermute | solution.py:352
  56.1 5.0 %collective-permute-start.24 = (bf16[32,2048]{1,0:T(8,128)(2,1)S(1)}, bf16[32,2048]{1,0:T(8,128)(2,1)S(1)}, u32[]{:S(2)}, u32[]{:S(2)}) collective-permute-start(bf16[32,2048]{1,0:T(8,128)(2,1)S(1)} %get-tuple-element.76), channel_id=1, source_target_pairs={{0,8},{4,5},{1,0},{5,6},{2,1},{6,7},{3,2},{7,15},{11,3},{15,14},{1... | collective-permute-start | bytes 393224 | tf_op jit(solution)/shard_map/ppermute | solution.py:352

commit v3 on v2

--- a/solution.py
+++ b/solution.py
@@ -359,12 +359,11 @@
     tie = lambda *arrays: lax.optimization_barrier(arrays)
     own = {0: message}
     own[1], own[-1], hot = tie(move(message, 1), move(message, -1), hot)
-    for far in (2, 3):
-        own[far], own[-far] = tie(move(own[far - 1], 1), move(own[1 - far], -1))
-    own[4] = move(own[3], 1)
+    own[2], own[-2] = tie(move(own[1], 1), move(own[-1], -1))
+    own[4], own[3], own[-3] = move(own[2], 2), move(own[2], 1), move(own[-2], -1)
     sib = {far: swap(own[far]) for far in own}
 
-    near, late = (3, -3, 2, -2, 1, -1, 0), (4,)
+    near, late = (2, -2, 1, -1, 0), (4, 3, -3)
     pad = lambda n: -(-n * cold_cap // 16) * 16
     lanes = lambda cap: -(-cap // LANES) * LANES
     n_near, n_late = 2 * len(near), 2 * len(late)
@@ -437,15 +436,11 @@
     from_late = swap(back_late)
     (own_late,) = results(late, late, (hid_late, packed_late, spread_late, gain_late))
     add_up(late, own_late, from_late)
-    first = low(total[4])
-    behind = move(first, -1)
-    back, mine = results((3, -3), near, sides, (first,))
-    add_up((3, -3), mine, swap(back))
-    ahead, behind = tie(low(total[-3]), low(total[3] + behind.astype(f32)))
-    rest = (2, -2, 1, -1, 0)
-    back, mine = results(rest, near, sides, (behind,))
-    ahead, behind = move(ahead, 1), move(behind, -1)
-    add_up(rest, mine, swap(back))
+    first, ahead, behind = tie(low(total[4]), low(total[-3]), low(total[3]))
+    back, mine = results(near, near, sides, (first,))
+    first, ahead, behind = move(first, -2), move(ahead, 1), move(behind, -1)
+    add_up(near, mine, swap(back))
+    total[2] = total[2] + first.astype(f32)
     for far in (2, 1):
         ahead, behind = tie(ahead, behind)
         ahead, behind = tie(low(total[-far] + ahead.astype(f32)), low(total[far] + behind.astype(f32)))

time: 61.9 us -> 56.2 us (0.908)
  waiting for transfers between devices: 30.2 us -> 22.9 us
  starting transfers between devices: 18.4 us -> 20.8 us
  Pallas kernels: 12.1 us -> 11.2 us
    ppermute x14, waiting for transfers between devices: 29.4 us -> 21.9 us  [dense_body(): move = lambda a, by: lax.ppermute(a, axes, hop(by))]
    ppermute x14, starting transfers between devices: 15.8 us -> 18.3 us  [dense_body(): move = lambda a, by: lax.ppermute(a, axes, hop(by))]
    pallas_call x5 -> x4, Pallas kernels: 6.52 us -> 5.6 us  [run_kernel(): pl.pallas_call(kernel, out_shape=[pltpu.VMEM(shape, dtype) for shape, dty...]
    ppermute x11 -> x10, starting transfers between devices: 2.59 us -> 2.52 us  [dense_body(): swap = lambda a: lax.ppermute(a, axes, swap_pairs)]
  transfers between devices with their start and end apart: 25 -> 24, of which waited for: 14 -> 12; matrix products, arithmetic and copies ran while one was open for 0% -> 0% of each run, Pallas kernels for 11% -> 11%
where the time goes in v3:
time: 56.2 us; the launch traced here: 56 us
  waiting for transfers between devices  22.9 us (41%)
  starting transfers between devices  20.8 us (37%)
  Pallas kernels  11.2 us (20%)
  other arithmetic  1 us (2%)
    ppermute x14, waiting for transfers between devices, dense_body(): move = lambda a, by: lax.ppermute(a, axes, hop(by))  21.9 us
    ppermute x14, starting transfers between devices, dense_body(): move = lambda a, by: lax.ppermute(a, axes, hop(by))  18.3 us
    pallas_call x4, Pallas kernels, run_kernel(): pl.pallas_call(kernel, out_shape=[pltpu.VMEM(shape, dtype) for shape, dty...  5.6 us
    pallas_call x1, Pallas kernels, load_weights(): pl.pallas_call(functools.partial(load_kernel, n), out_shape=[pltpu.VMEM(w...  4.48 us
    ppermute x10, starting transfers between devices, dense_body(): swap = lambda a: lax.ppermute(a, axes, swap_pairs)  2.52 us
  transfers between devices with their start and end apart: 24, of which 12 were waited for; matrix products, arithmetic and copies ran while one was open for 0% of the time, Pallas kernels for 11%

profile of v3, /device:TPU:0, one launch (start us, length us, event | category | flops | bytes accessed | tf_op | source)
XLA Modules:
  0.0 56.0 jit_solution(9342708713368230264)
XLA Ops:
  0.0 1.1 %shard_map.82 = (bf16[32,2176]{1,0:T(8,128)(2,1)S(1)}, f32[8,128]{1,0:T(8,128)S(1)}) custom-call(s32[4]{0:T(128)} %hot_list_ref.1, s32[16]{0:T(128)} %slot_ref.1, bf16[32,2048]{1,0:T(8,128)(2,1)} %tok_ref.1, s32[8,32]{1,0:T(8,128)} %bitcast.4, f32[8,32]{1,0:T(8,128)} %bitcast.5), custom_call_target="tpu_custom_call" | custom-call | tf_op jit(solution)/shard_map/pallas_call | solution.py:311
  1.1 2.9 %collective-permute-start.1 = (bf16[32,2176]{1,0:T(8,128)(2,1)S(1)}, bf16[32,2176]{1,0:T(8,128)(2,1)S(1)}, u32[]{:S(2)}, u32[]{:S(2)}) collective-permute-start(bf16[32,2176]{1,0:T(8,128)(2,1)S(1)} %get-tuple-element.39.refs_3_.refs_4_), channel_id=1, source_target_pairs={{0,8},{4,5},{1,0},{5,6},{2,1},{6,7},{3,2},{7,15},{11,3},{15,14},{1... | collective-permute-start | bytes 417800 | tf_op jit(solution)/shard_map/ppermute | solution.py:352
  4.2 4.5 %shard_map.83 = (bf16[1,2048,1536]{2,1,0:T(8,128)(2,1)S(1)}, bf16[1,768,2048]{2,1,0:T(8,128)(2,1)S(1)}, bf16[1,3,192,2048]{3,2,1,0:T(8,128)(2,1)S(1)}) custom-call(bf16[1,2048,1536]{2,1,0:T(8,128)(2,1)} %refs_0_.1, bf16[1,768,2048]{2,1,0:T(8,128)(2,1)} %refs_1_.1, bf16[1,3,192,2048]{3,2,1,0:T(8,128)(2,1)} %bitcast.3, ...), custom_call_target="tpu_custom_call" | custom-call | bytes 11796480 | tf_op jit(solution)/shard_map/pallas_call | solution.py:294
  9.1 1.6 %collective-permute-start.2 = (bf16[32,2176]{1,0:T(8,128)(2,1)S(1)}, bf16[32,2176]{1,0:T(8,128)(2,1)S(1)}, u32[]{:S(2)}, u32[]{:S(2)}) collective-permute-start(bf16[32,2176]{1,0:T(8,128)(2,1)S(1)} %collective-permute-done.refs_2_), channel_id=1, source_target_pairs={{0,1},{4,12},{1,2},{5,4},{2,3},{6,5},{3,11},{7,6},{11,10},{15,7},{... | collective-permute-start | bytes 417800 | tf_op jit(solution)/shard_map/ppermute | solution.py:352
  11.1 0.5 collective-permute-start.6
  11.6 3.6 %collective-permute-done.2.refs_0_ = bf16[32,2176]{1,0:T(8,128)(2,1)S(1)} collective-permute-done((bf16[32,2176]{1,0:T(8,128)(2,1)S(1)}, bf16[32,2176]{1,0:T(8,128)(2,1)S(1)}, u32[]{:S(2)}, u32[]{:S(2)}) %collective-permute-start.2) | collective-permute-done | bytes 139296 | tf_op jit(solution)/shard_map/ppermute | solution.py:352
  15.2 0.6 %collective-permute-done.3.refs_1_ = bf16[32,2176]{1,0:T(8,128)(2,1)S(1)} collective-permute-done((bf16[32,2176]{1,0:T(8,128)(2,1)S(1)}, bf16[32,2176]{1,0:T(8,128)(2,1)S(1)}, u32[]{:S(2)}, u32[]{:S(2)}) %collective-permute-start.3) | collective-permute-done | bytes 139296 | tf_op jit(solution)/shard_map/ppermute | solution.py:352
  15.8 1.0 %collective-permute-start.11 = (bf16[32,2176]{1,0:T(8,128)(2,1)S(1)}, bf16[32,2176]{1,0:T(8,128)(2,1)S(1)}, u32[]{:S(2)}, u32[]{:S(2)}) collective-permute-start(bf16[32,2176]{1,0:T(8,128)(2,1)S(1)} %collective-permute-done.3.refs_1_), channel_id=1, source_target_pairs={{0,8},{4,5},{1,0},{5,6},{2,1},{6,7},{3,2},{7,15},{11,3},{15,14},{1... | collective-permute-start | bytes 417800 | tf_op jit(solution)/shard_map/ppermute | solution.py:352
  16.8 1.0 %collective-permute-start.10 = (bf16[32,2176]{1,0:T(8,128)(2,1)S(1)}, bf16[32,2176]{1,0:T(8,128)(2,1)S(1)}, u32[]{:S(2)}, u32[]{:S(2)}) collective-permute-start(bf16[32,2176]{1,0:T(8,128)(2,1)S(1)} %collective-permute-done.2.refs_0_), channel_id=1, source_target_pairs={{0,1},{4,12},{1,2},{5,4},{2,3},{6,5},{3,11},{7,6},{11,10},{15,7},{... | collective-permute-start | bytes 417800 | tf_op jit(solution)/shard_map/ppermute | solution.py:352
  17.8 2.6 %collective-permute-start.9 = (bf16[32,2176]{1,0:T(8,128)(2,1)S(1)}, bf16[32,2176]{1,0:T(8,128)(2,1)S(1)}, u32[]{:S(2)}, u32[]{:S(2)}) collective-permute-start(bf16[32,2176]{1,0:T(8,128)(2,1)S(1)} %collective-permute-done.2.refs_0_), channel_id=1, source_target_pairs={{0,2},{4,13},{1,3},{5,12},{2,11},{6,4},{3,10},{7,5},{11,9},{15,6},... | collective-permute-start | bytes 417800 | tf_op jit(solution)/shard_map/ppermute | solution.py:352
  20.4 0.5 collective-permute-start.4
  20.9 1.6 %collective-permute-done.11.refs_2_ = bf16[32,2176]{1,0:T(8,128)(2,1)S(1)} collective-permute-done((bf16[32,2176]{1,0:T(8,128)(2,1)S(1)}, bf16[32,2176]{1,0:T(8,128)(2,1)S(1)}, u32[]{:S(2)}, u32[]{:S(2)}) %collective-permute-start.11) | collective-permute-done | bytes 139296 | tf_op jit(solution)/shard_map/ppermute | solution.py:352
  22.5 0.5 collective-permute-start.13
  23.0 2.6 %collective-permute-done.9.refs_0_ = bf16[32,2176]{1,0:T(8,128)(2,1)S(1)} collective-permute-done((bf16[32,2176]{1,0:T(8,128)(2,1)S(1)}, bf16[32,2176]{1,0:T(8,128)(2,1)S(1)}, u32[]{:S(2)}, u32[]{:S(2)}) %collective-permute-start.9) | collective-permute-done | bytes 139296 | tf_op jit(solution)/shard_map/ppermute | solution.py:352
  25.6 1.3 %shard_map.84 = (bf16[320,192]{1,0:T(8,128)(2,1)S(1)}, bf16[112,2048]{1,0:T(8,128)(2,1)S(1)}, bf16[320,128]{1,0:T(8,128)(2,1)S(1)}, f32[320,128]{1,0:T(8,128)S(1)}) custom-call(f32[8,128]{1,0:T(8,128)S(1)} %get-tuple-element.38.key_ref, bf16[32,2176]{1,0:T(8,128)(2,1)S(1)} %collective-permute-done.2.refs_0_, ...), custom_call_target="tpu_custom_call" | custom-call | flops 650117120 | bytes 2621440 | tf_op jit(solution)/shard_map/pallas_call | solution.py:280
  27.0 3.1 %shard_map.85 = (bf16[96,2048]{1,0:T(8,128)(2,1)S(1)}, bf16[192,192]{1,0:T(8,128)(2,1)S(1)}, bf16[112,2048]{1,0:T(8,128)(2,1)S(1)}, bf16[80,2048]{1,0:T(8,128)(2...) custom-call(f32[8,128]{1,0:T(8,128)S(1)} %get-tuple-element.38.key_ref, ...), custom_call_target="tpu_custom_call" | custom-call | flops 1811939328 | bytes 1572864 | tf_op jit(solution)/shard_map/pallas_call | solution.py:280
  30.1 0.5 collective-permute-start.15
  31.0 1.0 %collective-permute-done.15 = bf16[96,2048]{1,0:T(8,128)(2,1)S(1)} collective-permute-done((bf16[96,2048]{1,0:T(8,128)(2,1)S(1)}, bf16[96,2048]{1,0:T(8,128)(2,1)S(1)}, u32[]{:S(2)}, u32[]{:S(2)}) %collective-permute-start.15) | collective-permute-done | bytes 393248 | tf_op jit(solution)/shard_map/ppermute | solution.py:353
  32.0 0.9 %shard_map.87 = (bf16[160,2048]{1,0:T(8,128)(2,1)S(1)}, f32[160,2048]{1,0:T(8,128)S(1)}) custom-call(bf16[320,192]{1,0:T(8,128)(2,1)S(1)} %get-tuple-element.46.hid_ref, bf16[112,2048]{1,0:T(8,128)(2,1)S(1)} %get-tuple-element.50.packed_ref, bf16[320,128]{1,0:T(8,128)(2,1)S(1)} %get-tuple-element.51.spread_ref, f32[320,128]{1,0:T(8,128)S(1)} %get-tuple-element.52.gain_ref, ...), custom_call_target="tpu_custom_call" | custom-call | flops 398458880 | bytes 2621440 | tf_op jit(solution)/shard_map/pallas_call | solution.py:280
  33.4 0.7 %collective-permute-start.17 = (bf16[32,2048]{1,0:T(8,128)(2,1)S(1)}, bf16[32,2048]{1,0:T(8,128)(2,1)S(1)}, u32[]{:S(2)}, u32[]{:S(2)}) collective-permute-start(bf16[32,2048]{1,0:T(8,128)(2,1)S(1)} %get-tuple-element.61), channel_id=1, source_target_pairs={{0,1},{4,12},{1,2},{5,4},{2,3},{6,5},{3,11},{7,6},{11,10},{15,7},{... | collective-permute-start | bytes 393224 | tf_op jit(solution)/shard_map/ppermute | solution.py:352
  34.0 1.3 %collective-permute-start.18 = (bf16[32,2048]{1,0:T(8,128)(2,1)S(1)}, bf16[32,2048]{1,0:T(8,128)(2,1)S(1)}, u32[]{:S(2)}, u32[]{:S(2)}) collective-permute-start(bf16[32,2048]{1,0:T(8,128)(2,1)S(1)} %get-tuple-element.62), channel_id=1, source_target_pairs={{0,8},{4,5},{1,0},{5,6},{2,1},{6,7},{3,2},{7,15},{11,3},{15,14},{1... | collective-permute-start | bytes 393224 | tf_op jit(solution)/shard_map/ppermute | solution.py:352
  35.4 1.6 %collective-permute-start.19 = (bf16[32,2048]{1,0:T(8,128)(2,1)S(1)}, bf16[32,2048]{1,0:T(8,128)(2,1)S(1)}, u32[]{:S(2)}, u32[]{:S(2)}) collective-permute-start(bf16[32,2048]{1,0:T(8,128)(2,1)S(1)} %get-tuple-element.58.refs_0_), channel_id=1, source_target_pairs={{0,9},{4,6},{1,8},{5,7},{2,0},{6,15},{3,1},{7,14},{11,2},{15,13},{... | collective-permute-start | bytes 393224 | tf_op jit(solution)/shard_map/ppermute | solution.py:352
  37.0 2.0 %collective-permute-done.17 = bf16[32,2048]{1,0:T(8,128)(2,1)S(1)} collective-permute-done((bf16[32,2048]{1,0:T(8,128)(2,1)S(1)}, bf16[32,2048]{1,0:T(8,128)(2,1)S(1)}, u32[]{:S(2)}, u32[]{:S(2)}) %collective-permute-start.17) | collective-permute-done | bytes 131104 | tf_op jit(solution)/shard_map/ppermute | solution.py:352
  39.0 2.5 %collective-permute-done.19 = bf16[32,2048]{1,0:T(8,128)(2,1)S(1)} collective-permute-done((bf16[32,2048]{1,0:T(8,128)(2,1)S(1)}, bf16[32,2048]{1,0:T(8,128)(2,1)S(1)}, u32[]{:S(2)}, u32[]{:S(2)}) %collective-permute-start.19) | collective-permute-done | bytes 131104 | tf_op jit(solution)/shard_map/ppermute | solution.py:352
  41.7 2.3 %collective-permute-start.20 = (bf16[32,2048]{1,0:T(8,128)(2,1)S(1)}, bf16[32,2048]{1,0:T(8,128)(2,1)S(1)}, u32[]{:S(2)}, u32[]{:S(2)}) collective-permute-start(bf16[32,2048]{1,0:T(8,128)(2,1)S(1)} %get-tuple-element.65), channel_id=1, source_target_pairs={{0,1},{4,12},{1,2},{5,4},{2,3},{6,5},{3,11},{7,6},{11,10},{15,7},{... | collective-permute-start | bytes 393224 | tf_op jit(solution)/shard_map/ppermute | solution.py:352
  43.9 0.6 %collective-permute-start.21 = (bf16[32,2048]{1,0:T(8,128)(2,1)S(1)}, bf16[32,2048]{1,0:T(8,128)(2,1)S(1)}, u32[]{:S(2)}, u32[]{:S(2)}) collective-permute-start(bf16[32,2048]{1,0:T(8,128)(2,1)S(1)} %get-tuple-element.66), channel_id=1, source_target_pairs={{0,8},{4,5},{1,0},{5,6},{2,1},{6,7},{3,2},{7,15},{11,3},{15,14},{1... | collective-permute-start | bytes 393224 | tf_op jit(solution)/shard_map/ppermute | solution.py:352
  44.6 4.2 %collective-permute-done.20 = bf16[32,2048]{1,0:T(8,128)(2,1)S(1)} collective-permute-done((bf16[32,2048]{1,0:T(8,128)(2,1)S(1)}, bf16[32,2048]{1,0:T(8,128)(2,1)S(1)}, u32[]{:S(2)}, u32[]{:S(2)}) %collective-permute-start.20) | collective-permute-done | bytes 131104 | tf_op jit(solution)/shard_map/ppermute | solution.py:352
  49.0 1.3 %collective-permute-start.22 = (bf16[32,2048]{1,0:T(8,128)(2,1)S(1)}, bf16[32,2048]{1,0:T(8,128)(2,1)S(1)}, u32[]{:S(2)}, u32[]{:S(2)}) collective-permute-start(bf16[32,2048]{1,0:T(8,128)(2,1)S(1)} %get-tuple-element.69), channel_id=1, source_target_pairs={{0,1},{4,12},{1,2},{5,4},{2,3},{6,5},{3,11},{7,6},{11,10},{15,7},{... | collective-permute-start | bytes 393224 | tf_op jit(solution)/shard_map/ppermute | solution.py:352
  50.3 0.7 %collective-permute-start.23 = (bf16[32,2048]{1,0:T(8,128)(2,1)S(1)}, bf16[32,2048]{1,0:T(8,128)(2,1)S(1)}, u32[]{:S(2)}, u32[]{:S(2)}) collective-permute-start(bf16[32,2048]{1,0:T(8,128)(2,1)S(1)} %get-tuple-element.70), channel_id=1, source_target_pairs={{0,8},{4,5},{1,0},{5,6},{2,1},{6,7},{3,2},{7,15},{11,3},{15,14},{1... | collective-permute-start | bytes 393224 | tf_op jit(solution)/shard_map/ppermute | solution.py:352
  51.1 3.7 %collective-permute-done.22 = bf16[32,2048]{1,0:T(8,128)(2,1)S(1)} collective-permute-done((bf16[32,2048]{1,0:T(8,128)(2,1)S(1)}, bf16[32,2048]{1,0:T(8,128)(2,1)S(1)}, u32[]{:S(2)}, u32[]{:S(2)}) %collective-permute-start.22) | collective-permute-done | bytes 131104 | tf_op jit(solution)/shard_map/ppermute | solution.py:352
  54.8 0.5 collective-permute-done.23
  55.3 0.7 %add_convert_fusion = bf16[32,2048]{1,0:T(8,128)(2,1)} fusion(bf16[32,2048]{1,0:T(8,128)(2,1)S(1)} %collective-permute-done.23, bf16[32,2048]{1,0:T(8,128)(2,1)S(1)} %collective-permute-done.22, f32[160,2048]{1,0:T(8,128)S(1)} %get-tuple-element.59, bf16[160,2048]{1,0:T(8,128)(2,1)S(1)} %collective-permute-done.16), kind=kLoop, calls=%fused_computation.6 | loop fusion | flops 458752 | bytes 786432 | tf_op jit(solution)/shard_map/convert_element_type | solution.py:434
  (26 shorter events, 2.3 us)
Async XLA Ops:
  1.1 7.6 %collective-permute-start.1 = (bf16[32,2176]{1,0:T(8,128)(2,1)S(1)}, bf16[32,2176]{1,0:T(8,128)(2,1)S(1)}, u32[]{:S(2)}, u32[]{:S(2)}) collective-permute-start(bf16[32,2176]{1,0:T(8,128)(2,1)S(1)} %get-tuple-element.39.refs_3_.refs_4_), channel_id=1, source_target_pairs={{0,8},{4,5},{1,0},{5,6},{2,1},{6,7},{3,2},{7,15},{11,3},{15,14},{1... | collective-permute-start | bytes 417800 | tf_op jit(solution)/shard_map/ppermute | solution.py:352
  4.0 5.1 %collective-permute-start = (bf16[32,2176]{1,0:T(8,128)(2,1)S(1)}, bf16[32,2176]{1,0:T(8,128)(2,1)S(1)}, u32[]{:S(2)}, u32[]{:S(2)}) collective-permute-start(bf16[32,2176]{1,0:T(8,128)(2,1)S(1)} %get-tuple-element.39.refs_3_.refs_4_), channel_id=1, source_target_pairs={{0,1},{4,12},{1,2},{5,4},{2,3},{6,5},{3,11},{7,6},{11,10},{15,7},{... | collective-permute-start | bytes 417800 | tf_op jit(solution)/shard_map/ppermute | solution.py:352
  9.1 6.1 %collective-permute-start.2 = (bf16[32,2176]{1,0:T(8,128)(2,1)S(1)}, bf16[32,2176]{1,0:T(8,128)(2,1)S(1)}, u32[]{:S(2)}, u32[]{:S(2)}) collective-permute-start(bf16[32,2176]{1,0:T(8,128)(2,1)S(1)} %collective-permute-done.refs_2_), channel_id=1, source_target_pairs={{0,1},{4,12},{1,2},{5,4},{2,3},{6,5},{3,11},{7,6},{11,10},{15,7},{... | collective-permute-start | bytes 417800 | tf_op jit(solution)/shard_map/ppermute | solution.py:352
  10.7 5.1 %collective-permute-start.3 = (bf16[32,2176]{1,0:T(8,128)(2,1)S(1)}, bf16[32,2176]{1,0:T(8,128)(2,1)S(1)}, u32[]{:S(2)}, u32[]{:S(2)}) collective-permute-start(bf16[32,2176]{1,0:T(8,128)(2,1)S(1)} %collective-permute-done.1.refs_3_), channel_id=1, source_target_pairs={{0,8},{4,5},{1,0},{5,6},{2,1},{6,7},{3,2},{7,15},{11,3},{15,14},{1... | collective-permute-start | bytes 417800 | tf_op jit(solution)/shard_map/ppermute | solution.py:352
  11.1 6.7 %collective-permute-start.8 = (bf16[32,2176]{1,0:T(8,128)(2,1)S(1)}, bf16[32,2176]{1,0:T(8,128)(2,1)S(1)}, u32[]{:S(2)}, u32[]{:S(2)}) collective-permute-start(bf16[32,2176]{1,0:T(8,128)(2,1)S(1)} %get-tuple-element.39.refs_3_.refs_4_), channel_id=1, source_target_pairs={{0,4},{4,0},{1,5},{5,1},{2,6},{6,2},{3,7},{7,3},{11,15},{15,11},{1... | collective-permute-start | bytes 417800 | tf_op jit(solution)/shard_map/ppermute | solution.py:353
  11.1 9.3 %collective-permute-start.6 = (bf16[32,2176]{1,0:T(8,128)(2,1)S(1)}, bf16[32,2176]{1,0:T(8,128)(2,1)S(1)}, u32[]{:S(2)}, u32[]{:S(2)}) collective-permute-start(bf16[32,2176]{1,0:T(8,128)(2,1)S(1)} %collective-permute-done.refs_2_), channel_id=1, source_target_pairs={{0,4},{4,0},{1,5},{5,1},{2,6},{6,2},{3,7},{7,3},{11,15},{15,11},{1... | collective-permute-start | bytes 417800 | tf_op jit(solution)/shard_map/ppermute | solution.py:353
  11.6 8.8 %collective-permute-start.7 = (bf16[32,2176]{1,0:T(8,128)(2,1)S(1)}, bf16[32,2176]{1,0:T(8,128)(2,1)S(1)}, u32[]{:S(2)}, u32[]{:S(2)}) collective-permute-start(bf16[32,2176]{1,0:T(8,128)(2,1)S(1)} %collective-permute-done.1.refs_3_), channel_id=1, source_target_pairs={{0,4},{4,0},{1,5},{5,1},{2,6},{6,2},{3,7},{7,3},{11,15},{15,11},{1... | collective-permute-start | bytes 417800 | tf_op jit(solution)/shard_map/ppermute | solution.py:353
  15.8 6.7 %collective-permute-start.11 = (bf16[32,2176]{1,0:T(8,128)(2,1)S(1)}, bf16[32,2176]{1,0:T(8,128)(2,1)S(1)}, u32[]{:S(2)}, u32[]{:S(2)}) collective-permute-start(bf16[32,2176]{1,0:T(8,128)(2,1)S(1)} %collective-permute-done.3.refs_1_), channel_id=1, source_target_pairs={{0,8},{4,5},{1,0},{5,6},{2,1},{6,7},{3,2},{7,15},{11,3},{15,14},{1... | collective-permute-start | bytes 417800 | tf_op jit(solution)/shard_map/ppermute | solution.py:352
  16.8 5.7 %collective-permute-start.10 = (bf16[32,2176]{1,0:T(8,128)(2,1)S(1)}, bf16[32,2176]{1,0:T(8,128)(2,1)S(1)}, u32[]{:S(2)}, u32[]{:S(2)}) collective-permute-start(bf16[32,2176]{1,0:T(8,128)(2,1)S(1)} %collective-permute-done.2.refs_0_), channel_id=1, source_target_pairs={{0,1},{4,12},{1,2},{5,4},{2,3},{6,5},{3,11},{7,6},{11,10},{15,7},{... | collective-permute-start | bytes 417800 | tf_op jit(solution)/shard_map/ppermute | solution.py:352
  17.8 7.8 %collective-permute-start.9 = (bf16[32,2176]{1,0:T(8,128)(2,1)S(1)}, bf16[32,2176]{1,0:T(8,128)(2,1)S(1)}, u32[]{:S(2)}, u32[]{:S(2)}) collective-permute-start(bf16[32,2176]{1,0:T(8,128)(2,1)S(1)} %collective-permute-done.2.refs_0_), channel_id=1, source_target_pairs={{0,2},{4,13},{1,3},{5,12},{2,11},{6,4},{3,10},{7,5},{11,9},{15,6},... | collective-permute-start | bytes 417800 | tf_op jit(solution)/shard_map/ppermute | solution.py:352
  20.4 5.2 %collective-permute-start.5 = (bf16[32,2176]{1,0:T(8,128)(2,1)S(1)}, bf16[32,2176]{1,0:T(8,128)(2,1)S(1)}, u32[]{:S(2)}, u32[]{:S(2)}) collective-permute-start(bf16[32,2176]{1,0:T(8,128)(2,1)S(1)} %collective-permute-done.3.refs_1_), channel_id=1, source_target_pairs={{0,4},{4,0},{1,5},{5,1},{2,6},{6,2},{3,7},{7,3},{11,15},{15,11},{1... | collective-permute-start | bytes 417800 | tf_op jit(solution)/shard_map/ppermute | solution.py:353
  20.4 5.2 %collective-permute-start.4 = (bf16[32,2176]{1,0:T(8,128)(2,1)S(1)}, bf16[32,2176]{1,0:T(8,128)(2,1)S(1)}, u32[]{:S(2)}, u32[]{:S(2)}) collective-permute-start(bf16[32,2176]{1,0:T(8,128)(2,1)S(1)} %collective-permute-done.2.refs_0_), channel_id=1, source_target_pairs={{0,4},{4,0},{1,5},{5,1},{2,6},{6,2},{3,7},{7,3},{11,15},{15,11},{1... | collective-permute-start | bytes 417800 | tf_op jit(solution)/shard_map/ppermute | solution.py:353
  22.5 4.4 %collective-permute-start.14 = (bf16[32,2176]{1,0:T(8,128)(2,1)S(1)}, bf16[32,2176]{1,0:T(8,128)(2,1)S(1)}, u32[]{:S(2)}, u32[]{:S(2)}) collective-permute-start(bf16[32,2176]{1,0:T(8,128)(2,1)S(1)} %collective-permute-done.11.refs_2_), channel_id=1, source_target_pairs={{0,4},{4,0},{1,5},{5,1},{2,6},{6,2},{3,7},{7,3},{11,15},{15,11},{1... | collective-permute-start | bytes 417800 | tf_op jit(solution)/shard_map/ppermute | solution.py:353
  22.5 4.4 %collective-permute-start.13 = (bf16[32,2176]{1,0:T(8,128)(2,1)S(1)}, bf16[32,2176]{1,0:T(8,128)(2,1)S(1)}, u32[]{:S(2)}, u32[]{:S(2)}) collective-permute-start(bf16[32,2176]{1,0:T(8,128)(2,1)S(1)} %collective-permute-done.10.refs_1_), channel_id=1, source_target_pairs={{0,4},{4,0},{1,5},{5,1},{2,6},{6,2},{3,7},{7,3},{11,15},{15,11},{1... | collective-permute-start | bytes 417800 | tf_op jit(solution)/shard_map/ppermute | solution.py:353
  25.6 1.4 %collective-permute-start.12 = (bf16[32,2176]{1,0:T(8,128)(2,1)S(1)}, bf16[32,2176]{1,0:T(8,128)(2,1)S(1)}, u32[]{:S(2)}, u32[]{:S(2)}) collective-permute-start(bf16[32,2176]{1,0:T(8,128)(2,1)S(1)} %collective-permute-done.9.refs_0_), channel_id=1, source_target_pairs={{0,4},{4,0},{1,5},{5,1},{2,6},{6,2},{3,7},{7,3},{11,15},{15,11},{1... | collective-permute-start | bytes 417800 | tf_op jit(solution)/shard_map/ppermute | solution.py:353
  30.1 1.9 %collective-permute-start.15 = (bf16[96,2048]{1,0:T(8,128)(2,1)S(1)}, bf16[96,2048]{1,0:T(8,128)(2,1)S(1)}, u32[]{:S(2)}, u32[]{:S(2)}) collective-permute-start(bf16[96,2048]{1,0:T(8,128)(2,1)S(1)} %get-tuple-element.57), channel_id=1, source_target_pairs={{0,4},{4,0},{1,5},{5,1},{2,6},{6,2},{3,7},{7,3},{11,15},{15,11},{1... | collective-permute-start | bytes 1179656 | tf_op jit(solution)/shard_map/ppermute | solution.py:353
  32.9 8.6 %collective-permute-start.16 = (bf16[160,2048]{1,0:T(8,128)(2,1)S(1)}, bf16[160,2048]{1,0:T(8,128)(2,1)S(1)}, u32[]{:S(2)}, u32[]{:S(2)}) collective-permute-start(bf16[160,2048]{1,0:T(8,128)(2,1)S(1)} %get-tuple-element.60), channel_id=1, source_target_pairs={{0,4},{4,0},{1,5},{5,1},{2,6},{6,2},{3,7},{7,3},{11,15},{15,11},{1... | collective-permute-start | bytes 1966088 | tf_op jit(solution)/shard_map/ppermute | solution.py:353
  33.4 5.7 %collective-permute-start.17 = (bf16[32,2048]{1,0:T(8,128)(2,1)S(1)}, bf16[32,2048]{1,0:T(8,128)(2,1)S(1)}, u32[]{:S(2)}, u32[]{:S(2)}) collective-permute-start(bf16[32,2048]{1,0:T(8,128)(2,1)S(1)} %get-tuple-element.61), channel_id=1, source_target_pairs={{0,1},{4,12},{1,2},{5,4},{2,3},{6,5},{3,11},{7,6},{11,10},{15,7},{... | collective-permute-start | bytes 393224 | tf_op jit(solution)/shard_map/ppermute | solution.py:352
  34.0 5.0 %collective-permute-start.18 = (bf16[32,2048]{1,0:T(8,128)(2,1)S(1)}, bf16[32,2048]{1,0:T(8,128)(2,1)S(1)}, u32[]{:S(2)}, u32[]{:S(2)}) collective-permute-start(bf16[32,2048]{1,0:T(8,128)(2,1)S(1)} %get-tuple-element.62), channel_id=1, source_target_pairs={{0,8},{4,5},{1,0},{5,6},{2,1},{6,7},{3,2},{7,15},{11,3},{15,14},{1... | collective-permute-start | bytes 393224 | tf_op jit(solution)/shard_map/ppermute | solution.py:352
  35.4 6.2 %collective-permute-start.19 = (bf16[32,2048]{1,0:T(8,128)(2,1)S(1)}, bf16[32,2048]{1,0:T(8,128)(2,1)S(1)}, u32[]{:S(2)}, u32[]{:S(2)}) collective-permute-start(bf16[32,2048]{1,0:T(8,128)(2,1)S(1)} %get-tuple-element.58.refs_0_), channel_id=1, source_target_pairs={{0,9},{4,6},{1,8},{5,7},{2,0},{6,15},{3,1},{7,14},{11,2},{15,13},{... | collective-permute-start | bytes 393224 | tf_op jit(solution)/shard_map/ppermute | solution.py:352
  41.7 7.1 %collective-permute-start.20 = (bf16[32,2048]{1,0:T(8,128)(2,1)S(1)}, bf16[32,2048]{1,0:T(8,128)(2,1)S(1)}, u32[]{:S(2)}, u32[]{:S(2)}) collective-permute-start(bf16[32,2048]{1,0:T(8,128)(2,1)S(1)} %get-tuple-element.65), channel_id=1, source_target_pairs={{0,1},{4,12},{1,2},{5,4},{2,3},{6,5},{3,11},{7,6},{11,10},{15,7},{... | collective-permute-start | bytes 393224 | tf_op jit(solution)/shard_map/ppermute | solution.py:352
  43.9 5.0 %collective-permute-start.21 = (bf16[32,2048]{1,0:T(8,128)(2,1)S(1)}, bf16[32,2048]{1,0:T(8,128)(2,1)S(1)}, u32[]{:S(2)}, u32[]{:S(2)}) collective-permute-start(bf16[32,2048]{1,0:T(8,128)(2,1)S(1)} %get-tuple-element.66), channel_id=1, source_target_pairs={{0,8},{4,5},{1,0},{5,6},{2,1},{6,7},{3,2},{7,15},{11,3},{15,14},{1... | collective-permute-start | bytes 393224 | tf_op jit(solution)/shard_map/ppermute | solution.py:352
  49.0 5.8 %collective-permute-start.22 = (bf16[32,2048]{1,0:T(8,128)(2,1)S(1)}, bf16[32,2048]{1,0:T(8,128)(2,1)S(1)}, u32[]{:S(2)}, u32[]{:S(2)}) collective-permute-start(bf16[32,2048]{1,0:T(8,128)(2,1)S(1)} %get-tuple-element.69), channel_id=1, source_target_pairs={{0,1},{4,12},{1,2},{5,4},{2,3},{6,5},{3,11},{7,6},{11,10},{15,7},{... | collective-permute-start | bytes 393224 | tf_op jit(solution)/shard_map/ppermute | solution.py:352
  50.3 5.0 %collective-permute-start.23 = (bf16[32,2048]{1,0:T(8,128)(2,1)S(1)}, bf16[32,2048]{1,0:T(8,128)(2,1)S(1)}, u32[]{:S(2)}, u32[]{:S(2)}) collective-permute-start(bf16[32,2048]{1,0:T(8,128)(2,1)S(1)} %get-tuple-element.70), channel_id=1, source_target_pairs={{0,8},{4,5},{1,0},{5,6},{2,1},{6,7},{3,2},{7,15},{11,3},{15,14},{1... | collective-permute-start | bytes 393224 | tf_op jit(solution)/shard_map/ppermute | solution.py:352

commit v4 on v3

--- a/solution.py
+++ b/solution.py
@@ -119,21 +119,25 @@
     return (gate / (1.0 + jnp.exp(-gate)) * up).astype(jnp.bfloat16)
 
 
-def message_kernel(hot_list_ref, slot_ref, tok_ref, ids_ref, gain_ref, out_ref, key_ref):
-    width = tok_ref.shape[1]
-    out_ref[:, :width] = tok_ref[...]
-    top = ids_ref.shape[0]
+def message_kernel(hot_list_ref, slot_ref, *refs):
+    out_ref, key_ref = refs[-2:]
     bf16, f32 = jnp.bfloat16, jnp.float32
-    gains = gain_ref[...]
-    terms = [ids_ref[...].astype(f32)]
-    for _ in range(3):
-        term = gains.astype(bf16).astype(f32)
-        terms.append(term)
-        gains = gains - term
-    stacked = jnp.concatenate(terms, axis=0).astype(bf16)
-    shape = (4 * top, LANES)
-    place = lax.broadcasted_iota(jnp.int32, shape, 0) == lax.broadcasted_iota(jnp.int32, shape, 1)
-    out_ref[:, width:] = mm(stacked, jnp.where(place, 1.0, 0.0).astype(bf16), TN).astype(bf16)
+    for half in range(2):
+        tok_ref, ids_ref, gain_ref = refs[3 * half : 3 * half + 3]
+        height, width = tok_ref.shape
+        at = slice(half * height, (half + 1) * height)
+        out_ref[at, :width] = tok_ref[...]
+        gains = gain_ref[...]
+        terms = [ids_ref[...].astype(f32)]
+        for _ in range(3):
+            term = gains.astype(bf16).astype(f32)
+            terms.append(term)
+            gains = gains - term
+        stacked = jnp.concatenate(terms, axis=0).astype(bf16)
+        shape = (stacked.shape[0], LANES)
+        row, lane = (lax.broadcasted_iota(jnp.int32, shape, axis) for axis in (0, 1))
+        place = jnp.where(row == lane, 1.0, 0.0).astype(bf16)
+        out_ref[at, width:] = mm(stacked, place, TN).astype(bf16)
     along = lax.axis_index("dp")
     me = lax.axis_index("ep") * lax.axis_size("dp") + along
     my_cold, my_hot = jnp.int32(0), jnp.int32(0)
@@ -171,8 +175,8 @@
         copy.wait()
 
 
-def routing(key_ref, metas, top, lanes):
-    meta = jnp.concatenate([m[...] for m in metas], axis=0).astype(jnp.float32)
+def routing(key_ref, meta, top, lanes):
+    meta = meta.astype(jnp.float32)
     total = meta.shape[0]
     ids = meta[:, :top]
     gains = meta[:, top : 2 * top] + meta[:, 2 * top : 3 * top] + meta[:, 3 * top : 4 * top]
@@ -190,14 +194,13 @@
     return cold_gain, hot_gain, spread
 
 
-def load_rows(blocks, x_ref):
-    height, width = blocks[0].shape[0], x_ref.shape[1]
-    for index, block in enumerate(blocks):
-        x_ref[index * height : (index + 1) * height, :] = block[:, :width]
-
-
-def tails(blocks, width):
-    return [block.at[:, width : width + LANES] for block in blocks]
+def load_rows(blocks, spans, x_ref):
+    width, at, tails = x_ref.shape[1], 0, []
+    for block, (first, size) in zip(blocks, spans):
+        x_ref[at : at + size, :] = block[first : first + size, :width]
+        tails.append(block[first : first + size, width : width + LANES])
+        at += size
+    return jnp.concatenate(tails, axis=0)
 
 
 def weigh(hidden, packed_ref, spread, hot_ref, cold_gain, hot_gain, out_ref, first=0):
@@ -215,11 +218,11 @@
     gain_ref[...] = jnp.where(lane == 0, cold_gain, hot_gain)
 
 
-def early_kernel(n, top, cap, key_ref, *refs):
-    blocks, (hot_ref, hid_ref, pick_ref, spread_ref, gain_ref, x_ref) = refs[:n], refs[n:]
-    load_rows(blocks, x_ref)
-    metas = tails(blocks, x_ref.shape[1])
-    cold_gain, hot_gain, spread = routing(key_ref, metas, top, spread_ref.shape[1])
+def early_kernel(spans, top, cap, key_ref, *refs):
+    n = len(spans)
+    hot_ref, hid_ref, pick_ref, spread_ref, gain_ref, x_ref = refs[n:]
+    meta = load_rows(refs[:n], spans, x_ref)
+    cold_gain, hot_gain, spread = routing(key_ref, meta, top, spread_ref.shape[1])
     spread_ref[...] = spread
     keep_gains(cold_gain, hot_gain, gain_ref)
     x = x_ref[...]
@@ -227,13 +230,14 @@
     pick_ref[...] = mm(spread[:, :cap], x, TN).astype(jnp.bfloat16)
 
 
-def late_kernel(n, top, cap, key_ref, *refs):
-    blocks, (early_ref, gate_up_ref, down_ref, hot_ref), rest = refs[:n], refs[n : n + 4], refs[n + 4 :]
+def late_kernel(spans, top, cap, key_ref, *refs):
+    n = len(spans)
+    (early_ref, gate_up_ref, down_ref, hot_ref), rest = refs[n : n + 4], refs[n + 4 :]
     sib_ref, hid_ref, near_ref, far_ref, spread_ref, gain_ref, x_ref, c_ref, h_ref = rest
     width = x_ref.shape[1]
     units = down_ref.shape[1]
-    load_rows(blocks, x_ref)
-    cold_gain, hot_gain, spread = routing(key_ref, tails(blocks, width), top, spread_ref.shape[1])
+    meta = load_rows(refs[:n], spans, x_ref)
+    cold_gain, hot_gain, spread = routing(key_ref, meta, top, spread_ref.shape[1])
     spread_ref[...] = spread
     keep_gains(cold_gain, hot_gain, gain_ref)
     spread = spread[:, :cap]
@@ -304,20 +308,20 @@
     )(*[hbm(w) for w in weights], after)
 
 
-def make_message(tokens, ids, gains, hot_list, slot_of):
-    rows, width = tokens.shape
+def make_message(hot_list, slot_of, *sides):
+    rows, width = sides[0].shape
     vmem, smem = pl.BlockSpec(memory_space=pltpu.VMEM), pl.BlockSpec(memory_space=pltpu.SMEM)
     hbm = lambda a: pltpu.with_memory_space_constraint(a, pltpu.HBM)
     return pl.pallas_call(
         message_kernel,
         out_shape=[
-            pltpu.VMEM((rows, width + LANES), tokens.dtype),
+            pltpu.VMEM((2 * rows, width + LANES), sides[0].dtype),
             pltpu.VMEM((8, LANES), jnp.float32),
         ],
-        in_specs=[smem] * 2 + [vmem] * 3,
+        in_specs=[smem] * 2 + [vmem] * 6,
         out_specs=[vmem] * 2,
         compiler_params=pltpu.CompilerParams(vmem_limit_bytes=2**21),
-    )(*[hbm(a) for a in (hot_list, slot_of, tokens, ids, gains)])
+    )(hbm(hot_list), hbm(slot_of), *[hbm(a) for a in sides[:3]], *[pin(a) for a in sides[3:]])
 
 
 def ring_perms(n_dp):
@@ -328,9 +332,9 @@
         x, z = chips[place % size]
         return (2 * x + core) * n_dp + z
 
-    def hop(by):
+    def hop(by, cross):
         return [
-            (device(i, core), device(i + (-by if core else by), core))
+            (device(i, core), device(i + (-by if core else by), core ^ cross))
             for i in range(size)
             for core in range(2)
         ]
@@ -349,30 +353,34 @@
     f32, bf16 = jnp.float32, jnp.bfloat16
     hop, swap_pairs = ring_perms(n_dp)
     axes = ("ep", "dp")
-    move = lambda a, by: lax.ppermute(a, axes, hop(by))
+    move = lambda a, by: lax.ppermute(a, axes, hop(by, 0))
+    cross = lambda a, by: lax.ppermute(a, axes, hop(by, 1))
     swap = lambda a: lax.ppermute(a, axes, swap_pairs)
-
-    message, key = make_message(tokens, expert_ids.T, route_w.T, hot_list, slot_of)
+    tie = lambda *arrays: lax.optimization_barrier(arrays)
+
+    given = (tokens, expert_ids, route_w)
+    sides = [a for side in (given, [swap(a) for a in given]) for a in side]
+    sides = [a.T if index % 3 else a for index, a in enumerate(sides)]
+    message, key = make_message(hot_list, slot_of, *sides)
     weights = (cold_gate_up, cold_down, jnp.swapaxes(hot_weights, 2, 3))
     gate_up, down, hot = load_weights(weights, message)
 
-    tie = lambda *arrays: lax.optimization_barrier(arrays)
-    own = {0: message}
-    own[1], own[-1], hot = tie(move(message, 1), move(message, -1), hot)
-    own[2], own[-2] = tie(move(own[1], 1), move(own[-1], -1))
-    own[4], own[3], own[-3] = move(own[2], 2), move(own[2], 1), move(own[-2], -1)
-    sib = {far: swap(own[far]) for far in own}
-
-    near, late = (2, -2, 1, -1, 0), (4, 3, -3)
+    two = move(message, 2)
+    later, hot = tie(message, hot)
+    one = move(later, 1)
+    two, hot = tie(two, hot)
+    four, three = move(two[:tok_rows], 2), move(two, 1)
+
+    whole, half, rest = (0, 2 * tok_rows), (0, tok_rows), (tok_rows, tok_rows)
+    near_rows = ((two, whole), (one, whole), (message, half), (swap(two), whole), (swap(one), whole), (message, rest))
+    late_rows = ((four, half), (three, whole), (swap(four), half), (swap(three), whole))
     pad = lambda n: -(-n * cold_cap // 16) * 16
     lanes = lambda cap: -(-cap // LANES) * LANES
-    n_near, n_late = 2 * len(near), 2 * len(late)
-    cap_near, cap_late = pad(n_near), pad(n_late)
-    rows_near, rows_late = n_near * tok_rows, n_late * tok_rows
-    gather = lambda fars: [own[f] for f in fars] + [sib[f] for f in fars]
+    rows_near, rows_late = (sum(span[1] for _, span in rows) for rows in (near_rows, late_rows))
+    cap_near, cap_late = pad(rows_near // tok_rows), pad(rows_late // tok_rows)
     hid_near, picked, spread_near, gain_near = run_kernel(
-        functools.partial(early_kernel, n_near, top, cap_near),
-        (key, *gather(near), hot),
+        functools.partial(early_kernel, [span for _, span in near_rows], top, cap_near),
+        (key, *[a for a, _ in near_rows], hot),
         [
             ((rows_near, hot_units), bf16),
             ((cap_near, width), bf16),
@@ -384,8 +392,8 @@
         4 * rows_near * width,
     )
     back_late, hid_late, packed_near, packed_late, spread_late, gain_late = run_kernel(
-        functools.partial(late_kernel, n_late, top, cap_late),
-        (key, *gather(late), picked, gate_up, down, hot),
+        functools.partial(late_kernel, [span for _, span in late_rows], top, cap_late),
+        (key, *[a for a, _ in late_rows], picked, gate_up, down, hot),
         [
             ((rows_late // 2, width), bf16),
             ((rows_late, hot_units), bf16),
@@ -403,49 +411,31 @@
         4 * rows_late * width,
     )
 
-    def results(fars, pool, sides, after=()):
-        hid, packed, spread, gain = sides
-        first, size = pool.index(fars[0]) * tok_rows, len(fars) * tok_rows
-        shift = len(pool) * tok_rows
-        outs = [((size, width), f32)]
-        if pool is near:
-            outs = [((size, width), bf16)] + outs
+    def results(size, both, hid, packed, spread, gain):
+        outs = [((size, width), bf16)] if both else []
         return run_kernel(
-            functools.partial(
-                result_kernel,
-                (first, size),
-                (first + shift, size) if pool is near else None,
-                len(after),
-            ),
-            (hid, packed, spread, gain, hot, *after),
-            outs,
+            functools.partial(result_kernel, (0, size), (size, size) if both else None, 0),
+            (hid, packed, spread, gain, hot),
+            outs + [((size, width), f32)],
             [],
             4 * size * width * (hot_units + packed.shape[0]),
             8 * size * width,
         )
 
-    total = {}
-
-    def add_up(fars, mine, other):
-        for index, far in enumerate(fars):
-            at = slice(index * tok_rows, (index + 1) * tok_rows)
-            total[far] = mine[at] + other[at].astype(f32)
-
     low = lambda a: a.astype(bf16)
-    sides = (hid_near, packed_near, spread_near, gain_near)
     from_late = swap(back_late)
-    (own_late,) = results(late, late, (hid_late, packed_late, spread_late, gain_late))
-    add_up(late, own_late, from_late)
-    first, ahead, behind = tie(low(total[4]), low(total[-3]), low(total[3]))
-    back, mine = results(near, near, sides, (first,))
-    first, ahead, behind = move(first, -2), move(ahead, 1), move(behind, -1)
-    add_up(near, mine, swap(back))
-    total[2] = total[2] + first.astype(f32)
-    for far in (2, 1):
-        ahead, behind = tie(ahead, behind)
-        ahead, behind = tie(low(total[-far] + ahead.astype(f32)), low(total[far] + behind.astype(f32)))
-        ahead, behind = move(ahead, 1), move(behind, -1)
-    return low(total[0] + ahead.astype(f32) + behind.astype(f32))
+    (mine_late,) = results(rows_late // 2, False, hid_late, packed_late, spread_late, gain_late)
+    back, mine = results(rows_near // 2, True, hid_near, packed_near, spread_near, gain_near)
+    from_late, mine = tie(from_late, mine)
+    late = mine_late + from_late.astype(f32)
+    fourth, third = tie(low(late[:tok_rows]), low(late[tok_rows:]))
+    fourth, third = move(fourth, -2).astype(f32), move(third, -1).astype(f32)
+    near = mine + swap(back).astype(f32)
+    part = lambda index: near[index * tok_rows : (index + 1) * tok_rows]
+    far = tie(low(part(0) + third[:tok_rows] + fourth), low(part(1) + third[tok_rows:]))
+    close = move(low(near[2 * tok_rows : 4 * tok_rows]), -1)
+    parts = (close[:tok_rows], swap(close[tok_rows:]), move(far[0], -2), cross(far[1], -2))
+    return low(sum((a.astype(f32) for a in parts), part(4)))
 
 
 def body(tokens, expert_ids, *rest):

time: 56.2 us -> 51.1 us (0.909)
  the two profiles are of different devices: /device:TPU:0 before, /device:TPU:9 now
where the time goes in v4:
time: 51.1 us; the launch traced here: 51 us
  starting transfers between devices  25.5 us (50%)
  waiting for transfers between devices  13 us (25%)
  Pallas kernels  11.2 us (22%)
  other arithmetic  1.1 us (2%)
    ppermute x8, starting transfers between devices, dense_body(): move = lambda a, by: lax.ppermute(a, axes, hop(by, 0))  12.1 us
    ppermute x10, starting transfers between devices, dense_body(): swap = lambda a: lax.ppermute(a, axes, swap_pairs)  10.6 us
    ppermute x8, waiting for transfers between devices, dense_body(): move = lambda a, by: lax.ppermute(a, axes, hop(by, 0))  6.66 us
    pallas_call x4, Pallas kernels, run_kernel(): pl.pallas_call(kernel, out_shape=[pltpu.VMEM(shape, dtype) for shape, dty...  5.63 us
    ppermute x1, waiting for transfers between devices, dense_body(): cross = lambda a, by: lax.ppermute(a, axes, hop(by, 1))  5.27 us
    pallas_call x1, Pallas kernels, load_weights(): pl.pallas_call(functools.partial(load_kernel, n), out_shape=[pltpu.VMEM(w...  4.48 us
    ppermute x1, starting transfers between devices, dense_body(): cross = lambda a, by: lax.ppermute(a, axes, hop(by, 1))  2.76 us
    pallas_call x1, Pallas kernels, make_message(): pl.pallas_call(message_kernel, out_shape=[pltpu.VMEM((2 * rows, width + L...  1.11 us
  transfers between devices with their start and end apart: 19, of which 8 were waited for; matrix products, arithmetic and copies ran while one was open for 1% of the time, Pallas kernels for 14%

profile of v4, /device:TPU:9, one launch (start us, length us, event | category | flops | bytes accessed | tf_op | source)
XLA Modules:
  0.0 51.0 jit_solution(15391601295990375131)
XLA Ops:
  0.0 0.7 %collective-permute-start = (bf16[32,2048]{1,0:T(8,128)(2,1)}, bf16[32,2048]{1,0:T(8,128)(2,1)S(1)}, u32[]{:S(2)}, u32[]{:S(2)}) collective-permute-start(bf16[32,2048]{1,0:T(8,128)(2,1)} %refs_0_.2), channel_id=1, source_target_pairs={{0,4},{4,0},{1,5},{5,1},{2,6},{6,2},{3,7},{7,3},{11,15},{15,11},{1... | collective-permute-start | bytes 393224 | tf_op jit(solution)/shard_map/ppermute | solution.py:358
  0.7 0.5 collective-permute-start.2
  1.2 0.9 %collective-permute-done.1 = s32[32,8]{0,1:T(8,128)S(1)} collective-permute-done((s32[32,8]{0,1:T(8,128)}, s32[32,8]{0,1:T(8,128)S(1)}, u32[]{:S(2)}, u32[]{:S(2)}) %collective-permute-start.1) | collective-permute-done | bytes 1056 | tf_op jit(solution)/shard_map/ppermute | solution.py:358
  2.1 0.2 collective-permute-done.2
  2.2 1.1 %shard_map.82 = (bf16[64,2176]{1,0:T(8,128)(2,1)S(1)}, f32[8,128]{1,0:T(8,128)S(1)}) custom-call(s32[4]{0:T(128)} %hot_list_ref.1, s32[16]{0:T(128)} %slot_ref.1, bf16[32,2048]{1,0:T(8,128)(2,1)} %refs_0_.2, s32[8,32]{1,0:T(8,128)} %bitcast.8, f32[8,32]{1,0:T(8,128)} %bitcast.9, bf16[32,2048]{1,0:T(8,128)(2,1)S(1)} %collective-permute-done.refs_3_, ...), custom_call_target="tpu_custom_call" | custom-call | tf_op jit(solution)/shard_map/pallas_call | solution.py:315
  3.3 1.1 %collective-permute-start.3 = (bf16[64,2176]{1,0:T(8,128)(2,1)S(1)}, bf16[64,2176]{1,0:T(8,128)(2,1)S(1)}, u32[]{:S(2)}, u32[]{:S(2)}) collective-permute-start(bf16[64,2176]{1,0:T(8,128)(2,1)S(1)} %get-tuple-element.37.refs_3_.refs_2_.refs_5_), channel_id=1, source_target_pairs={{0,2},{4,13},{1,3},{5,12},{2,11},{6,4},{3,10},{7,5},{11,9},{15,6},... | collective-permute-start | bytes 835592 | tf_op jit(solution)/shard_map/ppermute | solution.py:356
  4.4 4.5 %shard_map.83 = (bf16[1,2048,1536]{2,1,0:T(8,128)(2,1)S(1)}, bf16[1,768,2048]{2,1,0:T(8,128)(2,1)S(1)}, bf16[1,3,192,2048]{3,2,1,0:T(8,128)(2,1)S(1)}) custom-call(bf16[1,2048,1536]{2,1,0:T(8,128)(2,1)} %refs_0_.3, bf16[1,768,2048]{2,1,0:T(8,128)(2,1)} %refs_1_.1, bf16[1,3,192,2048]{3,2,1,0:T(8,128)(2,1)} %bitcast.7, ...), custom_call_target="tpu_custom_call" | custom-call | bytes 11796480 | tf_op jit(solution)/shard_map/pallas_call | solution.py:298
  8.9 1.3 %collective-permute-start.8 = (bf16[64,2176]{1,0:T(8,128)(2,1)S(1)}, bf16[64,2176]{1,0:T(8,128)(2,1)S(1)}, u32[]{:S(2)}, u32[]{:S(2)}) collective-permute-start(bf16[64,2176]{1,0:T(8,128)(2,1)S(1)} %get-tuple-element.37.refs_3_.refs_2_.refs_5_), channel_id=1, source_target_pairs={{0,1},{4,12},{1,2},{5,4},{2,3},{6,5},{3,11},{7,6},{11,10},{15,7},{... | collective-permute-start | bytes 835592 | tf_op jit(solution)/shard_map/ppermute | solution.py:356
  10.3 0.8 %collective-permute-done.3.refs_0_ = bf16[64,2176]{1,0:T(8,128)(2,1)S(1)} collective-permute-done((bf16[64,2176]{1,0:T(8,128)(2,1)S(1)}, bf16[64,2176]{1,0:T(8,128)(2,1)S(1)}, u32[]{:S(2)}, u32[]{:S(2)}) %collective-permute-start.3) | collective-permute-done | bytes 278560 | tf_op jit(solution)/shard_map/ppermute | solution.py:356
  11.1 1.9 %collective-permute-start.5 = (bf16[64,2176]{1,0:T(8,128)(2,1)S(1)}, bf16[64,2176]{1,0:T(8,128)(2,1)S(1)}, u32[]{:S(2)}, u32[]{:S(2)}) collective-permute-start(bf16[64,2176]{1,0:T(8,128)(2,1)S(1)} %collective-permute-done.3.refs_0_), channel_id=1, source_target_pairs={{0,1},{4,12},{1,2},{5,4},{2,3},{6,5},{3,11},{7,6},{11,10},{15,7},{... | collective-permute-start | bytes 835592 | tf_op jit(solution)/shard_map/ppermute | solution.py:356
  13.0 1.9 %collective-permute-start.9 = (bf16[64,2176]{1,0:T(8,128)(2,1)S(1)}, bf16[64,2176]{1,0:T(8,128)(2,1)S(1)}, u32[]{:S(2)}, u32[]{:S(2)}) collective-permute-start(bf16[64,2176]{1,0:T(8,128)(2,1)S(1)} %collective-permute-done.3.refs_0_), channel_id=1, source_target_pairs={{0,4},{4,0},{1,5},{5,1},{2,6},{6,2},{3,7},{7,3},{11,15},{15,11},{1... | collective-permute-start | bytes 835592 | tf_op jit(solution)/shard_map/ppermute | solution.py:358
  14.9 2.5 %collective-permute-start.10 = (bf16[64,2176]{1,0:T(8,128)(2,1)S(1)}, bf16[64,2176]{1,0:T(8,128)(2,1)S(1)}, u32[]{:S(2)}, u32[]{:S(2)}) collective-permute-start(bf16[64,2176]{1,0:T(8,128)(2,1)S(1)} %collective-permute-done.8.refs_1_), channel_id=1, source_target_pairs={{0,4},{4,0},{1,5},{5,1},{2,6},{6,2},{3,7},{7,3},{11,15},{15,11},{1... | collective-permute-start | bytes 835592 | tf_op jit(solution)/shard_map/ppermute | solution.py:358
  17.5 0.3 collective-permute-done.5.refs_1_
  17.8 2.7 %collective-permute-start.7 = (bf16[64,2176]{1,0:T(8,128)(2,1)S(1)}, bf16[64,2176]{1,0:T(8,128)(2,1)S(1)}, u32[]{:S(2)}, u32[]{:S(2)}) collective-permute-start(bf16[64,2176]{1,0:T(8,128)(2,1)S(1)} %collective-permute-done.5.refs_1_), channel_id=1, source_target_pairs={{0,4},{4,0},{1,5},{5,1},{2,6},{6,2},{3,7},{7,3},{11,15},{15,11},{1... | collective-permute-start | bytes 835592 | tf_op jit(solution)/shard_map/ppermute | solution.py:358
  20.5 2.9 %collective-permute-done.4.refs_0_ = bf16[32,2176]{1,0:T(8,128)(2,1)S(1)} collective-permute-done((bf16[32,2176]{1,0:T(8,128)(2,1)S(1)}, bf16[32,2176]{1,0:T(8,128)(2,1)S(1)}, u32[]{:S(2)}, u32[]{:S(2)}) %collective-permute-start.4) | collective-permute-done | bytes 139296 | tf_op jit(solution)/shard_map/ppermute | solution.py:356
  23.4 0.4 collective-permute-start.6
  23.8 1.3 %shard_map.84 = (bf16[320,192]{1,0:T(8,128)(2,1)S(1)}, bf16[112,2048]{1,0:T(8,128)(2,1)S(1)}, bf16[320,128]{1,0:T(8,128)(2,1)S(1)}, f32[320,128]{1,0:T(8,128)S(1)}) custom-call(f32[8,128]{1,0:T(8,128)S(1)} %get-tuple-element.32.key_ref, bf16[64,2176]{1,0:T(8,128)(2,1)S(1)} %collective-permute-done.3.refs_0_, ...), custom_call_target="tpu_custom_call" | custom-call | flops 650117120 | bytes 2621440 | tf_op jit(solution)/shard_map/pallas_call | solution.py:284
  25.1 3.1 %shard_map.85 = (bf16[96,2048]{1,0:T(8,128)(2,1)S(1)}, bf16[192,192]{1,0:T(8,128)(2,1)S(1)}, bf16[112,2048]{1,0:T(8,128)(2,1)S(1)}, bf16[80,2048]{1,0:T(8,128)(2...) custom-call(f32[8,128]{1,0:T(8,128)S(1)} %get-tuple-element.32.key_ref, ...), custom_call_target="tpu_custom_call" | custom-call | flops 1811939328 | bytes 1572864 | tf_op jit(solution)/shard_map/pallas_call | solution.py:284
  28.3 0.1 collective-permute-start.11
  28.4 0.9 %shard_map.86 = (bf16[160,2048]{1,0:T(8,128)(2,1)S(1)}, f32[160,2048]{1,0:T(8,128)S(1)}) custom-call(bf16[320,192]{1,0:T(8,128)(2,1)S(1)} %get-tuple-element.43.hid_ref, bf16[112,2048]{1,0:T(8,128)(2,1)S(1)} %get-tuple-element.44.packed_ref, bf16[320,128]{1,0:T(8,128)(2,1)S(1)} %get-tuple-element.45.spread_ref, f32[320,128]{1,0:T(8,128)S(1)} %get-tuple-element.46.gain_ref, ...), custom_call_target="tpu_custom_call" | custom-call | flops 398458880 | bytes 2621440 | tf_op jit(solution)/shard_map/pallas_call | solution.py:284
  29.3 0.5 collective-permute-start.12
  29.8 0.4 shard_map.87
  30.3 0.9 %collective-permute-start.15 = (bf16[64,2048]{1,0:T(8,128)(2,1)S(1)}, bf16[64,2048]{1,0:T(8,128)(2,1)S(1)}, u32[]{:S(2)}, u32[]{:S(2)}) collective-permute-start(bf16[64,2048]{1,0:T(8,128)(2,1)S(1)} %slice.53), channel_id=1, source_target_pairs={{0,8},{4,5},{1,0},{5,6},{2,1},{6,7},{3,2},{7,15},{11,3},{15,14},{1... | collective-permute-start | bytes 786440 | tf_op jit(solution)/shard_map/ppermute | solution.py:356
  31.3 2.3 %collective-permute-start.16 = (bf16[32,2048]{1,0:T(8,128)(2,1)S(1)}, bf16[32,2048]{1,0:T(8,128)(2,1)S(1)}, u32[]{:S(2)}, u32[]{:S(2)}) collective-permute-start(bf16[32,2048]{1,0:T(8,128)(2,1)S(1)} %slice.52), channel_id=1, source_target_pairs={{0,9},{4,6},{1,8},{5,7},{2,0},{6,15},{3,1},{7,14},{11,2},{15,13},{... | collective-permute-start | bytes 393224 | tf_op jit(solution)/shard_map/ppermute | solution.py:356
  33.5 2.5 %collective-permute-done.15 = bf16[64,2048]{1,0:T(8,128)(2,1)S(1)} collective-permute-done((bf16[64,2048]{1,0:T(8,128)(2,1)S(1)}, bf16[64,2048]{1,0:T(8,128)(2,1)S(1)}, u32[]{:S(2)}, u32[]{:S(2)}) %collective-permute-start.15) | collective-permute-done | bytes 262176 | tf_op jit(solution)/shard_map/ppermute | solution.py:356
  36.1 0.2 convert_add_fusion
  36.3 2.5 %collective-permute-start.13 = (bf16[64,2048]{1,0:T(8,128)(2,1)S(1)}, bf16[64,2048]{1,0:T(8,128)(2,1)S(1)}, u32[]{:S(2)}, u32[]{:S(2)}) collective-permute-start(bf16[64,2048]{1,0:T(8,128)(2,1)S(1)} %slice.78), channel_id=1, source_target_pairs={{0,8},{4,5},{1,0},{5,6},{2,1},{6,7},{3,2},{7,15},{11,3},{15,14},{1... | collective-permute-start | bytes 786440 | tf_op jit(solution)/shard_map/ppermute | solution.py:356
  38.9 2.0 %collective-permute-start.17 = (bf16[32,2048]{1,0:T(8,128)(2,1)S(1)}, bf16[32,2048]{1,0:T(8,128)(2,1)S(1)}, u32[]{:S(2)}, u32[]{:S(2)}) collective-permute-start(bf16[32,2048]{1,0:T(8,128)(2,1)S(1)} %get-tuple-element.57), channel_id=1, source_target_pairs={{0,9},{4,6},{1,8},{5,7},{2,0},{6,15},{3,1},{7,14},{11,2},{15,13},{... | collective-permute-start | bytes 393224 | tf_op jit(solution)/shard_map/ppermute | solution.py:356
  40.9 2.8 %collective-permute-start.18 = (bf16[32,2048]{1,0:T(8,128)(2,1)S(1)}, bf16[32,2048]{1,0:T(8,128)(2,1)S(1)}, u32[]{:S(2)}, u32[]{:S(2)}) collective-permute-start(bf16[32,2048]{1,0:T(8,128)(2,1)S(1)} %get-tuple-element.58), channel_id=1, source_target_pairs={{0,13},{4,2},{1,12},{5,3},{2,4},{6,11},{3,5},{7,10},{11,6},{15,9},... | collective-permute-start | bytes 393224 | tf_op jit(solution)/shard_map/ppermute | solution.py:357
  43.6 1.2 %collective-permute-start.14 = (bf16[32,2048]{1,0:T(8,128)(2,1)S(1)}, bf16[32,2048]{1,0:T(8,128)(2,1)S(1)}, u32[]{:S(2)}, u32[]{:S(2)}) collective-permute-start(bf16[32,2048]{1,0:T(8,128)(2,1)S(1)} %slice.50), channel_id=1, source_target_pairs={{0,4},{4,0},{1,5},{5,1},{2,6},{6,2},{3,7},{7,3},{11,15},{15,11},{1... | collective-permute-start | bytes 393224 | tf_op jit(solution)/shard_map/ppermute | solution.py:358
  45.0 5.3 %collective-permute-done.18 = bf16[32,2048]{1,0:T(8,128)(2,1)S(1)} collective-permute-done((bf16[32,2048]{1,0:T(8,128)(2,1)S(1)}, bf16[32,2048]{1,0:T(8,128)(2,1)S(1)}, u32[]{:S(2)}, u32[]{:S(2)}) %collective-permute-start.18) | collective-permute-done | bytes 131104 | tf_op jit(solution)/shard_map/ppermute | solution.py:357
  50.2 0.7 %fusion.6 = bf16[32,2048]{1,0:T(8,128)(2,1)} fusion(f32[160,2048]{1,0:T(8,128)S(1)} %convert_add_fusion, bf16[32,2048]{1,0:T(8,128)(2,1)S(1)} %collective-permute-done.18, bf16[32,2048]{1,0:T(8,128)(2,1)S(1)} %collective-permute-done.17, bf16[32,2048]{1,0:T(8,128)(2,1)S(1)} %collective-permute-done.14, bf16[64,2048]{1,0:T(8,128)(2,1)S(1)} %collective-permute-done.13), kind=kLoop, calls=%fused_computation.12 | loop fusion | flops 589824 | bytes 917504 | tf_op jit(solution)/shard_map/convert_element_type | solution.py:425
  (22 shorter events, 0.5 us)
Async XLA Ops:
  0.0 2.2 %collective-permute-start = (bf16[32,2048]{1,0:T(8,128)(2,1)}, bf16[32,2048]{1,0:T(8,128)(2,1)S(1)}, u32[]{:S(2)}, u32[]{:S(2)}) collective-permute-start(bf16[32,2048]{1,0:T(8,128)(2,1)} %refs_0_.2), channel_id=1, source_target_pairs={{0,4},{4,0},{1,5},{5,1},{2,6},{6,2},{3,7},{7,3},{11,15},{15,11},{1... | collective-permute-start | bytes 393224 | tf_op jit(solution)/shard_map/ppermute | solution.py:358
  0.7 1.4 %collective-permute-start.1 = (s32[32,8]{0,1:T(8,128)}, s32[32,8]{0,1:T(8,128)S(1)}, u32[]{:S(2)}, u32[]{:S(2)}) collective-permute-start(s32[32,8]{0,1:T(8,128)} %param.9), channel_id=1, source_target_pairs={{0,4},{4,0},{1,5},{5,1},{2,6},{6,2},{3,7},{7,3},{11,15},{15,11},{1... | collective-permute-start | bytes 3080 | tf_op jit(solution)/shard_map/ppermute | solution.py:358
  0.7 1.5 %collective-permute-start.2 = (f32[32,8]{0,1:T(8,128)}, f32[32,8]{0,1:T(8,128)S(1)}, u32[]{:S(2)}, u32[]{:S(2)}) collective-permute-start(f32[32,8]{0,1:T(8,128)} %param.10), channel_id=1, source_target_pairs={{0,4},{4,0},{1,5},{5,1},{2,6},{6,2},{3,7},{7,3},{11,15},{15,11},{1... | collective-permute-start | bytes 3080 | tf_op jit(solution)/shard_map/ppermute | solution.py:358
  3.3 7.8 %collective-permute-start.3 = (bf16[64,2176]{1,0:T(8,128)(2,1)S(1)}, bf16[64,2176]{1,0:T(8,128)(2,1)S(1)}, u32[]{:S(2)}, u32[]{:S(2)}) collective-permute-start(bf16[64,2176]{1,0:T(8,128)(2,1)S(1)} %get-tuple-element.37.refs_3_.refs_2_.refs_5_), channel_id=1, source_target_pairs={{0,2},{4,13},{1,3},{5,12},{2,11},{6,4},{3,10},{7,5},{11,9},{15,6},... | collective-permute-start | bytes 835592 | tf_op jit(solution)/shard_map/ppermute | solution.py:356
  8.9 6.0 %collective-permute-start.8 = (bf16[64,2176]{1,0:T(8,128)(2,1)S(1)}, bf16[64,2176]{1,0:T(8,128)(2,1)S(1)}, u32[]{:S(2)}, u32[]{:S(2)}) collective-permute-start(bf16[64,2176]{1,0:T(8,128)(2,1)S(1)} %get-tuple-element.37.refs_3_.refs_2_.refs_5_), channel_id=1, source_target_pairs={{0,1},{4,12},{1,2},{5,4},{2,3},{6,5},{3,11},{7,6},{11,10},{15,7},{... | collective-permute-start | bytes 835592 | tf_op jit(solution)/shard_map/ppermute | solution.py:356
  11.1 6.7 %collective-permute-start.5 = (bf16[64,2176]{1,0:T(8,128)(2,1)S(1)}, bf16[64,2176]{1,0:T(8,128)(2,1)S(1)}, u32[]{:S(2)}, u32[]{:S(2)}) collective-permute-start(bf16[64,2176]{1,0:T(8,128)(2,1)S(1)} %collective-permute-done.3.refs_0_), channel_id=1, source_target_pairs={{0,1},{4,12},{1,2},{5,4},{2,3},{6,5},{3,11},{7,6},{11,10},{15,7},{... | collective-permute-start | bytes 835592 | tf_op jit(solution)/shard_map/ppermute | solution.py:356
  13.0 10.8 %collective-permute-start.9 = (bf16[64,2176]{1,0:T(8,128)(2,1)S(1)}, bf16[64,2176]{1,0:T(8,128)(2,1)S(1)}, u32[]{:S(2)}, u32[]{:S(2)}) collective-permute-start(bf16[64,2176]{1,0:T(8,128)(2,1)S(1)} %collective-permute-done.3.refs_0_), channel_id=1, source_target_pairs={{0,4},{4,0},{1,5},{5,1},{2,6},{6,2},{3,7},{7,3},{11,15},{15,11},{1... | collective-permute-start | bytes 835592 | tf_op jit(solution)/shard_map/ppermute | solution.py:358
  14.9 8.9 %collective-permute-start.10 = (bf16[64,2176]{1,0:T(8,128)(2,1)S(1)}, bf16[64,2176]{1,0:T(8,128)(2,1)S(1)}, u32[]{:S(2)}, u32[]{:S(2)}) collective-permute-start(bf16[64,2176]{1,0:T(8,128)(2,1)S(1)} %collective-permute-done.8.refs_1_), channel_id=1, source_target_pairs={{0,4},{4,0},{1,5},{5,1},{2,6},{6,2},{3,7},{7,3},{11,15},{15,11},{1... | collective-permute-start | bytes 835592 | tf_op jit(solution)/shard_map/ppermute | solution.py:358
  17.4 6.0 %collective-permute-start.4 = (bf16[32,2176]{1,0:T(8,128)(2,1)S(1)}, bf16[32,2176]{1,0:T(8,128)(2,1)S(1)}, u32[]{:S(2)}, u32[]{:S(2)}) collective-permute-start(bf16[32,2176]{1,0:T(8,128)(2,1)S(1)} %slice.36), channel_id=1, source_target_pairs={{0,2},{4,13},{1,3},{5,12},{2,11},{6,4},{3,10},{7,5},{11,9},{15,6},... | collective-permute-start | bytes 417800 | tf_op jit(solution)/shard_map/ppermute | solution.py:356
  17.8 7.3 %collective-permute-start.7 = (bf16[64,2176]{1,0:T(8,128)(2,1)S(1)}, bf16[64,2176]{1,0:T(8,128)(2,1)S(1)}, u32[]{:S(2)}, u32[]{:S(2)}) collective-permute-start(bf16[64,2176]{1,0:T(8,128)(2,1)S(1)} %collective-permute-done.5.refs_1_), channel_id=1, source_target_pairs={{0,4},{4,0},{1,5},{5,1},{2,6},{6,2},{3,7},{7,3},{11,15},{15,11},{1... | collective-permute-start | bytes 835592 | tf_op jit(solution)/shard_map/ppermute | solution.py:358
  23.4 1.7 %collective-permute-start.6 = (bf16[32,2176]{1,0:T(8,128)(2,1)S(1)}, bf16[32,2176]{1,0:T(8,128)(2,1)S(1)}, u32[]{:S(2)}, u32[]{:S(2)}) collective-permute-start(bf16[32,2176]{1,0:T(8,128)(2,1)S(1)} %collective-permute-done.4.refs_0_), channel_id=1, source_target_pairs={{0,4},{4,0},{1,5},{5,1},{2,6},{6,2},{3,7},{7,3},{11,15},{15,11},{1... | collective-permute-start | bytes 417800 | tf_op jit(solution)/shard_map/ppermute | solution.py:358
  28.3 1.9 %collective-permute-start.11 = (bf16[96,2048]{1,0:T(8,128)(2,1)S(1)}, bf16[96,2048]{1,0:T(8,128)(2,1)S(1)}, u32[]{:S(2)}, u32[]{:S(2)}) collective-permute-start(bf16[96,2048]{1,0:T(8,128)(2,1)S(1)} %get-tuple-element.42), channel_id=1, source_target_pairs={{0,4},{4,0},{1,5},{5,1},{2,6},{6,2},{3,7},{7,3},{11,15},{15,11},{1... | collective-permute-start | bytes 1179656 | tf_op jit(solution)/shard_map/ppermute | solution.py:358
  29.3 6.8 %collective-permute-start.12 = (bf16[160,2048]{1,0:T(8,128)(2,1)S(1)}, bf16[160,2048]{1,0:T(8,128)(2,1)S(1)}, u32[]{:S(2)}, u32[]{:S(2)}) collective-permute-start(bf16[160,2048]{1,0:T(8,128)(2,1)S(1)} %get-tuple-element.49), channel_id=1, source_target_pairs={{0,4},{4,0},{1,5},{5,1},{2,6},{6,2},{3,7},{7,3},{11,15},{15,11},{1... | collective-permute-start | bytes 1966088 | tf_op jit(solution)/shard_map/ppermute | solution.py:358
  30.3 5.8 %collective-permute-start.15 = (bf16[64,2048]{1,0:T(8,128)(2,1)S(1)}, bf16[64,2048]{1,0:T(8,128)(2,1)S(1)}, u32[]{:S(2)}, u32[]{:S(2)}) collective-permute-start(bf16[64,2048]{1,0:T(8,128)(2,1)S(1)} %slice.53), channel_id=1, source_target_pairs={{0,8},{4,5},{1,0},{5,6},{2,1},{6,7},{3,2},{7,15},{11,3},{15,14},{1... | collective-permute-start | bytes 786440 | tf_op jit(solution)/shard_map/ppermute | solution.py:356
  31.3 7.5 %collective-permute-start.16 = (bf16[32,2048]{1,0:T(8,128)(2,1)S(1)}, bf16[32,2048]{1,0:T(8,128)(2,1)S(1)}, u32[]{:S(2)}, u32[]{:S(2)}) collective-permute-start(bf16[32,2048]{1,0:T(8,128)(2,1)S(1)} %slice.52), channel_id=1, source_target_pairs={{0,9},{4,6},{1,8},{5,7},{2,0},{6,15},{3,1},{7,14},{11,2},{15,13},{... | collective-permute-start | bytes 393224 | tf_op jit(solution)/shard_map/ppermute | solution.py:356
  36.3 7.3 %collective-permute-start.13 = (bf16[64,2048]{1,0:T(8,128)(2,1)S(1)}, bf16[64,2048]{1,0:T(8,128)(2,1)S(1)}, u32[]{:S(2)}, u32[]{:S(2)}) collective-permute-start(bf16[64,2048]{1,0:T(8,128)(2,1)S(1)} %slice.78), channel_id=1, source_target_pairs={{0,8},{4,5},{1,0},{5,6},{2,1},{6,7},{3,2},{7,15},{11,3},{15,14},{1... | collective-permute-start | bytes 786440 | tf_op jit(solution)/shard_map/ppermute | solution.py:356
  38.9 6.1 %collective-permute-start.17 = (bf16[32,2048]{1,0:T(8,128)(2,1)S(1)}, bf16[32,2048]{1,0:T(8,128)(2,1)S(1)}, u32[]{:S(2)}, u32[]{:S(2)}) collective-permute-start(bf16[32,2048]{1,0:T(8,128)(2,1)S(1)} %get-tuple-element.57), channel_id=1, source_target_pairs={{0,9},{4,6},{1,8},{5,7},{2,0},{6,15},{3,1},{7,14},{11,2},{15,13},{... | collective-permute-start | bytes 393224 | tf_op jit(solution)/shard_map/ppermute | solution.py:356
  40.9 9.4 %collective-permute-start.18 = (bf16[32,2048]{1,0:T(8,128)(2,1)S(1)}, bf16[32,2048]{1,0:T(8,128)(2,1)S(1)}, u32[]{:S(2)}, u32[]{:S(2)}) collective-permute-start(bf16[32,2048]{1,0:T(8,128)(2,1)S(1)} %get-tuple-element.58), channel_id=1, source_target_pairs={{0,13},{4,2},{1,12},{5,3},{2,4},{6,11},{3,5},{7,10},{11,6},{15,9},... | collective-permute-start | bytes 393224 | tf_op jit(solution)/shard_map/ppermute | solution.py:357
  43.6 6.6 %collective-permute-start.14 = (bf16[32,2048]{1,0:T(8,128)(2,1)S(1)}, bf16[32,2048]{1,0:T(8,128)(2,1)S(1)}, u32[]{:S(2)}, u32[]{:S(2)}) collective-permute-start(bf16[32,2048]{1,0:T(8,128)(2,1)S(1)} %slice.50), channel_id=1, source_target_pairs={{0,4},{4,0},{1,5},{5,1},{2,6},{6,2},{3,7},{7,3},{11,15},{15,11},{1... | collective-permute-start | bytes 393224 | tf_op jit(solution)/shard_map/ppermute | solution.py:358

commit v5 on v4

--- a/solution.py
+++ b/solution.py
@@ -119,25 +119,21 @@
     return (gate / (1.0 + jnp.exp(-gate)) * up).astype(jnp.bfloat16)
 
 
-def message_kernel(hot_list_ref, slot_ref, *refs):
-    out_ref, key_ref = refs[-2:]
+def message_kernel(hot_list_ref, slot_ref, tok_ref, ids_ref, gain_ref, out_ref, key_ref):
+    width = tok_ref.shape[1]
+    out_ref[:, :width] = tok_ref[...]
     bf16, f32 = jnp.bfloat16, jnp.float32
-    for half in range(2):
-        tok_ref, ids_ref, gain_ref = refs[3 * half : 3 * half + 3]
-        height, width = tok_ref.shape
-        at = slice(half * height, (half + 1) * height)
-        out_ref[at, :width] = tok_ref[...]
-        gains = gain_ref[...]
-        terms = [ids_ref[...].astype(f32)]
-        for _ in range(3):
-            term = gains.astype(bf16).astype(f32)
-            terms.append(term)
-            gains = gains - term
-        stacked = jnp.concatenate(terms, axis=0).astype(bf16)
-        shape = (stacked.shape[0], LANES)
-        row, lane = (lax.broadcasted_iota(jnp.int32, shape, axis) for axis in (0, 1))
-        place = jnp.where(row == lane, 1.0, 0.0).astype(bf16)
-        out_ref[at, width:] = mm(stacked, place, TN).astype(bf16)
+    gains = gain_ref[...]
+    terms = [ids_ref[...].astype(f32)]
+    for _ in range(3):
+        term = gains.astype(bf16).astype(f32)
+        terms.append(term)
+        gains = gains - term
+    stacked = jnp.concatenate(terms, axis=0).astype(bf16)
+    shape = (stacked.shape[0], LANES)
+    row, lane = (lax.broadcasted_iota(jnp.int32, shape, axis) for axis in (0, 1))
+    place = jnp.where(row == lane, 1.0, 0.0).astype(bf16)
+    out_ref[:, width:] = mm(stacked, place, TN).astype(bf16)
     along = lax.axis_index("dp")
     me = lax.axis_index("ep") * lax.axis_size("dp") + along
     my_cold, my_hot = jnp.int32(0), jnp.int32(0)
@@ -149,6 +145,12 @@
         my_hot = jnp.where(along == place, hot_list_ref[place], my_hot)
     row = lax.broadcasted_iota(jnp.int32, key_ref.shape, 0)
     key_ref[...] = jnp.where(row == 0, my_cold, my_hot).astype(f32)
+
+
+def join_kernel(mine_ref, other_ref, out_ref):
+    height = mine_ref.shape[0]
+    out_ref[:height, :] = mine_ref[...]
+    out_ref[height:, :] = other_ref[...]
 
 
 def load_kernel(n, *refs):
@@ -230,52 +232,72 @@
     pick_ref[...] = mm(spread[:, :cap], x, TN).astype(jnp.bfloat16)
 
 
-def late_kernel(spans, top, cap, key_ref, *refs):
+def cold_expert(cold, gate_up_ref, down_ref, h_ref, packed_refs):
+    units, width = down_ref.shape[1:]
+    for start in range(0, units, STEP):
+        gate = mm(cold, gate_up_ref[0, :, start : start + STEP])
+        up = mm(cold, gate_up_ref[0, :, units + start : units + start + STEP])
+        h_ref[:, start : start + STEP] = swish(gate, up)
+    cold_hidden = h_ref[...]
+    for start in range(0, width, STEP):
+        at = slice(start, start + STEP)
+        packed, end = mm(cold_hidden, down_ref[0, :, at]).astype(jnp.bfloat16), 0
+        for packed_ref in packed_refs:
+            packed_ref[:, at] = packed[end : end + packed_ref.shape[0]]
+            end += packed_ref.shape[0]
+
+
+def first_kernel(spans, top, cap, key_ref, *refs):
     n = len(spans)
-    (early_ref, gate_up_ref, down_ref, hot_ref), rest = refs[n : n + 4], refs[n + 4 :]
-    sib_ref, hid_ref, near_ref, far_ref, spread_ref, gain_ref, x_ref, c_ref, h_ref = rest
+    (gate_up_ref, down_ref, hot_ref), rest = refs[n : n + 3], refs[n + 3 :]
+    hid_ref, packed_ref, spread_ref, gain_ref, x_ref, h_ref = rest
+    meta = load_rows(refs[:n], spans, x_ref)
+    cold_gain, hot_gain, spread = routing(key_ref, meta, top, spread_ref.shape[1])
+    spread_ref[...] = spread
+    keep_gains(cold_gain, hot_gain, gain_ref)
+    x = x_ref[...]
+    hid_ref[...] = swish(mm(x, hot_ref[0, 0], NT), mm(x, hot_ref[0, 1], NT))
+    cold = mm(spread[:, :cap], x, TN).astype(jnp.bfloat16)
+    cold_expert(cold, gate_up_ref, down_ref, h_ref, (packed_ref,))
+
+
+def late_kernel(spans, top, cap, skip, key_ref, *refs):
+    n = len(spans)
+    (pick_ref, gate_up_ref, down_ref, hot_ref), rest = refs[n : n + 4], refs[n + 4 :]
+    sib_ref, hid_ref, *packed_refs = rest[:4]
+    spread_ref, gain_ref, x_ref, c_ref, h_ref = rest[4:]
     width = x_ref.shape[1]
-    units = down_ref.shape[1]
     meta = load_rows(refs[:n], spans, x_ref)
     cold_gain, hot_gain, spread = routing(key_ref, meta, top, spread_ref.shape[1])
     spread_ref[...] = spread
     keep_gains(cold_gain, hot_gain, gain_ref)
     spread = spread[:, :cap]
     x = x_ref[...]
-    n_early = early_ref.shape[0]
-    c_ref[:n_early, :] = early_ref[...]
-    c_ref[n_early:, :] = mm(spread, x, TN).astype(jnp.bfloat16)
-    cold = c_ref[...]
-    for start in range(0, units, STEP):
-        gate = mm(cold, gate_up_ref[0, :, start : start + STEP])
-        up = mm(cold, gate_up_ref[0, :, units + start : units + start + STEP])
-        h_ref[:, start : start + STEP] = swish(gate, up)
+    n_picked = pick_ref.shape[0]
+    c_ref[:n_picked, :] = pick_ref[...]
+    c_ref[n_picked:, :] = mm(spread, x, TN).astype(jnp.bfloat16)
+    cold_expert(c_ref[...], gate_up_ref, down_ref, h_ref, packed_refs)
     hidden = swish(mm(x, hot_ref[0, 0], NT), mm(x, hot_ref[0, 1], NT))
     hid_ref[...] = hidden
-    half = hidden.shape[0] // 2
-    cold_hidden = h_ref[...]
-    for start in range(0, width, STEP):
-        at = slice(start, start + STEP)
-        packed = mm(cold_hidden, down_ref[0, :, at]).astype(jnp.bfloat16)
-        near_ref[:, at] = packed[:n_early]
-        far_ref[:, at] = packed[n_early:]
-    weigh(hidden[half:], far_ref, spread[half:], hot_ref, cold_gain[half:], hot_gain[half:], sib_ref)
-
-
-def result_kernel(own_rows, sib_rows, after, hid_ref, packed_ref, spread_ref, gain_ref, hot_ref, *refs):
-    outs = refs[after:]
-    cap = packed_ref.shape[0]
-    spans = ([sib_rows] if sib_rows else []) + [own_rows]
-    for (first, size), out_ref in zip(spans, outs):
+    weigh(
+        hidden[skip:], packed_refs[1], spread[skip:], hot_ref, cold_gain[skip:], hot_gain[skip:], sib_ref
+    )
+
+
+def result_kernel(n_groups, jobs, hot_ref, *refs):
+    outs = refs[4 * n_groups :]
+    for group, first, size, out, place in jobs:
+        hid_ref, packed_ref, spread_ref, gain_ref = refs[4 * group : 4 * group + 4]
         at = slice(first, first + size)
         weigh(
             hid_ref[at, :],
             packed_ref,
-            spread_ref[at, :cap],
+            spread_ref[at, : packed_ref.shape[0]],
             hot_ref,
             gain_ref[at, 0:1],
             gain_ref[at, 1:2],
-            out_ref,
+            outs[out],
+            place,
         )
 
 
@@ -308,20 +330,20 @@
     )(*[hbm(w) for w in weights], after)
 
 
-def make_message(hot_list, slot_of, *sides):
-    rows, width = sides[0].shape
+def make_message(hot_list, slot_of, tokens, ids, gains):
+    rows, width = tokens.shape
     vmem, smem = pl.BlockSpec(memory_space=pltpu.VMEM), pl.BlockSpec(memory_space=pltpu.SMEM)
     hbm = lambda a: pltpu.with_memory_space_constraint(a, pltpu.HBM)
     return pl.pallas_call(
         message_kernel,
         out_shape=[
-            pltpu.VMEM((2 * rows, width + LANES), sides[0].dtype),
+            pltpu.VMEM((rows, width + LANES), tokens.dtype),
             pltpu.VMEM((8, LANES), jnp.float32),
         ],
-        in_specs=[smem] * 2 + [vmem] * 6,
+        in_specs=[smem] * 2 + [vmem] * 3,
         out_specs=[vmem] * 2,
         compiler_params=pltpu.CompilerParams(vmem_limit_bytes=2**21),
-    )(hbm(hot_list), hbm(slot_of), *[hbm(a) for a in sides[:3]], *[pin(a) for a in sides[3:]])
+    )(*[hbm(a) for a in (hot_list, slot_of, tokens, ids, gains)])
 
 
 def ring_perms(n_dp):
@@ -358,10 +380,10 @@
     swap = lambda a: lax.ppermute(a, axes, swap_pairs)
     tie = lambda *arrays: lax.optimization_barrier(arrays)
 
-    given = (tokens, expert_ids, route_w)
-    sides = [a for side in (given, [swap(a) for a in given]) for a in side]
-    sides = [a.T if index % 3 else a for index, a in enumerate(sides)]
-    message, key = make_message(hot_list, slot_of, *sides)
+    mine, key = make_message(hot_list, slot_of, tokens, expert_ids.T, route_w.T)
+    (message,) = run_kernel(
+        join_kernel, (mine, swap(mine)), [((2 * tok_rows, mine.shape[1]), bf16)], [], 0, 4 * mine.size, 2
+    )
     weights = (cold_gate_up, cold_down, jnp.swapaxes(hot_weights, 2, 3))
     gate_up, down, hot = load_weights(weights, message)
 
@@ -371,71 +393,101 @@
     two, hot = tie(two, hot)
     four, three = move(two[:tok_rows], 2), move(two, 1)
 
+    sib_two = swap(two)
     whole, half, rest = (0, 2 * tok_rows), (0, tok_rows), (tok_rows, tok_rows)
-    near_rows = ((two, whole), (one, whole), (message, half), (swap(two), whole), (swap(one), whole), (message, rest))
-    late_rows = ((four, half), (three, whole), (swap(four), half), (swap(three), whole))
     pad = lambda n: -(-n * cold_cap // 16) * 16
     lanes = lambda cap: -(-cap // LANES) * LANES
-    rows_near, rows_late = (sum(span[1] for _, span in rows) for rows in (near_rows, late_rows))
-    cap_near, cap_late = pad(rows_near // tok_rows), pad(rows_late // tok_rows)
-    hid_near, picked, spread_near, gain_near = run_kernel(
-        functools.partial(early_kernel, [span for _, span in near_rows], top, cap_near),
-        (key, *[a for a, _ in near_rows], hot),
+
+    def facts(spans):
+        rows = sum(size for _, size in spans)
+        cap = pad(rows // tok_rows)
+        kept = [((rows, lanes(cap)), bf16), ((rows, LANES), f32)]
+        return rows, cap, kept
+
+    def early(blocks, spans):
+        rows, cap, kept = facts(spans)
+        return run_kernel(
+            functools.partial(early_kernel, spans, top, cap),
+            (key, *blocks, hot),
+            [((rows, hot_units), bf16), ((cap, width), bf16), *kept],
+            [((rows, width), bf16)],
+            2 * rows * width * (2 * hot_units + cap),
+            4 * rows * width,
+        )
+
+    spans = (whole, half, whole, rest, whole)
+    rows, cap_a, kept = facts(spans)
+    a_rows = run_kernel(
+        functools.partial(first_kernel, spans, top, cap_a),
+        (key, two, message, sib_two, message, one, gate_up, down, hot),
+        [((rows, hot_units), bf16), ((cap_a, width), bf16), *kept],
+        [((rows, width), bf16), ((cap_a, units), bf16)],
+        2 * cap_a * 3 * units * width,
+        4 * rows * width,
+    )
+    def results(groups, jobs, outs):
+        size = sum(job[2] for job in jobs)
+        return run_kernel(
+            functools.partial(result_kernel, len(groups), jobs),
+            (hot, *[a for group in groups for a in group]),
+            outs,
+            [],
+            2 * size * width * (hot_units + cap_a),
+            4 * size * width,
+        )
+
+    r = tok_rows
+    back_a, mine = results(
+        (a_rows,),
+        (
+            (0, 3 * r, 3 * r, 0, 0),
+            (0, 0, 2 * r, 1, 0),
+            (0, 6 * r, 2 * r, 1, 2 * r),
+            (0, 2 * r, r, 1, 4 * r),
+        ),
+        [((3 * r, width), bf16), ((5 * r, width), f32)],
+    )
+    four, three, one, mine = tie(four, three, one, mine)
+    sib_one, sib_four, sib_three = swap(one), swap(four), swap(three)
+    hid_b, pick_b, *kept_b = early((four, three), (half, whole))
+    spans = (whole, half, whole)
+    rows, cap, kept = facts(spans)
+    cap_b, skip = pick_b.shape[0], 2 * tok_rows
+    back_late, hid_c, packed_b, packed_c, *kept_c = run_kernel(
+        functools.partial(late_kernel, spans, top, cap, skip),
+        (key, sib_one, sib_four, sib_three, pick_b, gate_up, down, hot),
         [
-            ((rows_near, hot_units), bf16),
-            ((cap_near, width), bf16),
-            ((rows_near, lanes(cap_near)), bf16),
-            ((rows_near, LANES), f32),
+            ((rows - skip, width), bf16),
+            ((rows, hot_units), bf16),
+            ((cap_b, width), bf16),
+            ((cap, width), bf16),
+            *kept,
         ],
-        [((rows_near, width), bf16)],
-        2 * rows_near * width * (2 * hot_units + cap_near),
-        4 * rows_near * width,
-    )
-    back_late, hid_late, packed_near, packed_late, spread_late, gain_late = run_kernel(
-        functools.partial(late_kernel, [span for _, span in late_rows], top, cap_late),
-        (key, *[a for a, _ in late_rows], picked, gate_up, down, hot),
-        [
-            ((rows_late // 2, width), bf16),
-            ((rows_late, hot_units), bf16),
-            ((cap_near, width), bf16),
-            ((cap_late, width), bf16),
-            ((rows_late, lanes(cap_late)), bf16),
-            ((rows_late, LANES), f32),
-        ],
-        [
-            ((rows_late, width), bf16),
-            ((cap_near + cap_late, width), bf16),
-            ((cap_near + cap_late, units), bf16),
-        ],
-        2 * (cap_near + cap_late) * 3 * units * width,
-        4 * rows_late * width,
-    )
-
-    def results(size, both, hid, packed, spread, gain):
-        outs = [((size, width), bf16)] if both else []
-        return run_kernel(
-            functools.partial(result_kernel, (0, size), (size, size) if both else None, 0),
-            (hid, packed, spread, gain, hot),
-            outs + [((size, width), f32)],
-            [],
-            4 * size * width * (hot_units + packed.shape[0]),
-            8 * size * width,
-        )
-
+        [((rows, width), bf16), ((cap_b + cap, width), bf16), ((cap_b + cap, units), bf16)],
+        2 * (cap_b + cap) * 3 * units * width,
+        4 * rows * width,
+    )
+    b_rows = (hid_b, packed_b, *kept_b)
+    c_rows = (hid_c, packed_c, *kept_c)
     low = lambda a: a.astype(bf16)
     from_late = swap(back_late)
-    (mine_late,) = results(rows_late // 2, False, hid_late, packed_late, spread_late, gain_late)
-    back, mine = results(rows_near // 2, True, hid_near, packed_near, spread_near, gain_near)
-    from_late, mine = tie(from_late, mine)
+    back_one, mine_late = results(
+        (b_rows, c_rows),
+        ((1, 0, 2 * r, 0, 0), (0, 0, 3 * r, 1, 0)),
+        [((2 * r, width), bf16), ((3 * r, width), f32)],
+    )
+    from_a, from_one = swap(back_a).astype(f32), swap(back_one).astype(f32)
     late = mine_late + from_late.astype(f32)
     fourth, third = tie(low(late[:tok_rows]), low(late[tok_rows:]))
     fourth, third = move(fourth, -2).astype(f32), move(third, -1).astype(f32)
-    near = mine + swap(back).astype(f32)
-    part = lambda index: near[index * tok_rows : (index + 1) * tok_rows]
-    far = tie(low(part(0) + third[:tok_rows] + fourth), low(part(1) + third[tok_rows:]))
-    close = move(low(near[2 * tok_rows : 4 * tok_rows]), -1)
+    far_sum = mine[: 2 * r] + from_a[: 2 * r]
+    one_sum = mine[2 * r : 4 * r] + from_one
+    own_sum = mine[4 * r :] + from_a[2 * r :]
+    fourth, nearest = tie(fourth, low(one_sum))
+    close = move(nearest, -1)
+    far = tie(low(far_sum[:r] + third[:r] + fourth), low(far_sum[r:] + third[r:]))
     parts = (close[:tok_rows], swap(close[tok_rows:]), move(far[0], -2), cross(far[1], -2))
-    return low(sum((a.astype(f32) for a in parts), part(4)))
+    return low(sum((a.astype(f32) for a in parts), own_sum))
 
 
 def body(tokens, expert_ids, *rest):

time: 51.1 us -> 50.4 us (0.986)
  the two profiles are of different devices: /device:TPU:9 before, /device:TPU:0 now
where the time goes in v5:
time: 50.4 us; the launch traced here: 50 us
  starting transfers between devices  18.3 us (36%)
  waiting for transfers between devices  17.4 us (35%)
  Pallas kernels  13.1 us (26%)
  other arithmetic  1.13 us (2%)
    ppermute x8, starting transfers between devices, dense_body(): move = lambda a, by: lax.ppermute(a, axes, hop(by, 0))  16 us
    ppermute x8, waiting for transfers between devices, dense_body(): move = lambda a, by: lax.ppermute(a, axes, hop(by, 0))  12.7 us
    pallas_call x6, Pallas kernels, run_kernel(): pl.pallas_call(kernel, out_shape=[pltpu.VMEM(shape, dtype) for shape, dty...  7.48 us
    pallas_call x1, Pallas kernels, load_weights(): pl.pallas_call(functools.partial(load_kernel, n), out_shape=[pltpu.VMEM(w...  4.48 us
    ppermute x1, waiting for transfers between devices, dense_body(): cross = lambda a, by: lax.ppermute(a, axes, hop(by, 1))  2.72 us
    ppermute x9, starting transfers between devices, dense_body(): swap = lambda a: lax.ppermute(a, axes, swap_pairs)  2.3 us
    ppermute x9, waiting for transfers between devices, dense_body(): swap = lambda a: lax.ppermute(a, axes, swap_pairs)  1.92 us
    pallas_call x1, Pallas kernels, make_message(): pl.pallas_call(message_kernel, out_shape=[pltpu.VMEM((rows, width + LANES...  1.11 us
  transfers between devices with their start and end apart: 18, of which 10 were waited for; matrix products, arithmetic and copies ran while one was open for 1% of the time, Pallas kernels for 24%

profile of v5, /device:TPU:0, one launch (start us, length us, event | category | flops | bytes accessed | tf_op | source)
XLA Modules:
  0.0 50.0 jit_solution(6904445605255380170)
XLA Ops:
  0.0 1.1 %shard_map.82 = (bf16[32,2176]{1,0:T(8,128)(2,1)S(1)}, f32[8,128]{1,0:T(8,128)S(1)}) custom-call(s32[4]{0:T(128)} %hot_list_ref.1, s32[16]{0:T(128)} %slot_ref.1, bf16[32,2048]{1,0:T(8,128)(2,1)} %tok_ref.1, s32[8,32]{1,0:T(8,128)} %bitcast.4, f32[8,32]{1,0:T(8,128)} %bitcast.5), custom_call_target="tpu_custom_call" | custom-call | tf_op jit(solution)/shard_map/pallas_call | solution.py:337
  1.1 0.5 collective-permute-start
  1.6 1.0 %collective-permute-done.other_ref = bf16[32,2176]{1,0:T(8,128)(2,1)S(1)} collective-permute-done((bf16[32,2176]{1,0:T(8,128)(2,1)S(1)}, bf16[32,2176]{1,0:T(8,128)(2,1)S(1)}, u32[]{:S(2)}, u32[]{:S(2)}) %collective-permute-start) | collective-permute-done | bytes 139296 | tf_op jit(solution)/shard_map/ppermute | solution.py:380
  2.6 4.0 %collective-permute-start.1 = (bf16[64,2176]{1,0:T(8,128)(2,1)S(1)}, bf16[64,2176]{1,0:T(8,128)(2,1)S(1)}, u32[]{:S(2)}, u32[]{:S(2)}) collective-permute-start(bf16[64,2176]{1,0:T(8,128)(2,1)S(1)} %shard_map.83.refs_3_.refs_1_), channel_id=1, source_target_pairs={{0,2},{4,13},{1,3},{5,12},{2,11},{6,4},{3,10},{7,5},{11,9},{15,6},... | collective-permute-start | bytes 835592 | tf_op jit(solution)/shard_map/ppermute | solution.py:378
  6.6 4.5 %shard_map.84 = (bf16[1,2048,1536]{2,1,0:T(8,128)(2,1)S(1)}, bf16[1,768,2048]{2,1,0:T(8,128)(2,1)S(1)}, bf16[1,3,192,2048]{3,2,1,0:T(8,128)(2,1)S(1)}) custom-call(bf16[1,2048,1536]{2,1,0:T(8,128)(2,1)} %refs_0_.1, bf16[1,768,2048]{2,1,0:T(8,128)(2,1)} %refs_1_.1, bf16[1,3,192,2048]{3,2,1,0:T(8,128)(2,1)} %bitcast.3, ...), custom_call_target="tpu_custom_call" | custom-call | bytes 11796480 | tf_op jit(solution)/shard_map/pallas_call | solution.py:320
  11.1 1.6 %collective-permute-start.4 = (bf16[64,2176]{1,0:T(8,128)(2,1)S(1)}, bf16[64,2176]{1,0:T(8,128)(2,1)S(1)}, u32[]{:S(2)}, u32[]{:S(2)}) collective-permute-start(bf16[64,2176]{1,0:T(8,128)(2,1)S(1)} %shard_map.83.refs_3_.refs_1_), channel_id=1, source_target_pairs={{0,1},{4,12},{1,2},{5,4},{2,3},{6,5},{3,11},{7,6},{11,10},{15,7},{... | collective-permute-start | bytes 835592 | tf_op jit(solution)/shard_map/ppermute | solution.py:378
  12.7 0.8 %collective-permute-done.1.refs_0_ = bf16[64,2176]{1,0:T(8,128)(2,1)S(1)} collective-permute-done((bf16[64,2176]{1,0:T(8,128)(2,1)S(1)}, bf16[64,2176]{1,0:T(8,128)(2,1)S(1)}, u32[]{:S(2)}, u32[]{:S(2)}) %collective-permute-start.1) | collective-permute-done | bytes 278560 | tf_op jit(solution)/shard_map/ppermute | solution.py:378
  13.6 0.1 collective-permute-start.5
  13.7 2.1 %collective-permute-start.3 = (bf16[64,2176]{1,0:T(8,128)(2,1)S(1)}, bf16[64,2176]{1,0:T(8,128)(2,1)S(1)}, u32[]{:S(2)}, u32[]{:S(2)}) collective-permute-start(bf16[64,2176]{1,0:T(8,128)(2,1)S(1)} %collective-permute-done.1.refs_0_), channel_id=1, source_target_pairs={{0,1},{4,12},{1,2},{5,4},{2,3},{6,5},{3,11},{7,6},{11,10},{15,7},{... | collective-permute-start | bytes 835592 | tf_op jit(solution)/shard_map/ppermute | solution.py:378
  15.8 2.9 %collective-permute-start.2 = (bf16[32,2176]{1,0:T(8,128)(2,1)S(1)}, bf16[32,2176]{1,0:T(8,128)(2,1)S(1)}, u32[]{:S(2)}, u32[]{:S(2)}) collective-permute-start(bf16[32,2176]{1,0:T(8,128)(2,1)S(1)} %slice.44), channel_id=1, source_target_pairs={{0,2},{4,13},{1,3},{5,12},{2,11},{6,4},{3,10},{7,5},{11,9},{15,6},... | collective-permute-start | bytes 417800 | tf_op jit(solution)/shard_map/ppermute | solution.py:378
  18.7 2.6 %shard_map.85 = (bf16[256,192]{1,0:T(8,128)(2,1)S(1)}, bf16[96,2048]{1,0:T(8,128)(2,1)S(1)}, bf16[256,128]{1,0:T(8,128)(2,1)S(1)}, f32[256,128]{1,0:T(8,128)S(1)}) custom-call(f32[8,128]{1,0:T(8,128)S(1)} %get-tuple-element.48.key_ref, bf16[64,2176]{1,0:T(8,128)(2,1)S(1)} %collective-permute-done.1.refs_0_, bf16[64,2176]{1,0:T(8,128)(2,1)S(1)} %shard_map.83.refs_3_.refs_1_, ...), custom_call_target="tpu_custom_call" | custom-call | flops 905969664 | bytes 2097152 | tf_op jit(solution)/shard_map/pallas_call | solution.py:306
  21.3 0.9 %shard_map.86 = (bf16[96,2048]{1,0:T(8,128)(2,1)S(1)}, f32[160,2048]{1,0:T(8,128)S(1)}) custom-call(bf16[1,3,192,2048]{3,2,1,0:T(8,128)(2,1)S(1)} %get-tuple-element.47.refs_7_.hot_ref.refs_2_.refs_6_, bf16[256,192]{1,0:T(8,128)(2,1)S(1)} %get-tuple-element.51.refs_0_, bf16[96,2048]{1,0:T(8,128)(2,1)S(1)} %get-tuple-element.52.refs_1_, ...), custom_call_target="tpu_custom_call" | custom-call | flops 301989888 | bytes 2097152 | tf_op jit(solution)/shard_map/pallas_call | solution.py:306
  22.1 1.9 %collective-permute-done.2.refs_0_ = bf16[32,2176]{1,0:T(8,128)(2,1)S(1)} collective-permute-done((bf16[32,2176]{1,0:T(8,128)(2,1)S(1)}, bf16[32,2176]{1,0:T(8,128)(2,1)S(1)}, u32[]{:S(2)}, u32[]{:S(2)}) %collective-permute-start.2) | collective-permute-done | bytes 139296 | tf_op jit(solution)/shard_map/ppermute | solution.py:378
  24.0 0.5 %collective-permute-start.9 = (bf16[64,2176]{1,0:T(8,128)(2,1)S(1)}, bf16[64,2176]{1,0:T(8,128)(2,1)S(1)}, u32[]{:S(2)}, u32[]{:S(2)}) collective-permute-start(bf16[64,2176]{1,0:T(8,128)(2,1)S(1)} %collective-permute-done.3.refs_1_), channel_id=1, source_target_pairs={{0,4},{4,0},{1,5},{5,1},{2,6},{6,2},{3,7},{7,3},{11,15},{15,11},{1... | collective-permute-start | bytes 835592 | tf_op jit(solution)/shard_map/ppermute | solution.py:380
  24.5 0.5 %collective-permute-start.6 = (bf16[96,2048]{1,0:T(8,128)(2,1)S(1)}, bf16[96,2048]{1,0:T(8,128)(2,1)S(1)}, u32[]{:S(2)}, u32[]{:S(2)}) collective-permute-start(bf16[96,2048]{1,0:T(8,128)(2,1)S(1)} %get-tuple-element.57), channel_id=1, source_target_pairs={{0,4},{4,0},{1,5},{5,1},{2,6},{6,2},{3,7},{7,3},{11,15},{15,11},{1... | collective-permute-start | bytes 1179656 | tf_op jit(solution)/shard_map/ppermute | solution.py:380
  25.0 0.8 %shard_map.87 = (bf16[96,192]{1,0:T(8,128)(2,1)S(1)}, bf16[48,2048]{1,0:T(8,128)(2,1)S(1)}, bf16[96,128]{1,0:T(8,128)(2,1)S(1)}, f32[96,128]{1,0:T(8,128)S(1)}) custom-call(f32[8,128]{1,0:T(8,128)S(1)} %get-tuple-element.48.key_ref, bf16[32,2176]{1,0:T(8,128)(2,1)S(1)} %collective-permute-done.2.refs_0_, ...), custom_call_target="tpu_custom_call" | custom-call | flops 169869312 | bytes 786432 | tf_op jit(solution)/shard_map/pallas_call | solution.py:306
  25.8 0.4 collective-permute-done.8.refs_1_
  26.2 2.7 %shard_map.88 = (bf16[96,2048]{1,0:T(8,128)(2,1)S(1)}, bf16[160,192]{1,0:T(8,128)(2,1)S(1)}, bf16[48,2048]{1,0:T(8,128)(2,1)S(1)}, bf16[64,2048]{1,0:T(8,128)(2,...) custom-call(f32[8,128]{1,0:T(8,128)S(1)} %get-tuple-element.48.key_ref, ...), custom_call_target="tpu_custom_call" | custom-call | flops 1056964608 | bytes 1310720 | tf_op jit(solution)/shard_map/pallas_call | solution.py:306
  28.9 0.2 collective-permute-start.10
  29.1 0.5 %shard_map.89 = (bf16[64,2048]{1,0:T(8,128)(2,1)S(1)}, f32[96,2048]{1,0:T(8,128)S(1)}) custom-call(bf16[1,3,192,2048]{3,2,1,0:T(8,128)(2,1)S(1)} %get-tuple-element.47.refs_7_.hot_ref.refs_2_.refs_6_, bf16[96,192]{1,0:T(8,128)(2,1)S(1)} %get-tuple-element.60.refs_0_, bf16[48,2048]{1,0:T(8,128)(2,1)S(1)} %get-tuple-element.63.refs_1_, ...), custom_call_target="tpu_custom_call" | custom-call | flops 188743680 | bytes 1310720 | tf_op jit(solution)/shard_map/pallas_call | solution.py:306
  29.7 0.4 collective-permute-start.12
  30.2 0.5 %collective-permute-done.10 = bf16[96,2048]{1,0:T(8,128)(2,1)S(1)} collective-permute-done((bf16[96,2048]{1,0:T(8,128)(2,1)S(1)}, bf16[96,2048]{1,0:T(8,128)(2,1)S(1)}, u32[]{:S(2)}, u32[]{:S(2)}) %collective-permute-start.10) | collective-permute-done | bytes 393248 | tf_op jit(solution)/shard_map/ppermute | solution.py:380
  30.9 3.0 %collective-permute-start.11 = (bf16[32,2048]{1,0:T(8,128)(2,1)S(1)}, bf16[32,2048]{1,0:T(8,128)(2,1)S(1)}, u32[]{:S(2)}, u32[]{:S(2)}) collective-permute-start(bf16[32,2048]{1,0:T(8,128)(2,1)S(1)} %slice.59), channel_id=1, source_target_pairs={{0,9},{4,6},{1,8},{5,7},{2,0},{6,15},{3,1},{7,14},{11,2},{15,13},{... | collective-permute-start | bytes 393224 | tf_op jit(solution)/shard_map/ppermute | solution.py:378
  33.9 0.1 slice_add_fusion
  34.0 4.3 %collective-permute-done.11 = bf16[32,2048]{1,0:T(8,128)(2,1)S(1)} collective-permute-done((bf16[32,2048]{1,0:T(8,128)(2,1)S(1)}, bf16[32,2048]{1,0:T(8,128)(2,1)S(1)}, u32[]{:S(2)}, u32[]{:S(2)}) %collective-permute-start.11) | collective-permute-done | bytes 131104 | tf_op jit(solution)/shard_map/ppermute | solution.py:378
  38.3 0.2 collective-permute-start.13
  38.6 1.8 %collective-permute-done.15 = bf16[64,2048]{1,0:T(8,128)(2,1)S(1)} collective-permute-done((bf16[64,2048]{1,0:T(8,128)(2,1)S(1)}, bf16[64,2048]{1,0:T(8,128)(2,1)S(1)}, u32[]{:S(2)}, u32[]{:S(2)}) %collective-permute-start.15) | collective-permute-done | bytes 262176 | tf_op jit(solution)/shard_map/ppermute | solution.py:378
  40.5 2.0 %collective-permute-start.16 = (bf16[32,2048]{1,0:T(8,128)(2,1)S(1)}, bf16[32,2048]{1,0:T(8,128)(2,1)S(1)}, u32[]{:S(2)}, u32[]{:S(2)}) collective-permute-start(bf16[32,2048]{1,0:T(8,128)(2,1)S(1)} %get-tuple-element.77), channel_id=1, source_target_pairs={{0,9},{4,6},{1,8},{5,7},{2,0},{6,15},{3,1},{7,14},{11,2},{15,13},{... | collective-permute-start | bytes 393224 | tf_op jit(solution)/shard_map/ppermute | solution.py:378
  42.6 2.2 %collective-permute-done.13 = bf16[64,2048]{1,0:T(8,128)(2,1)S(1)} collective-permute-done((bf16[64,2048]{1,0:T(8,128)(2,1)S(1)}, bf16[64,2048]{1,0:T(8,128)(2,1)S(1)}, u32[]{:S(2)}, u32[]{:S(2)}) %collective-permute-start.13) | collective-permute-done | bytes 262176 | tf_op jit(solution)/shard_map/ppermute | solution.py:378
  44.8 1.7 %collective-permute-done.16 = bf16[32,2048]{1,0:T(8,128)(2,1)S(1)} collective-permute-done((bf16[32,2048]{1,0:T(8,128)(2,1)S(1)}, bf16[32,2048]{1,0:T(8,128)(2,1)S(1)}, u32[]{:S(2)}, u32[]{:S(2)}) %collective-permute-start.16) | collective-permute-done | bytes 131104 | tf_op jit(solution)/shard_map/ppermute | solution.py:378
  46.5 2.7 %collective-permute-done.17 = bf16[32,2048]{1,0:T(8,128)(2,1)S(1)} collective-permute-done((bf16[32,2048]{1,0:T(8,128)(2,1)S(1)}, bf16[32,2048]{1,0:T(8,128)(2,1)S(1)}, u32[]{:S(2)}, u32[]{:S(2)}) %collective-permute-start.17) | collective-permute-done | bytes 131104 | tf_op jit(solution)/shard_map/ppermute | solution.py:379
  49.3 0.8 %fusion.7 = bf16[32,2048]{1,0:T(8,128)(2,1)} fusion(f32[96,2048]{1,0:T(8,128)S(1)} %convert_element_type.41, bf16[32,2048]{1,0:T(8,128)(2,1)S(1)} %collective-permute-done.17, bf16[32,2048]{1,0:T(8,128)(2,1)S(1)} %collective-permute-done.16, bf16[32,2048]{1,0:T(8,128)(2,1)S(1)} %collective-permute-done.14, f32[160,2048]{1,0:T(8,128)S(1)} %get-tuple-element.56, ...), kind=kLoop, calls=%fused_computation.13 | loop fusion | flops 655360 | bytes 1179648 | tf_op jit(solution)/shard_map/convert_element_type | solution.py:472
  (23 shorter events, 0.4 us)
Async XLA Ops:
  1.1 1.4 %collective-permute-start = (bf16[32,2176]{1,0:T(8,128)(2,1)S(1)}, bf16[32,2176]{1,0:T(8,128)(2,1)S(1)}, u32[]{:S(2)}, u32[]{:S(2)}) collective-permute-start(bf16[32,2176]{1,0:T(8,128)(2,1)S(1)} %get-tuple-element.42.mine_ref), channel_id=1, source_target_pairs={{0,4},{4,0},{1,5},{5,1},{2,6},{6,2},{3,7},{7,3},{11,15},{15,11},{1... | collective-permute-start | bytes 417800 | tf_op jit(solution)/shard_map/ppermute | solution.py:380
  2.6 11.0 %collective-permute-start.1 = (bf16[64,2176]{1,0:T(8,128)(2,1)S(1)}, bf16[64,2176]{1,0:T(8,128)(2,1)S(1)}, u32[]{:S(2)}, u32[]{:S(2)}) collective-permute-start(bf16[64,2176]{1,0:T(8,128)(2,1)S(1)} %shard_map.83.refs_3_.refs_1_), channel_id=1, source_target_pairs={{0,2},{4,13},{1,3},{5,12},{2,11},{6,4},{3,10},{7,5},{11,9},{15,6},... | collective-permute-start | bytes 835592 | tf_op jit(solution)/shard_map/ppermute | solution.py:378
  11.1 7.6 %collective-permute-start.4 = (bf16[64,2176]{1,0:T(8,128)(2,1)S(1)}, bf16[64,2176]{1,0:T(8,128)(2,1)S(1)}, u32[]{:S(2)}, u32[]{:S(2)}) collective-permute-start(bf16[64,2176]{1,0:T(8,128)(2,1)S(1)} %shard_map.83.refs_3_.refs_1_), channel_id=1, source_target_pairs={{0,1},{4,12},{1,2},{5,4},{2,3},{6,5},{3,11},{7,6},{11,10},{15,7},{... | collective-permute-start | bytes 835592 | tf_op jit(solution)/shard_map/ppermute | solution.py:378
  13.6 5.2 %collective-permute-start.5 = (bf16[64,2176]{1,0:T(8,128)(2,1)S(1)}, bf16[64,2176]{1,0:T(8,128)(2,1)S(1)}, u32[]{:S(2)}, u32[]{:S(2)}) collective-permute-start(bf16[64,2176]{1,0:T(8,128)(2,1)S(1)} %collective-permute-done.1.refs_0_), channel_id=1, source_target_pairs={{0,4},{4,0},{1,5},{5,1},{2,6},{6,2},{3,7},{7,3},{11,15},{15,11},{1... | collective-permute-start | bytes 835592 | tf_op jit(solution)/shard_map/ppermute | solution.py:380
  13.7 10.3 %collective-permute-start.3 = (bf16[64,2176]{1,0:T(8,128)(2,1)S(1)}, bf16[64,2176]{1,0:T(8,128)(2,1)S(1)}, u32[]{:S(2)}, u32[]{:S(2)}) collective-permute-start(bf16[64,2176]{1,0:T(8,128)(2,1)S(1)} %collective-permute-done.1.refs_0_), channel_id=1, source_target_pairs={{0,1},{4,12},{1,2},{5,4},{2,3},{6,5},{3,11},{7,6},{11,10},{15,7},{... | collective-permute-start | bytes 835592 | tf_op jit(solution)/shard_map/ppermute | solution.py:378
  15.8 8.2 %collective-permute-start.2 = (bf16[32,2176]{1,0:T(8,128)(2,1)S(1)}, bf16[32,2176]{1,0:T(8,128)(2,1)S(1)}, u32[]{:S(2)}, u32[]{:S(2)}) collective-permute-start(bf16[32,2176]{1,0:T(8,128)(2,1)S(1)} %slice.44), channel_id=1, source_target_pairs={{0,2},{4,13},{1,3},{5,12},{2,11},{6,4},{3,10},{7,5},{11,9},{15,6},... | collective-permute-start | bytes 417800 | tf_op jit(solution)/shard_map/ppermute | solution.py:378
  24.0 2.2 %collective-permute-start.7 = (bf16[64,2176]{1,0:T(8,128)(2,1)S(1)}, bf16[64,2176]{1,0:T(8,128)(2,1)S(1)}, u32[]{:S(2)}, u32[]{:S(2)}) collective-permute-start(bf16[64,2176]{1,0:T(8,128)(2,1)S(1)} %collective-permute-done.4.refs_4_), channel_id=1, source_target_pairs={{0,4},{4,0},{1,5},{5,1},{2,6},{6,2},{3,7},{7,3},{11,15},{15,11},{1... | collective-permute-start | bytes 835592 | tf_op jit(solution)/shard_map/ppermute | solution.py:380
  24.0 2.2 %collective-permute-start.9 = (bf16[64,2176]{1,0:T(8,128)(2,1)S(1)}, bf16[64,2176]{1,0:T(8,128)(2,1)S(1)}, u32[]{:S(2)}, u32[]{:S(2)}) collective-permute-start(bf16[64,2176]{1,0:T(8,128)(2,1)S(1)} %collective-permute-done.3.refs_1_), channel_id=1, source_target_pairs={{0,4},{4,0},{1,5},{5,1},{2,6},{6,2},{3,7},{7,3},{11,15},{15,11},{1... | collective-permute-start | bytes 835592 | tf_op jit(solution)/shard_map/ppermute | solution.py:380
  24.5 1.6 %collective-permute-start.8 = (bf16[32,2176]{1,0:T(8,128)(2,1)S(1)}, bf16[32,2176]{1,0:T(8,128)(2,1)S(1)}, u32[]{:S(2)}, u32[]{:S(2)}) collective-permute-start(bf16[32,2176]{1,0:T(8,128)(2,1)S(1)} %collective-permute-done.2.refs_0_), channel_id=1, source_target_pairs={{0,4},{4,0},{1,5},{5,1},{2,6},{6,2},{3,7},{7,3},{11,15},{15,11},{1... | collective-permute-start | bytes 417800 | tf_op jit(solution)/shard_map/ppermute | solution.py:380
  24.5 5.6 %collective-permute-start.6 = (bf16[96,2048]{1,0:T(8,128)(2,1)S(1)}, bf16[96,2048]{1,0:T(8,128)(2,1)S(1)}, u32[]{:S(2)}, u32[]{:S(2)}) collective-permute-start(bf16[96,2048]{1,0:T(8,128)(2,1)S(1)} %get-tuple-element.57), channel_id=1, source_target_pairs={{0,4},{4,0},{1,5},{5,1},{2,6},{6,2},{3,7},{7,3},{11,15},{15,11},{1... | collective-permute-start | bytes 1179656 | tf_op jit(solution)/shard_map/ppermute | solution.py:380
  28.9 1.8 %collective-permute-start.10 = (bf16[96,2048]{1,0:T(8,128)(2,1)S(1)}, bf16[96,2048]{1,0:T(8,128)(2,1)S(1)}, u32[]{:S(2)}, u32[]{:S(2)}) collective-permute-start(bf16[96,2048]{1,0:T(8,128)(2,1)S(1)} %get-tuple-element.71), channel_id=1, source_target_pairs={{0,4},{4,0},{1,5},{5,1},{2,6},{6,2},{3,7},{7,3},{11,15},{15,11},{1... | collective-permute-start | bytes 1179656 | tf_op jit(solution)/shard_map/ppermute | solution.py:380
  29.7 4.2 %collective-permute-start.12 = (bf16[64,2048]{1,0:T(8,128)(2,1)S(1)}, bf16[64,2048]{1,0:T(8,128)(2,1)S(1)}, u32[]{:S(2)}, u32[]{:S(2)}) collective-permute-start(bf16[64,2048]{1,0:T(8,128)(2,1)S(1)} %get-tuple-element.73), channel_id=1, source_target_pairs={{0,4},{4,0},{1,5},{5,1},{2,6},{6,2},{3,7},{7,3},{11,15},{15,11},{1... | collective-permute-start | bytes 786440 | tf_op jit(solution)/shard_map/ppermute | solution.py:380
  30.9 7.4 %collective-permute-start.11 = (bf16[32,2048]{1,0:T(8,128)(2,1)S(1)}, bf16[32,2048]{1,0:T(8,128)(2,1)S(1)}, u32[]{:S(2)}, u32[]{:S(2)}) collective-permute-start(bf16[32,2048]{1,0:T(8,128)(2,1)S(1)} %slice.59), channel_id=1, source_target_pairs={{0,9},{4,6},{1,8},{5,7},{2,0},{6,15},{3,1},{7,14},{11,2},{15,13},{... | collective-permute-start | bytes 393224 | tf_op jit(solution)/shard_map/ppermute | solution.py:378
  33.9 6.5 %collective-permute-start.15 = (bf16[64,2048]{1,0:T(8,128)(2,1)S(1)}, bf16[64,2048]{1,0:T(8,128)(2,1)S(1)}, u32[]{:S(2)}, u32[]{:S(2)}) collective-permute-start(bf16[64,2048]{1,0:T(8,128)(2,1)S(1)} %slice.60), channel_id=1, source_target_pairs={{0,8},{4,5},{1,0},{5,6},{2,1},{6,7},{3,2},{7,15},{11,3},{15,14},{1... | collective-permute-start | bytes 786440 | tf_op jit(solution)/shard_map/ppermute | solution.py:378
  38.3 6.4 %collective-permute-start.13 = (bf16[64,2048]{1,0:T(8,128)(2,1)S(1)}, bf16[64,2048]{1,0:T(8,128)(2,1)S(1)}, u32[]{:S(2)}, u32[]{:S(2)}) collective-permute-start(bf16[64,2048]{1,0:T(8,128)(2,1)S(1)} %get-tuple-element.74), channel_id=1, source_target_pairs={{0,8},{4,5},{1,0},{5,6},{2,1},{6,7},{3,2},{7,15},{11,3},{15,14},{1... | collective-permute-start | bytes 786440 | tf_op jit(solution)/shard_map/ppermute | solution.py:378
  40.5 6.0 %collective-permute-start.16 = (bf16[32,2048]{1,0:T(8,128)(2,1)S(1)}, bf16[32,2048]{1,0:T(8,128)(2,1)S(1)}, u32[]{:S(2)}, u32[]{:S(2)}) collective-permute-start(bf16[32,2048]{1,0:T(8,128)(2,1)S(1)} %get-tuple-element.77), channel_id=1, source_target_pairs={{0,9},{4,6},{1,8},{5,7},{2,0},{6,15},{3,1},{7,14},{11,2},{15,13},{... | collective-permute-start | bytes 393224 | tf_op jit(solution)/shard_map/ppermute | solution.py:378
  42.6 6.7 %collective-permute-start.17 = (bf16[32,2048]{1,0:T(8,128)(2,1)S(1)}, bf16[32,2048]{1,0:T(8,128)(2,1)S(1)}, u32[]{:S(2)}, u32[]{:S(2)}) collective-permute-start(bf16[32,2048]{1,0:T(8,128)(2,1)S(1)} %get-tuple-element.78), channel_id=1, source_target_pairs={{0,13},{4,2},{1,12},{5,3},{2,4},{6,11},{3,5},{7,10},{11,6},{15,9},... | collective-permute-start | bytes 393224 | tf_op jit(solution)/shard_map/ppermute | solution.py:379
  44.7 4.5 %collective-permute-start.14 = (bf16[32,2048]{1,0:T(8,128)(2,1)S(1)}, bf16[32,2048]{1,0:T(8,128)(2,1)S(1)}, u32[]{:S(2)}, u32[]{:S(2)}) collective-permute-start(bf16[32,2048]{1,0:T(8,128)(2,1)S(1)} %slice.62), channel_id=1, source_target_pairs={{0,4},{4,0},{1,5},{5,1},{2,6},{6,2},{3,7},{7,3},{11,15},{15,11},{1... | collective-permute-start | bytes 393224 | tf_op jit(solution)/shard_map/ppermute | solution.py:380

commit v6 on v5

--- a/solution.py
+++ b/solution.py
@@ -476,16 +476,16 @@
         ((1, 0, 2 * r, 0, 0), (0, 0, 3 * r, 1, 0)),
         [((2 * r, width), bf16), ((3 * r, width), f32)],
     )
-    from_a, from_one = swap(back_a).astype(f32), swap(back_one).astype(f32)
-    late = mine_late + from_late.astype(f32)
-    fourth, third = tie(low(late[:tok_rows]), low(late[tok_rows:]))
-    fourth, third = move(fourth, -2).astype(f32), move(third, -1).astype(f32)
-    far_sum = mine[: 2 * r] + from_a[: 2 * r]
-    one_sum = mine[2 * r : 4 * r] + from_one
-    own_sum = mine[4 * r :] + from_a[2 * r :]
+    from_a, from_one = swap(back_a), swap(back_one)
+    join = lambda a, b: low(a + b.astype(f32))
+    fourth, third = join(mine_late[:r], from_late[:r]), join(mine_late[r:], from_late[r:])
+    fourth, third = move(fourth, -2), move(third, -1)
+    far_sum = mine[: 2 * r] + from_a[: 2 * r].astype(f32)
+    one_sum = mine[2 * r : 4 * r] + from_one.astype(f32)
+    own_sum = mine[4 * r :] + from_a[2 * r :].astype(f32)
     fourth, nearest = tie(fourth, low(one_sum))
     close = move(nearest, -1)
-    far = tie(low(far_sum[:r] + third[:r] + fourth), low(far_sum[r:] + third[r:]))
+    far = tie(low(far_sum[:r] + third[:r].astype(f32) + fourth.astype(f32)), join(far_sum[r:], third[r:]))
     parts = (close[:tok_rows], swap(close[tok_rows:]), move(far[0], -2), cross(far[1], -2))
     return low(sum((a.astype(f32) for a in parts), own_sum))
 

time: 50.4 us -> 50.2 us (level)
    convert_element_type x2 -> x5, other arithmetic: 0.82 us -> 1.03 us  [dense_body(): low = lambda a: a.astype(bf16)]
  transfers between devices with their start and end apart: 18 -> 18, of which waited for: 10 -> 10; matrix products, arithmetic and copies ran while one was open for 1% -> 1% of each run, Pallas kernels for 24% -> 18%
where the time goes in v6:
time: 50.2 us; the launch traced here: 50 us
  starting transfers between devices  17.9 us (36%)
  waiting for transfers between devices  17.9 us (36%)
  Pallas kernels  13.1 us (26%)
  other arithmetic  1.03 us (2%)
    ppermute x8, starting transfers between devices, dense_body(): move = lambda a, by: lax.ppermute(a, axes, hop(by, 0))  16 us
    ppermute x8, waiting for transfers between devices, dense_body(): move = lambda a, by: lax.ppermute(a, axes, hop(by, 0))  12.8 us
    pallas_call x6, Pallas kernels, run_kernel(): pl.pallas_call(kernel, out_shape=[pltpu.VMEM(shape, dtype) for shape, dty...  7.48 us
    pallas_call x1, Pallas kernels, load_weights(): pl.pallas_call(functools.partial(load_kernel, n), out_shape=[pltpu.VMEM(w...  4.48 us
    ppermute x1, waiting for transfers between devices, dense_body(): cross = lambda a, by: lax.ppermute(a, axes, hop(by, 1))  2.72 us
    ppermute x9, waiting for transfers between devices, dense_body(): swap = lambda a: lax.ppermute(a, axes, swap_pairs)  2.37 us
    ppermute x9, starting transfers between devices, dense_body(): swap = lambda a: lax.ppermute(a, axes, swap_pairs)  1.93 us
    pallas_call x1, Pallas kernels, make_message(): pl.pallas_call(message_kernel, out_shape=[pltpu.VMEM((rows, width + LANES...  1.11 us
  transfers between devices with their start and end apart: 18, of which 10 were waited for; matrix products, arithmetic and copies ran while one was open for 1% of the time, Pallas kernels for 18%

profile of v6, /device:TPU:0, one launch (start us, length us, event | category | flops | bytes accessed | tf_op | source)
XLA Modules:
  0.0 50.0 jit_solution(4647573448138679261)
XLA Ops:
  0.0 1.1 %shard_map.82 = (bf16[32,2176]{1,0:T(8,128)(2,1)S(1)}, f32[8,128]{1,0:T(8,128)S(1)}) custom-call(s32[4]{0:T(128)} %hot_list_ref.1, s32[16]{0:T(128)} %slot_ref.1, bf16[32,2048]{1,0:T(8,128)(2,1)} %tok_ref.1, s32[8,32]{1,0:T(8,128)} %bitcast.4, f32[8,32]{1,0:T(8,128)} %bitcast.5), custom_call_target="tpu_custom_call" | custom-call | tf_op jit(solution)/shard_map/pallas_call | solution.py:337
  1.1 0.5 collective-permute-start
  1.6 1.0 %collective-permute-done.other_ref = bf16[32,2176]{1,0:T(8,128)(2,1)S(1)} collective-permute-done((bf16[32,2176]{1,0:T(8,128)(2,1)S(1)}, bf16[32,2176]{1,0:T(8,128)(2,1)S(1)}, u32[]{:S(2)}, u32[]{:S(2)}) %collective-permute-start) | collective-permute-done | bytes 139296 | tf_op jit(solution)/shard_map/ppermute | solution.py:380
  2.6 4.0 %collective-permute-start.1 = (bf16[64,2176]{1,0:T(8,128)(2,1)S(1)}, bf16[64,2176]{1,0:T(8,128)(2,1)S(1)}, u32[]{:S(2)}, u32[]{:S(2)}) collective-permute-start(bf16[64,2176]{1,0:T(8,128)(2,1)S(1)} %shard_map.83.refs_3_.refs_1_), channel_id=1, source_target_pairs={{0,2},{4,13},{1,3},{5,12},{2,11},{6,4},{3,10},{7,5},{11,9},{15,6},... | collective-permute-start | bytes 835592 | tf_op jit(solution)/shard_map/ppermute | solution.py:378
  6.6 4.5 %shard_map.84 = (bf16[1,2048,1536]{2,1,0:T(8,128)(2,1)S(1)}, bf16[1,768,2048]{2,1,0:T(8,128)(2,1)S(1)}, bf16[1,3,192,2048]{3,2,1,0:T(8,128)(2,1)S(1)}) custom-call(bf16[1,2048,1536]{2,1,0:T(8,128)(2,1)} %refs_0_.1, bf16[1,768,2048]{2,1,0:T(8,128)(2,1)} %refs_1_.1, bf16[1,3,192,2048]{3,2,1,0:T(8,128)(2,1)} %bitcast.3, ...), custom_call_target="tpu_custom_call" | custom-call | bytes 11796480 | tf_op jit(solution)/shard_map/pallas_call | solution.py:320
  11.1 1.6 %collective-permute-start.4 = (bf16[64,2176]{1,0:T(8,128)(2,1)S(1)}, bf16[64,2176]{1,0:T(8,128)(2,1)S(1)}, u32[]{:S(2)}, u32[]{:S(2)}) collective-permute-start(bf16[64,2176]{1,0:T(8,128)(2,1)S(1)} %shard_map.83.refs_3_.refs_1_), channel_id=1, source_target_pairs={{0,1},{4,12},{1,2},{5,4},{2,3},{6,5},{3,11},{7,6},{11,10},{15,7},{... | collective-permute-start | bytes 835592 | tf_op jit(solution)/shard_map/ppermute | solution.py:378
  12.7 0.8 %collective-permute-done.1.refs_0_ = bf16[64,2176]{1,0:T(8,128)(2,1)S(1)} collective-permute-done((bf16[64,2176]{1,0:T(8,128)(2,1)S(1)}, bf16[64,2176]{1,0:T(8,128)(2,1)S(1)}, u32[]{:S(2)}, u32[]{:S(2)}) %collective-permute-start.1) | collective-permute-done | bytes 278560 | tf_op jit(solution)/shard_map/ppermute | solution.py:378
  13.6 0.1 collective-permute-start.5
  13.7 2.1 %collective-permute-start.3 = (bf16[64,2176]{1,0:T(8,128)(2,1)S(1)}, bf16[64,2176]{1,0:T(8,128)(2,1)S(1)}, u32[]{:S(2)}, u32[]{:S(2)}) collective-permute-start(bf16[64,2176]{1,0:T(8,128)(2,1)S(1)} %collective-permute-done.1.refs_0_), channel_id=1, source_target_pairs={{0,1},{4,12},{1,2},{5,4},{2,3},{6,5},{3,11},{7,6},{11,10},{15,7},{... | collective-permute-start | bytes 835592 | tf_op jit(solution)/shard_map/ppermute | solution.py:378
  15.8 2.9 %collective-permute-start.2 = (bf16[32,2176]{1,0:T(8,128)(2,1)S(1)}, bf16[32,2176]{1,0:T(8,128)(2,1)S(1)}, u32[]{:S(2)}, u32[]{:S(2)}) collective-permute-start(bf16[32,2176]{1,0:T(8,128)(2,1)S(1)} %slice.48), channel_id=1, source_target_pairs={{0,2},{4,13},{1,3},{5,12},{2,11},{6,4},{3,10},{7,5},{11,9},{15,6},... | collective-permute-start | bytes 417800 | tf_op jit(solution)/shard_map/ppermute | solution.py:378
  18.7 2.6 %shard_map.85 = (bf16[256,192]{1,0:T(8,128)(2,1)S(1)}, bf16[96,2048]{1,0:T(8,128)(2,1)S(1)}, bf16[256,128]{1,0:T(8,128)(2,1)S(1)}, f32[256,128]{1,0:T(8,128)S(1)}) custom-call(f32[8,128]{1,0:T(8,128)S(1)} %get-tuple-element.46.key_ref, bf16[64,2176]{1,0:T(8,128)(2,1)S(1)} %collective-permute-done.1.refs_0_, bf16[64,2176]{1,0:T(8,128)(2,1)S(1)} %shard_map.83.refs_3_.refs_1_, ...), custom_call_target="tpu_custom_call" | custom-call | flops 905969664 | bytes 2097152 | tf_op jit(solution)/shard_map/pallas_call | solution.py:306
  21.3 0.9 %shard_map.86 = (bf16[96,2048]{1,0:T(8,128)(2,1)S(1)}, f32[160,2048]{1,0:T(8,128)S(1)}) custom-call(bf16[1,3,192,2048]{3,2,1,0:T(8,128)(2,1)S(1)} %get-tuple-element.45.refs_7_.hot_ref.refs_2_.refs_6_, bf16[256,192]{1,0:T(8,128)(2,1)S(1)} %get-tuple-element.49.refs_0_, bf16[96,2048]{1,0:T(8,128)(2,1)S(1)} %get-tuple-element.50.refs_1_, ...), custom_call_target="tpu_custom_call" | custom-call | flops 301989888 | bytes 2097152 | tf_op jit(solution)/shard_map/pallas_call | solution.py:306
  22.1 1.9 %collective-permute-done.2.refs_0_ = bf16[32,2176]{1,0:T(8,128)(2,1)S(1)} collective-permute-done((bf16[32,2176]{1,0:T(8,128)(2,1)S(1)}, bf16[32,2176]{1,0:T(8,128)(2,1)S(1)}, u32[]{:S(2)}, u32[]{:S(2)}) %collective-permute-start.2) | collective-permute-done | bytes 139296 | tf_op jit(solution)/shard_map/ppermute | solution.py:378
  24.0 0.5 %collective-permute-start.9 = (bf16[64,2176]{1,0:T(8,128)(2,1)S(1)}, bf16[64,2176]{1,0:T(8,128)(2,1)S(1)}, u32[]{:S(2)}, u32[]{:S(2)}) collective-permute-start(bf16[64,2176]{1,0:T(8,128)(2,1)S(1)} %collective-permute-done.3.refs_1_), channel_id=1, source_target_pairs={{0,4},{4,0},{1,5},{5,1},{2,6},{6,2},{3,7},{7,3},{11,15},{15,11},{1... | collective-permute-start | bytes 835592 | tf_op jit(solution)/shard_map/ppermute | solution.py:380
  24.5 0.8 %shard_map.87 = (bf16[96,192]{1,0:T(8,128)(2,1)S(1)}, bf16[48,2048]{1,0:T(8,128)(2,1)S(1)}, bf16[96,128]{1,0:T(8,128)(2,1)S(1)}, f32[96,128]{1,0:T(8,128)S(1)}) custom-call(f32[8,128]{1,0:T(8,128)S(1)} %get-tuple-element.46.key_ref, bf16[32,2176]{1,0:T(8,128)(2,1)S(1)} %collective-permute-done.2.refs_0_, ...), custom_call_target="tpu_custom_call" | custom-call | flops 169869312 | bytes 786432 | tf_op jit(solution)/shard_map/pallas_call | solution.py:306
  25.3 0.9 %collective-permute-done.8.refs_1_ = bf16[32,2176]{1,0:T(8,128)(2,1)S(1)} collective-permute-done((bf16[32,2176]{1,0:T(8,128)(2,1)S(1)}, bf16[32,2176]{1,0:T(8,128)(2,1)S(1)}, u32[]{:S(2)}, u32[]{:S(2)}) %collective-permute-start.8) | collective-permute-done | bytes 139296 | tf_op jit(solution)/shard_map/ppermute | solution.py:380
  26.2 2.7 %shard_map.88 = (bf16[96,2048]{1,0:T(8,128)(2,1)S(1)}, bf16[160,192]{1,0:T(8,128)(2,1)S(1)}, bf16[48,2048]{1,0:T(8,128)(2,1)S(1)}, bf16[64,2048]{1,0:T(8,128)(2,...) custom-call(f32[8,128]{1,0:T(8,128)S(1)} %get-tuple-element.46.key_ref, ...), custom_call_target="tpu_custom_call" | custom-call | flops 1056964608 | bytes 1310720 | tf_op jit(solution)/shard_map/pallas_call | solution.py:306
  28.9 0.2 collective-permute-start.10
  29.1 0.4 collective-permute-start.6
  29.5 0.5 %shard_map.89 = (bf16[64,2048]{1,0:T(8,128)(2,1)S(1)}, f32[96,2048]{1,0:T(8,128)S(1)}) custom-call(bf16[1,3,192,2048]{3,2,1,0:T(8,128)(2,1)S(1)} %get-tuple-element.45.refs_7_.hot_ref.refs_2_.refs_6_, bf16[96,192]{1,0:T(8,128)(2,1)S(1)} %get-tuple-element.58.refs_0_, bf16[48,2048]{1,0:T(8,128)(2,1)S(1)} %get-tuple-element.61.refs_1_, ...), custom_call_target="tpu_custom_call" | custom-call | flops 188743680 | bytes 1310720 | tf_op jit(solution)/shard_map/pallas_call | solution.py:306
  30.0 0.2 collective-permute-start.12
  30.2 0.5 collective-permute-done.10
  30.7 3.0 %collective-permute-start.11 = (bf16[32,2048]{1,0:T(8,128)(2,1)S(1)}, bf16[32,2048]{1,0:T(8,128)(2,1)S(1)}, u32[]{:S(2)}, u32[]{:S(2)}) collective-permute-start(bf16[32,2048]{1,0:T(8,128)(2,1)S(1)} %add_convert_fusion.3), channel_id=1, source_target_pairs={{0,9},{4,6},{1,8},{5,7},{2,0},{6,15},{3,1},{7,14},{11,2},{15,13},{... | collective-permute-start | bytes 393224 | tf_op jit(solution)/shard_map/ppermute | solution.py:378
  33.9 0.1 add_convert_fusion.1
  34.0 4.1 %collective-permute-done.11 = bf16[32,2048]{1,0:T(8,128)(2,1)S(1)} collective-permute-done((bf16[32,2048]{1,0:T(8,128)(2,1)S(1)}, bf16[32,2048]{1,0:T(8,128)(2,1)S(1)}, u32[]{:S(2)}, u32[]{:S(2)}) %collective-permute-start.11) | collective-permute-done | bytes 131104 | tf_op jit(solution)/shard_map/ppermute | solution.py:378
  38.2 0.2 collective-permute-start.13
  38.4 2.0 %collective-permute-done.15 = bf16[64,2048]{1,0:T(8,128)(2,1)S(1)} collective-permute-done((bf16[64,2048]{1,0:T(8,128)(2,1)S(1)}, bf16[64,2048]{1,0:T(8,128)(2,1)S(1)}, u32[]{:S(2)}, u32[]{:S(2)}) %collective-permute-start.15) | collective-permute-done | bytes 262176 | tf_op jit(solution)/shard_map/ppermute | solution.py:378
  40.5 2.0 %collective-permute-start.16 = (bf16[32,2048]{1,0:T(8,128)(2,1)S(1)}, bf16[32,2048]{1,0:T(8,128)(2,1)S(1)}, u32[]{:S(2)}, u32[]{:S(2)}) collective-permute-start(bf16[32,2048]{1,0:T(8,128)(2,1)S(1)} %get-tuple-element.73), channel_id=1, source_target_pairs={{0,9},{4,6},{1,8},{5,7},{2,0},{6,15},{3,1},{7,14},{11,2},{15,13},{... | collective-permute-start | bytes 393224 | tf_op jit(solution)/shard_map/ppermute | solution.py:378
  42.5 2.0 %collective-permute-done.13 = bf16[64,2048]{1,0:T(8,128)(2,1)S(1)} collective-permute-done((bf16[64,2048]{1,0:T(8,128)(2,1)S(1)}, bf16[64,2048]{1,0:T(8,128)(2,1)S(1)}, u32[]{:S(2)}, u32[]{:S(2)}) %collective-permute-start.13) | collective-permute-done | bytes 262176 | tf_op jit(solution)/shard_map/ppermute | solution.py:378
  44.6 1.8 %collective-permute-done.16 = bf16[32,2048]{1,0:T(8,128)(2,1)S(1)} collective-permute-done((bf16[32,2048]{1,0:T(8,128)(2,1)S(1)}, bf16[32,2048]{1,0:T(8,128)(2,1)S(1)}, u32[]{:S(2)}, u32[]{:S(2)}) %collective-permute-start.16) | collective-permute-done | bytes 131104 | tf_op jit(solution)/shard_map/ppermute | solution.py:378
  46.5 2.7 %collective-permute-done.17 = bf16[32,2048]{1,0:T(8,128)(2,1)S(1)} collective-permute-done((bf16[32,2048]{1,0:T(8,128)(2,1)S(1)}, bf16[32,2048]{1,0:T(8,128)(2,1)S(1)}, u32[]{:S(2)}, u32[]{:S(2)}) %collective-permute-start.17) | collective-permute-done | bytes 131104 | tf_op jit(solution)/shard_map/ppermute | solution.py:379
  49.2 0.8 %add_convert_fusion.2 = bf16[32,2048]{1,0:T(8,128)(2,1)} fusion(bf16[32,2048]{1,0:T(8,128)(2,1)S(1)} %collective-permute-done.17, bf16[32,2048]{1,0:T(8,128)(2,1)S(1)} %collective-permute-done.16, bf16[32,2048]{1,0:T(8,128)(2,1)S(1)} %collective-permute-done.14, f32[160,2048]{1,0:T(8,128)S(1)} %get-tuple-element.54, ...), kind=kLoop, calls=%fused_computation.8 | loop fusion | flops 720896 | bytes 1048576 | tf_op jit(solution)/shard_map/convert_element_type | solution.py:472
  (19 shorter events, 0.4 us)
Async XLA Ops:
  1.1 1.4 %collective-permute-start = (bf16[32,2176]{1,0:T(8,128)(2,1)S(1)}, bf16[32,2176]{1,0:T(8,128)(2,1)S(1)}, u32[]{:S(2)}, u32[]{:S(2)}) collective-permute-start(bf16[32,2176]{1,0:T(8,128)(2,1)S(1)} %get-tuple-element.40.mine_ref), channel_id=1, source_target_pairs={{0,4},{4,0},{1,5},{5,1},{2,6},{6,2},{3,7},{7,3},{11,15},{15,11},{1... | collective-permute-start | bytes 417800 | tf_op jit(solution)/shard_map/ppermute | solution.py:380
  2.6 11.0 %collective-permute-start.1 = (bf16[64,2176]{1,0:T(8,128)(2,1)S(1)}, bf16[64,2176]{1,0:T(8,128)(2,1)S(1)}, u32[]{:S(2)}, u32[]{:S(2)}) collective-permute-start(bf16[64,2176]{1,0:T(8,128)(2,1)S(1)} %shard_map.83.refs_3_.refs_1_), channel_id=1, source_target_pairs={{0,2},{4,13},{1,3},{5,12},{2,11},{6,4},{3,10},{7,5},{11,9},{15,6},... | collective-permute-start | bytes 835592 | tf_op jit(solution)/shard_map/ppermute | solution.py:378
  11.1 7.6 %collective-permute-start.4 = (bf16[64,2176]{1,0:T(8,128)(2,1)S(1)}, bf16[64,2176]{1,0:T(8,128)(2,1)S(1)}, u32[]{:S(2)}, u32[]{:S(2)}) collective-permute-start(bf16[64,2176]{1,0:T(8,128)(2,1)S(1)} %shard_map.83.refs_3_.refs_1_), channel_id=1, source_target_pairs={{0,1},{4,12},{1,2},{5,4},{2,3},{6,5},{3,11},{7,6},{11,10},{15,7},{... | collective-permute-start | bytes 835592 | tf_op jit(solution)/shard_map/ppermute | solution.py:378
  13.6 5.2 %collective-permute-start.5 = (bf16[64,2176]{1,0:T(8,128)(2,1)S(1)}, bf16[64,2176]{1,0:T(8,128)(2,1)S(1)}, u32[]{:S(2)}, u32[]{:S(2)}) collective-permute-start(bf16[64,2176]{1,0:T(8,128)(2,1)S(1)} %collective-permute-done.1.refs_0_), channel_id=1, source_target_pairs={{0,4},{4,0},{1,5},{5,1},{2,6},{6,2},{3,7},{7,3},{11,15},{15,11},{1... | collective-permute-start | bytes 835592 | tf_op jit(solution)/shard_map/ppermute | solution.py:380
  13.7 10.3 %collective-permute-start.3 = (bf16[64,2176]{1,0:T(8,128)(2,1)S(1)}, bf16[64,2176]{1,0:T(8,128)(2,1)S(1)}, u32[]{:S(2)}, u32[]{:S(2)}) collective-permute-start(bf16[64,2176]{1,0:T(8,128)(2,1)S(1)} %collective-permute-done.1.refs_0_), channel_id=1, source_target_pairs={{0,1},{4,12},{1,2},{5,4},{2,3},{6,5},{3,11},{7,6},{11,10},{15,7},{... | collective-permute-start | bytes 835592 | tf_op jit(solution)/shard_map/ppermute | solution.py:378
  15.8 8.2 %collective-permute-start.2 = (bf16[32,2176]{1,0:T(8,128)(2,1)S(1)}, bf16[32,2176]{1,0:T(8,128)(2,1)S(1)}, u32[]{:S(2)}, u32[]{:S(2)}) collective-permute-start(bf16[32,2176]{1,0:T(8,128)(2,1)S(1)} %slice.48), channel_id=1, source_target_pairs={{0,2},{4,13},{1,3},{5,12},{2,11},{6,4},{3,10},{7,5},{11,9},{15,6},... | collective-permute-start | bytes 417800 | tf_op jit(solution)/shard_map/ppermute | solution.py:378
  24.0 2.2 %collective-permute-start.7 = (bf16[64,2176]{1,0:T(8,128)(2,1)S(1)}, bf16[64,2176]{1,0:T(8,128)(2,1)S(1)}, u32[]{:S(2)}, u32[]{:S(2)}) collective-permute-start(bf16[64,2176]{1,0:T(8,128)(2,1)S(1)} %collective-permute-done.4.refs_4_), channel_id=1, source_target_pairs={{0,4},{4,0},{1,5},{5,1},{2,6},{6,2},{3,7},{7,3},{11,15},{15,11},{1... | collective-permute-start | bytes 835592 | tf_op jit(solution)/shard_map/ppermute | solution.py:380
  24.0 2.2 %collective-permute-start.9 = (bf16[64,2176]{1,0:T(8,128)(2,1)S(1)}, bf16[64,2176]{1,0:T(8,128)(2,1)S(1)}, u32[]{:S(2)}, u32[]{:S(2)}) collective-permute-start(bf16[64,2176]{1,0:T(8,128)(2,1)S(1)} %collective-permute-done.3.refs_1_), channel_id=1, source_target_pairs={{0,4},{4,0},{1,5},{5,1},{2,6},{6,2},{3,7},{7,3},{11,15},{15,11},{1... | collective-permute-start | bytes 835592 | tf_op jit(solution)/shard_map/ppermute | solution.py:380
  24.5 1.6 %collective-permute-start.8 = (bf16[32,2176]{1,0:T(8,128)(2,1)S(1)}, bf16[32,2176]{1,0:T(8,128)(2,1)S(1)}, u32[]{:S(2)}, u32[]{:S(2)}) collective-permute-start(bf16[32,2176]{1,0:T(8,128)(2,1)S(1)} %collective-permute-done.2.refs_0_), channel_id=1, source_target_pairs={{0,4},{4,0},{1,5},{5,1},{2,6},{6,2},{3,7},{7,3},{11,15},{15,11},{1... | collective-permute-start | bytes 417800 | tf_op jit(solution)/shard_map/ppermute | solution.py:380
  28.9 1.8 %collective-permute-start.10 = (bf16[96,2048]{1,0:T(8,128)(2,1)S(1)}, bf16[96,2048]{1,0:T(8,128)(2,1)S(1)}, u32[]{:S(2)}, u32[]{:S(2)}) collective-permute-start(bf16[96,2048]{1,0:T(8,128)(2,1)S(1)} %get-tuple-element.69), channel_id=1, source_target_pairs={{0,4},{4,0},{1,5},{5,1},{2,6},{6,2},{3,7},{7,3},{11,15},{15,11},{1... | collective-permute-start | bytes 1179656 | tf_op jit(solution)/shard_map/ppermute | solution.py:380
  29.1 4.8 %collective-permute-start.6 = (bf16[96,2048]{1,0:T(8,128)(2,1)S(1)}, bf16[96,2048]{1,0:T(8,128)(2,1)S(1)}, u32[]{:S(2)}, u32[]{:S(2)}) collective-permute-start(bf16[96,2048]{1,0:T(8,128)(2,1)S(1)} %get-tuple-element.55), channel_id=1, source_target_pairs={{0,4},{4,0},{1,5},{5,1},{2,6},{6,2},{3,7},{7,3},{11,15},{15,11},{1... | collective-permute-start | bytes 1179656 | tf_op jit(solution)/shard_map/ppermute | solution.py:380
  30.0 3.9 %collective-permute-start.12 = (bf16[64,2048]{1,0:T(8,128)(2,1)S(1)}, bf16[64,2048]{1,0:T(8,128)(2,1)S(1)}, u32[]{:S(2)}, u32[]{:S(2)}) collective-permute-start(bf16[64,2048]{1,0:T(8,128)(2,1)S(1)} %get-tuple-element.70), channel_id=1, source_target_pairs={{0,4},{4,0},{1,5},{5,1},{2,6},{6,2},{3,7},{7,3},{11,15},{15,11},{1... | collective-permute-start | bytes 786440 | tf_op jit(solution)/shard_map/ppermute | solution.py:380
  30.7 7.4 %collective-permute-start.11 = (bf16[32,2048]{1,0:T(8,128)(2,1)S(1)}, bf16[32,2048]{1,0:T(8,128)(2,1)S(1)}, u32[]{:S(2)}, u32[]{:S(2)}) collective-permute-start(bf16[32,2048]{1,0:T(8,128)(2,1)S(1)} %add_convert_fusion.3), channel_id=1, source_target_pairs={{0,9},{4,6},{1,8},{5,7},{2,0},{6,15},{3,1},{7,14},{11,2},{15,13},{... | collective-permute-start | bytes 393224 | tf_op jit(solution)/shard_map/ppermute | solution.py:378
  33.8 6.6 %collective-permute-start.15 = (bf16[64,2048]{1,0:T(8,128)(2,1)S(1)}, bf16[64,2048]{1,0:T(8,128)(2,1)S(1)}, u32[]{:S(2)}, u32[]{:S(2)}) collective-permute-start(bf16[64,2048]{1,0:T(8,128)(2,1)S(1)} %add_convert_fusion), channel_id=1, source_target_pairs={{0,8},{4,5},{1,0},{5,6},{2,1},{6,7},{3,2},{7,15},{11,3},{15,14},{1... | collective-permute-start | bytes 786440 | tf_op jit(solution)/shard_map/ppermute | solution.py:378
  38.2 6.4 %collective-permute-start.13 = (bf16[64,2048]{1,0:T(8,128)(2,1)S(1)}, bf16[64,2048]{1,0:T(8,128)(2,1)S(1)}, u32[]{:S(2)}, u32[]{:S(2)}) collective-permute-start(bf16[64,2048]{1,0:T(8,128)(2,1)S(1)} %get-tuple-element.71), channel_id=1, source_target_pairs={{0,8},{4,5},{1,0},{5,6},{2,1},{6,7},{3,2},{7,15},{11,3},{15,14},{1... | collective-permute-start | bytes 786440 | tf_op jit(solution)/shard_map/ppermute | solution.py:378
  40.5 6.0 %collective-permute-start.16 = (bf16[32,2048]{1,0:T(8,128)(2,1)S(1)}, bf16[32,2048]{1,0:T(8,128)(2,1)S(1)}, u32[]{:S(2)}, u32[]{:S(2)}) collective-permute-start(bf16[32,2048]{1,0:T(8,128)(2,1)S(1)} %get-tuple-element.73), channel_id=1, source_target_pairs={{0,9},{4,6},{1,8},{5,7},{2,0},{6,15},{3,1},{7,14},{11,2},{15,13},{... | collective-permute-start | bytes 393224 | tf_op jit(solution)/shard_map/ppermute | solution.py:378
  42.5 6.7 %collective-permute-start.17 = (bf16[32,2048]{1,0:T(8,128)(2,1)S(1)}, bf16[32,2048]{1,0:T(8,128)(2,1)S(1)}, u32[]{:S(2)}, u32[]{:S(2)}) collective-permute-start(bf16[32,2048]{1,0:T(8,128)(2,1)S(1)} %get-tuple-element.74), channel_id=1, source_target_pairs={{0,13},{4,2},{1,12},{5,3},{2,4},{6,11},{3,5},{7,10},{11,6},{15,9},... | collective-permute-start | bytes 393224 | tf_op jit(solution)/shard_map/ppermute | solution.py:379
  44.6 4.7 %collective-permute-start.14 = (bf16[32,2048]{1,0:T(8,128)(2,1)S(1)}, bf16[32,2048]{1,0:T(8,128)(2,1)S(1)}, u32[]{:S(2)}, u32[]{:S(2)}) collective-permute-start(bf16[32,2048]{1,0:T(8,128)(2,1)S(1)} %slice.67), channel_id=1, source_target_pairs={{0,4},{4,0},{1,5},{5,1},{2,6},{6,2},{3,7},{7,3},{11,15},{15,11},{1... | collective-permute-start | bytes 393224 | tf_op jit(solution)/shard_map/ppermute | solution.py:380

commit v7 on v6

--- a/solution.py
+++ b/solution.py
@@ -486,7 +486,8 @@
     fourth, nearest = tie(fourth, low(one_sum))
     close = move(nearest, -1)
     far = tie(low(far_sum[:r] + third[:r].astype(f32) + fourth.astype(f32)), join(far_sum[r:], third[r:]))
-    parts = (close[:tok_rows], swap(close[tok_rows:]), move(far[0], -2), cross(far[1], -2))
+    crossed = cross(far[1], -2)
+    parts = (close[:tok_rows], swap(close[tok_rows:]), crossed, move(far[0], -2))
     return low(sum((a.astype(f32) for a in parts), own_sum))
 
 

time: 50.2 us -> 50.3 us (level)
  waiting for transfers between devices: 17.9 us -> 16.8 us
  starting transfers between devices: 17.9 us -> 18.7 us
    ppermute x8, waiting for transfers between devices: 12.8 us -> 11.9 us  [dense_body(): move = lambda a, by: lax.ppermute(a, axes, hop(by, 0))]
    ppermute x8, starting transfers between devices: 16 us -> 16.5 us  [dense_body(): move = lambda a, by: lax.ppermute(a, axes, hop(by, 0))]
where the time goes in v7:
time: 50.3 us; the launch traced here: 49.8 us
  starting transfers between devices  18.7 us (37%)
  waiting for transfers between devices  16.8 us (33%)
  Pallas kernels  13.1 us (26%)
  other arithmetic  1.03 us (2%)
    ppermute x8, starting transfers between devices, dense_body(): move = lambda a, by: lax.ppermute(a, axes, hop(by, 0))  16.5 us
    ppermute x8, waiting for transfers between devices, dense_body(): move = lambda a, by: lax.ppermute(a, axes, hop(by, 0))  11.9 us
    pallas_call x6, Pallas kernels, run_kernel(): pl.pallas_call(kernel, out_shape=[pltpu.VMEM(shape, dtype) for shape, dty...  7.48 us
    pallas_call x1, Pallas kernels, load_weights(): pl.pallas_call(functools.partial(load_kernel, n), out_shape=[pltpu.VMEM(w...  4.48 us
    ppermute x1, waiting for transfers between devices, dense_body(): cross = lambda a, by: lax.ppermute(a, axes, hop(by, 1))  2.53 us
    ppermute x9, waiting for transfers between devices, dense_body(): swap = lambda a: lax.ppermute(a, axes, swap_pairs)  2.37 us
    ppermute x9, starting transfers between devices, dense_body(): swap = lambda a: lax.ppermute(a, axes, swap_pairs)  1.93 us
    pallas_call x1, Pallas kernels, make_message(): pl.pallas_call(message_kernel, out_shape=[pltpu.VMEM((rows, width + LANES...  1.11 us
  transfers between devices with their start and end apart: 18, of which 10 were waited for; matrix products, arithmetic and copies ran while one was open for 1% of the time, Pallas kernels for 18%

profile of v7, /device:TPU:0, one launch (start us, length us, event | category | flops | bytes accessed | tf_op | source)
XLA Modules:
  0.0 49.8 jit_solution(2206850675927393440)
XLA Ops:
  0.0 1.1 %shard_map.82 = (bf16[32,2176]{1,0:T(8,128)(2,1)S(1)}, f32[8,128]{1,0:T(8,128)S(1)}) custom-call(s32[4]{0:T(128)} %hot_list_ref.1, s32[16]{0:T(128)} %slot_ref.1, bf16[32,2048]{1,0:T(8,128)(2,1)} %tok_ref.1, s32[8,32]{1,0:T(8,128)} %bitcast.4, f32[8,32]{1,0:T(8,128)} %bitcast.5), custom_call_target="tpu_custom_call" | custom-call | tf_op jit(solution)/shard_map/pallas_call | solution.py:337
  1.1 0.5 collective-permute-start
  1.6 1.0 %collective-permute-done.other_ref = bf16[32,2176]{1,0:T(8,128)(2,1)S(1)} collective-permute-done((bf16[32,2176]{1,0:T(8,128)(2,1)S(1)}, bf16[32,2176]{1,0:T(8,128)(2,1)S(1)}, u32[]{:S(2)}, u32[]{:S(2)}) %collective-permute-start) | collective-permute-done | bytes 139296 | tf_op jit(solution)/shard_map/ppermute | solution.py:380
  2.6 4.0 %collective-permute-start.1 = (bf16[64,2176]{1,0:T(8,128)(2,1)S(1)}, bf16[64,2176]{1,0:T(8,128)(2,1)S(1)}, u32[]{:S(2)}, u32[]{:S(2)}) collective-permute-start(bf16[64,2176]{1,0:T(8,128)(2,1)S(1)} %shard_map.83.refs_3_.refs_1_), channel_id=1, source_target_pairs={{0,2},{4,13},{1,3},{5,12},{2,11},{6,4},{3,10},{7,5},{11,9},{15,6},... | collective-permute-start | bytes 835592 | tf_op jit(solution)/shard_map/ppermute | solution.py:378
  6.6 4.5 %shard_map.84 = (bf16[1,2048,1536]{2,1,0:T(8,128)(2,1)S(1)}, bf16[1,768,2048]{2,1,0:T(8,128)(2,1)S(1)}, bf16[1,3,192,2048]{3,2,1,0:T(8,128)(2,1)S(1)}) custom-call(bf16[1,2048,1536]{2,1,0:T(8,128)(2,1)} %refs_0_.1, bf16[1,768,2048]{2,1,0:T(8,128)(2,1)} %refs_1_.1, bf16[1,3,192,2048]{3,2,1,0:T(8,128)(2,1)} %bitcast.3, ...), custom_call_target="tpu_custom_call" | custom-call | bytes 11796480 | tf_op jit(solution)/shard_map/pallas_call | solution.py:320
  11.1 1.6 %collective-permute-start.4 = (bf16[64,2176]{1,0:T(8,128)(2,1)S(1)}, bf16[64,2176]{1,0:T(8,128)(2,1)S(1)}, u32[]{:S(2)}, u32[]{:S(2)}) collective-permute-start(bf16[64,2176]{1,0:T(8,128)(2,1)S(1)} %shard_map.83.refs_3_.refs_1_), channel_id=1, source_target_pairs={{0,1},{4,12},{1,2},{5,4},{2,3},{6,5},{3,11},{7,6},{11,10},{15,7},{... | collective-permute-start | bytes 835592 | tf_op jit(solution)/shard_map/ppermute | solution.py:378
  12.7 0.8 %collective-permute-done.1.refs_0_ = bf16[64,2176]{1,0:T(8,128)(2,1)S(1)} collective-permute-done((bf16[64,2176]{1,0:T(8,128)(2,1)S(1)}, bf16[64,2176]{1,0:T(8,128)(2,1)S(1)}, u32[]{:S(2)}, u32[]{:S(2)}) %collective-permute-start.1) | collective-permute-done | bytes 278560 | tf_op jit(solution)/shard_map/ppermute | solution.py:378
  13.6 0.1 collective-permute-start.5
  13.7 2.1 %collective-permute-start.3 = (bf16[64,2176]{1,0:T(8,128)(2,1)S(1)}, bf16[64,2176]{1,0:T(8,128)(2,1)S(1)}, u32[]{:S(2)}, u32[]{:S(2)}) collective-permute-start(bf16[64,2176]{1,0:T(8,128)(2,1)S(1)} %collective-permute-done.1.refs_0_), channel_id=1, source_target_pairs={{0,1},{4,12},{1,2},{5,4},{2,3},{6,5},{3,11},{7,6},{11,10},{15,7},{... | collective-permute-start | bytes 835592 | tf_op jit(solution)/shard_map/ppermute | solution.py:378
  15.8 2.9 %collective-permute-start.2 = (bf16[32,2176]{1,0:T(8,128)(2,1)S(1)}, bf16[32,2176]{1,0:T(8,128)(2,1)S(1)}, u32[]{:S(2)}, u32[]{:S(2)}) collective-permute-start(bf16[32,2176]{1,0:T(8,128)(2,1)S(1)} %slice.48), channel_id=1, source_target_pairs={{0,2},{4,13},{1,3},{5,12},{2,11},{6,4},{3,10},{7,5},{11,9},{15,6},... | collective-permute-start | bytes 417800 | tf_op jit(solution)/shard_map/ppermute | solution.py:378
  18.7 2.6 %shard_map.85 = (bf16[256,192]{1,0:T(8,128)(2,1)S(1)}, bf16[96,2048]{1,0:T(8,128)(2,1)S(1)}, bf16[256,128]{1,0:T(8,128)(2,1)S(1)}, f32[256,128]{1,0:T(8,128)S(1)}) custom-call(f32[8,128]{1,0:T(8,128)S(1)} %get-tuple-element.46.key_ref, bf16[64,2176]{1,0:T(8,128)(2,1)S(1)} %collective-permute-done.1.refs_0_, bf16[64,2176]{1,0:T(8,128)(2,1)S(1)} %shard_map.83.refs_3_.refs_1_, ...), custom_call_target="tpu_custom_call" | custom-call | flops 905969664 | bytes 2097152 | tf_op jit(solution)/shard_map/pallas_call | solution.py:306
  21.3 0.9 %shard_map.86 = (bf16[96,2048]{1,0:T(8,128)(2,1)S(1)}, f32[160,2048]{1,0:T(8,128)S(1)}) custom-call(bf16[1,3,192,2048]{3,2,1,0:T(8,128)(2,1)S(1)} %get-tuple-element.45.refs_7_.hot_ref.refs_2_.refs_6_, bf16[256,192]{1,0:T(8,128)(2,1)S(1)} %get-tuple-element.49.refs_0_, bf16[96,2048]{1,0:T(8,128)(2,1)S(1)} %get-tuple-element.50.refs_1_, ...), custom_call_target="tpu_custom_call" | custom-call | flops 301989888 | bytes 2097152 | tf_op jit(solution)/shard_map/pallas_call | solution.py:306
  22.1 1.9 %collective-permute-done.2.refs_0_ = bf16[32,2176]{1,0:T(8,128)(2,1)S(1)} collective-permute-done((bf16[32,2176]{1,0:T(8,128)(2,1)S(1)}, bf16[32,2176]{1,0:T(8,128)(2,1)S(1)}, u32[]{:S(2)}, u32[]{:S(2)}) %collective-permute-start.2) | collective-permute-done | bytes 139296 | tf_op jit(solution)/shard_map/ppermute | solution.py:378
  24.0 0.5 %collective-permute-start.9 = (bf16[64,2176]{1,0:T(8,128)(2,1)S(1)}, bf16[64,2176]{1,0:T(8,128)(2,1)S(1)}, u32[]{:S(2)}, u32[]{:S(2)}) collective-permute-start(bf16[64,2176]{1,0:T(8,128)(2,1)S(1)} %collective-permute-done.3.refs_1_), channel_id=1, source_target_pairs={{0,4},{4,0},{1,5},{5,1},{2,6},{6,2},{3,7},{7,3},{11,15},{15,11},{1... | collective-permute-start | bytes 835592 | tf_op jit(solution)/shard_map/ppermute | solution.py:380
  24.5 0.8 %shard_map.87 = (bf16[96,192]{1,0:T(8,128)(2,1)S(1)}, bf16[48,2048]{1,0:T(8,128)(2,1)S(1)}, bf16[96,128]{1,0:T(8,128)(2,1)S(1)}, f32[96,128]{1,0:T(8,128)S(1)}) custom-call(f32[8,128]{1,0:T(8,128)S(1)} %get-tuple-element.46.key_ref, bf16[32,2176]{1,0:T(8,128)(2,1)S(1)} %collective-permute-done.2.refs_0_, ...), custom_call_target="tpu_custom_call" | custom-call | flops 169869312 | bytes 786432 | tf_op jit(solution)/shard_map/pallas_call | solution.py:306
  25.3 0.9 %collective-permute-done.8.refs_1_ = bf16[32,2176]{1,0:T(8,128)(2,1)S(1)} collective-permute-done((bf16[32,2176]{1,0:T(8,128)(2,1)S(1)}, bf16[32,2176]{1,0:T(8,128)(2,1)S(1)}, u32[]{:S(2)}, u32[]{:S(2)}) %collective-permute-start.8) | collective-permute-done | bytes 139296 | tf_op jit(solution)/shard_map/ppermute | solution.py:380
  26.2 2.7 %shard_map.88 = (bf16[96,2048]{1,0:T(8,128)(2,1)S(1)}, bf16[160,192]{1,0:T(8,128)(2,1)S(1)}, bf16[48,2048]{1,0:T(8,128)(2,1)S(1)}, bf16[64,2048]{1,0:T(8,128)(2,...) custom-call(f32[8,128]{1,0:T(8,128)S(1)} %get-tuple-element.46.key_ref, ...), custom_call_target="tpu_custom_call" | custom-call | flops 1056964608 | bytes 1310720 | tf_op jit(solution)/shard_map/pallas_call | solution.py:306
  28.9 0.2 collective-permute-start.10
  29.1 0.4 collective-permute-start.6
  29.5 0.5 %shard_map.89 = (bf16[64,2048]{1,0:T(8,128)(2,1)S(1)}, f32[96,2048]{1,0:T(8,128)S(1)}) custom-call(bf16[1,3,192,2048]{3,2,1,0:T(8,128)(2,1)S(1)} %get-tuple-element.45.refs_7_.hot_ref.refs_2_.refs_6_, bf16[96,192]{1,0:T(8,128)(2,1)S(1)} %get-tuple-element.58.refs_0_, bf16[48,2048]{1,0:T(8,128)(2,1)S(1)} %get-tuple-element.61.refs_1_, ...), custom_call_target="tpu_custom_call" | custom-call | flops 188743680 | bytes 1310720 | tf_op jit(solution)/shard_map/pallas_call | solution.py:306
  30.0 0.2 collective-permute-start.12
  30.2 0.5 collective-permute-done.10
  30.7 3.0 %collective-permute-start.11 = (bf16[32,2048]{1,0:T(8,128)(2,1)S(1)}, bf16[32,2048]{1,0:T(8,128)(2,1)S(1)}, u32[]{:S(2)}, u32[]{:S(2)}) collective-permute-start(bf16[32,2048]{1,0:T(8,128)(2,1)S(1)} %add_convert_fusion.3), channel_id=1, source_target_pairs={{0,9},{4,6},{1,8},{5,7},{2,0},{6,15},{3,1},{7,14},{11,2},{15,13},{... | collective-permute-start | bytes 393224 | tf_op jit(solution)/shard_map/ppermute | solution.py:378
  34.0 4.1 %collective-permute-done.11 = bf16[32,2048]{1,0:T(8,128)(2,1)S(1)} collective-permute-done((bf16[32,2048]{1,0:T(8,128)(2,1)S(1)}, bf16[32,2048]{1,0:T(8,128)(2,1)S(1)}, u32[]{:S(2)}, u32[]{:S(2)}) %collective-permute-start.11) | collective-permute-done | bytes 131104 | tf_op jit(solution)/shard_map/ppermute | solution.py:378
  38.2 0.2 collective-permute-start.13
  38.4 2.0 %collective-permute-done.15 = bf16[64,2048]{1,0:T(8,128)(2,1)S(1)} collective-permute-done((bf16[64,2048]{1,0:T(8,128)(2,1)S(1)}, bf16[64,2048]{1,0:T(8,128)(2,1)S(1)}, u32[]{:S(2)}, u32[]{:S(2)}) %collective-permute-start.15) | collective-permute-done | bytes 262176 | tf_op jit(solution)/shard_map/ppermute | solution.py:378
  40.5 0.2 collective-permute-start.16
  40.7 2.6 %collective-permute-start.17 = (bf16[32,2048]{1,0:T(8,128)(2,1)S(1)}, bf16[32,2048]{1,0:T(8,128)(2,1)S(1)}, u32[]{:S(2)}, u32[]{:S(2)}) collective-permute-start(bf16[32,2048]{1,0:T(8,128)(2,1)S(1)} %get-tuple-element.74), channel_id=1, source_target_pairs={{0,9},{4,6},{1,8},{5,7},{2,0},{6,15},{3,1},{7,14},{11,2},{15,13},{... | collective-permute-start | bytes 393224 | tf_op jit(solution)/shard_map/ppermute | solution.py:378
  43.3 1.2 %collective-permute-done.13 = bf16[64,2048]{1,0:T(8,128)(2,1)S(1)} collective-permute-done((bf16[64,2048]{1,0:T(8,128)(2,1)S(1)}, bf16[64,2048]{1,0:T(8,128)(2,1)S(1)}, u32[]{:S(2)}, u32[]{:S(2)}) %collective-permute-start.13) | collective-permute-done | bytes 262176 | tf_op jit(solution)/shard_map/ppermute | solution.py:378
  44.6 2.5 %collective-permute-done.16 = bf16[32,2048]{1,0:T(8,128)(2,1)S(1)} collective-permute-done((bf16[32,2048]{1,0:T(8,128)(2,1)S(1)}, bf16[32,2048]{1,0:T(8,128)(2,1)S(1)}, u32[]{:S(2)}, u32[]{:S(2)}) %collective-permute-start.16) | collective-permute-done | bytes 131104 | tf_op jit(solution)/shard_map/ppermute | solution.py:379
  47.2 1.8 %collective-permute-done.17 = bf16[32,2048]{1,0:T(8,128)(2,1)S(1)} collective-permute-done((bf16[32,2048]{1,0:T(8,128)(2,1)S(1)}, bf16[32,2048]{1,0:T(8,128)(2,1)S(1)}, u32[]{:S(2)}, u32[]{:S(2)}) %collective-permute-start.17) | collective-permute-done | bytes 131104 | tf_op jit(solution)/shard_map/ppermute | solution.py:378
  49.0 0.8 %add_convert_fusion.2 = bf16[32,2048]{1,0:T(8,128)(2,1)} fusion(bf16[32,2048]{1,0:T(8,128)(2,1)S(1)} %collective-permute-done.17, bf16[32,2048]{1,0:T(8,128)(2,1)S(1)} %collective-permute-done.16, bf16[32,2048]{1,0:T(8,128)(2,1)S(1)} %collective-permute-done.14, f32[160,2048]{1,0:T(8,128)S(1)} %get-tuple-element.54, ...), kind=kLoop, calls=%fused_computation.8 | loop fusion | flops 720896 | bytes 1048576 | tf_op jit(solution)/shard_map/convert_element_type | solution.py:472
  (19 shorter events, 0.5 us)
Async XLA Ops:
  1.1 1.4 %collective-permute-start = (bf16[32,2176]{1,0:T(8,128)(2,1)S(1)}, bf16[32,2176]{1,0:T(8,128)(2,1)S(1)}, u32[]{:S(2)}, u32[]{:S(2)}) collective-permute-start(bf16[32,2176]{1,0:T(8,128)(2,1)S(1)} %get-tuple-element.40.mine_ref), channel_id=1, source_target_pairs={{0,4},{4,0},{1,5},{5,1},{2,6},{6,2},{3,7},{7,3},{11,15},{15,11},{1... | collective-permute-start | bytes 417800 | tf_op jit(solution)/shard_map/ppermute | solution.py:380
  2.6 11.0 %collective-permute-start.1 = (bf16[64,2176]{1,0:T(8,128)(2,1)S(1)}, bf16[64,2176]{1,0:T(8,128)(2,1)S(1)}, u32[]{:S(2)}, u32[]{:S(2)}) collective-permute-start(bf16[64,2176]{1,0:T(8,128)(2,1)S(1)} %shard_map.83.refs_3_.refs_1_), channel_id=1, source_target_pairs={{0,2},{4,13},{1,3},{5,12},{2,11},{6,4},{3,10},{7,5},{11,9},{15,6},... | collective-permute-start | bytes 835592 | tf_op jit(solution)/shard_map/ppermute | solution.py:378
  11.1 7.6 %collective-permute-start.4 = (bf16[64,2176]{1,0:T(8,128)(2,1)S(1)}, bf16[64,2176]{1,0:T(8,128)(2,1)S(1)}, u32[]{:S(2)}, u32[]{:S(2)}) collective-permute-start(bf16[64,2176]{1,0:T(8,128)(2,1)S(1)} %shard_map.83.refs_3_.refs_1_), channel_id=1, source_target_pairs={{0,1},{4,12},{1,2},{5,4},{2,3},{6,5},{3,11},{7,6},{11,10},{15,7},{... | collective-permute-start | bytes 835592 | tf_op jit(solution)/shard_map/ppermute | solution.py:378
  13.6 5.2 %collective-permute-start.5 = (bf16[64,2176]{1,0:T(8,128)(2,1)S(1)}, bf16[64,2176]{1,0:T(8,128)(2,1)S(1)}, u32[]{:S(2)}, u32[]{:S(2)}) collective-permute-start(bf16[64,2176]{1,0:T(8,128)(2,1)S(1)} %collective-permute-done.1.refs_0_), channel_id=1, source_target_pairs={{0,4},{4,0},{1,5},{5,1},{2,6},{6,2},{3,7},{7,3},{11,15},{15,11},{1... | collective-permute-start | bytes 835592 | tf_op jit(solution)/shard_map/ppermute | solution.py:380
  13.7 10.3 %collective-permute-start.3 = (bf16[64,2176]{1,0:T(8,128)(2,1)S(1)}, bf16[64,2176]{1,0:T(8,128)(2,1)S(1)}, u32[]{:S(2)}, u32[]{:S(2)}) collective-permute-start(bf16[64,2176]{1,0:T(8,128)(2,1)S(1)} %collective-permute-done.1.refs_0_), channel_id=1, source_target_pairs={{0,1},{4,12},{1,2},{5,4},{2,3},{6,5},{3,11},{7,6},{11,10},{15,7},{... | collective-permute-start | bytes 835592 | tf_op jit(solution)/shard_map/ppermute | solution.py:378
  15.8 8.2 %collective-permute-start.2 = (bf16[32,2176]{1,0:T(8,128)(2,1)S(1)}, bf16[32,2176]{1,0:T(8,128)(2,1)S(1)}, u32[]{:S(2)}, u32[]{:S(2)}) collective-permute-start(bf16[32,2176]{1,0:T(8,128)(2,1)S(1)} %slice.48), channel_id=1, source_target_pairs={{0,2},{4,13},{1,3},{5,12},{2,11},{6,4},{3,10},{7,5},{11,9},{15,6},... | collective-permute-start | bytes 417800 | tf_op jit(solution)/shard_map/ppermute | solution.py:378
  24.0 2.2 %collective-permute-start.7 = (bf16[64,2176]{1,0:T(8,128)(2,1)S(1)}, bf16[64,2176]{1,0:T(8,128)(2,1)S(1)}, u32[]{:S(2)}, u32[]{:S(2)}) collective-permute-start(bf16[64,2176]{1,0:T(8,128)(2,1)S(1)} %collective-permute-done.4.refs_4_), channel_id=1, source_target_pairs={{0,4},{4,0},{1,5},{5,1},{2,6},{6,2},{3,7},{7,3},{11,15},{15,11},{1... | collective-permute-start | bytes 835592 | tf_op jit(solution)/shard_map/ppermute | solution.py:380
  24.0 2.2 %collective-permute-start.9 = (bf16[64,2176]{1,0:T(8,128)(2,1)S(1)}, bf16[64,2176]{1,0:T(8,128)(2,1)S(1)}, u32[]{:S(2)}, u32[]{:S(2)}) collective-permute-start(bf16[64,2176]{1,0:T(8,128)(2,1)S(1)} %collective-permute-done.3.refs_1_), channel_id=1, source_target_pairs={{0,4},{4,0},{1,5},{5,1},{2,6},{6,2},{3,7},{7,3},{11,15},{15,11},{1... | collective-permute-start | bytes 835592 | tf_op jit(solution)/shard_map/ppermute | solution.py:380
  24.5 1.6 %collective-permute-start.8 = (bf16[32,2176]{1,0:T(8,128)(2,1)S(1)}, bf16[32,2176]{1,0:T(8,128)(2,1)S(1)}, u32[]{:S(2)}, u32[]{:S(2)}) collective-permute-start(bf16[32,2176]{1,0:T(8,128)(2,1)S(1)} %collective-permute-done.2.refs_0_), channel_id=1, source_target_pairs={{0,4},{4,0},{1,5},{5,1},{2,6},{6,2},{3,7},{7,3},{11,15},{15,11},{1... | collective-permute-start | bytes 417800 | tf_op jit(solution)/shard_map/ppermute | solution.py:380
  28.9 1.8 %collective-permute-start.10 = (bf16[96,2048]{1,0:T(8,128)(2,1)S(1)}, bf16[96,2048]{1,0:T(8,128)(2,1)S(1)}, u32[]{:S(2)}, u32[]{:S(2)}) collective-permute-start(bf16[96,2048]{1,0:T(8,128)(2,1)S(1)} %get-tuple-element.69), channel_id=1, source_target_pairs={{0,4},{4,0},{1,5},{5,1},{2,6},{6,2},{3,7},{7,3},{11,15},{15,11},{1... | collective-permute-start | bytes 1179656 | tf_op jit(solution)/shard_map/ppermute | solution.py:380
  29.1 4.8 %collective-permute-start.6 = (bf16[96,2048]{1,0:T(8,128)(2,1)S(1)}, bf16[96,2048]{1,0:T(8,128)(2,1)S(1)}, u32[]{:S(2)}, u32[]{:S(2)}) collective-permute-start(bf16[96,2048]{1,0:T(8,128)(2,1)S(1)} %get-tuple-element.55), channel_id=1, source_target_pairs={{0,4},{4,0},{1,5},{5,1},{2,6},{6,2},{3,7},{7,3},{11,15},{15,11},{1... | collective-permute-start | bytes 1179656 | tf_op jit(solution)/shard_map/ppermute | solution.py:380
  30.0 3.9 %collective-permute-start.12 = (bf16[64,2048]{1,0:T(8,128)(2,1)S(1)}, bf16[64,2048]{1,0:T(8,128)(2,1)S(1)}, u32[]{:S(2)}, u32[]{:S(2)}) collective-permute-start(bf16[64,2048]{1,0:T(8,128)(2,1)S(1)} %get-tuple-element.70), channel_id=1, source_target_pairs={{0,4},{4,0},{1,5},{5,1},{2,6},{6,2},{3,7},{7,3},{11,15},{15,11},{1... | collective-permute-start | bytes 786440 | tf_op jit(solution)/shard_map/ppermute | solution.py:380
  30.7 7.4 %collective-permute-start.11 = (bf16[32,2048]{1,0:T(8,128)(2,1)S(1)}, bf16[32,2048]{1,0:T(8,128)(2,1)S(1)}, u32[]{:S(2)}, u32[]{:S(2)}) collective-permute-start(bf16[32,2048]{1,0:T(8,128)(2,1)S(1)} %add_convert_fusion.3), channel_id=1, source_target_pairs={{0,9},{4,6},{1,8},{5,7},{2,0},{6,15},{3,1},{7,14},{11,2},{15,13},{... | collective-permute-start | bytes 393224 | tf_op jit(solution)/shard_map/ppermute | solution.py:378
  33.8 6.6 %collective-permute-start.15 = (bf16[64,2048]{1,0:T(8,128)(2,1)S(1)}, bf16[64,2048]{1,0:T(8,128)(2,1)S(1)}, u32[]{:S(2)}, u32[]{:S(2)}) collective-permute-start(bf16[64,2048]{1,0:T(8,128)(2,1)S(1)} %add_convert_fusion), channel_id=1, source_target_pairs={{0,8},{4,5},{1,0},{5,6},{2,1},{6,7},{3,2},{7,15},{11,3},{15,14},{1... | collective-permute-start | bytes 786440 | tf_op jit(solution)/shard_map/ppermute | solution.py:378
  38.2 6.4 %collective-permute-start.13 = (bf16[64,2048]{1,0:T(8,128)(2,1)S(1)}, bf16[64,2048]{1,0:T(8,128)(2,1)S(1)}, u32[]{:S(2)}, u32[]{:S(2)}) collective-permute-start(bf16[64,2048]{1,0:T(8,128)(2,1)S(1)} %get-tuple-element.71), channel_id=1, source_target_pairs={{0,8},{4,5},{1,0},{5,6},{2,1},{6,7},{3,2},{7,15},{11,3},{15,14},{1... | collective-permute-start | bytes 786440 | tf_op jit(solution)/shard_map/ppermute | solution.py:378
  40.5 6.7 %collective-permute-start.16 = (bf16[32,2048]{1,0:T(8,128)(2,1)S(1)}, bf16[32,2048]{1,0:T(8,128)(2,1)S(1)}, u32[]{:S(2)}, u32[]{:S(2)}) collective-permute-start(bf16[32,2048]{1,0:T(8,128)(2,1)S(1)} %get-tuple-element.73), channel_id=1, source_target_pairs={{0,13},{4,2},{1,12},{5,3},{2,4},{6,11},{3,5},{7,10},{11,6},{15,9},... | collective-permute-start | bytes 393224 | tf_op jit(solution)/shard_map/ppermute | solution.py:379
  40.7 8.3 %collective-permute-start.17 = (bf16[32,2048]{1,0:T(8,128)(2,1)S(1)}, bf16[32,2048]{1,0:T(8,128)(2,1)S(1)}, u32[]{:S(2)}, u32[]{:S(2)}) collective-permute-start(bf16[32,2048]{1,0:T(8,128)(2,1)S(1)} %get-tuple-element.74), channel_id=1, source_target_pairs={{0,9},{4,6},{1,8},{5,7},{2,0},{6,15},{3,1},{7,14},{11,2},{15,13},{... | collective-permute-start | bytes 393224 | tf_op jit(solution)/shard_map/ppermute | solution.py:378
  44.6 4.5 %collective-permute-start.14 = (bf16[32,2048]{1,0:T(8,128)(2,1)S(1)}, bf16[32,2048]{1,0:T(8,128)(2,1)S(1)}, u32[]{:S(2)}, u32[]{:S(2)}) collective-permute-start(bf16[32,2048]{1,0:T(8,128)(2,1)S(1)} %slice.67), channel_id=1, source_target_pairs={{0,4},{4,0},{1,5},{5,1},{2,6},{6,2},{3,7},{7,3},{11,15},{15,11},{1... | collective-permute-start | bytes 393224 | tf_op jit(solution)/shard_map/ppermute | solution.py:380

commit v8 on v6

--- a/solution.py
+++ b/solution.py
@@ -159,7 +159,7 @@
     for index in range(n):
         src, dst = refs[index], refs[n + 1 + index]
         rows = src.shape[-2]
-        parts = 4
+        parts = 2
         for part in range(parts):
             at = pl.ds(part * (rows // parts), rows // parts)
             lead = (0,) * (len(src.shape) - 2)

time: 50.2 us -> 50.2 us (level)
  no operation moved by 1% of the time
where the time goes in v8:
time: 50.2 us; the launch traced here: 50 us
  waiting for transfers between devices  17.9 us (36%)
  starting transfers between devices  17.8 us (35%)
  Pallas kernels  13.1 us (26%)
  other arithmetic  1.03 us (2%)
    ppermute x8, starting transfers between devices, dense_body(): move = lambda a, by: lax.ppermute(a, axes, hop(by, 0))  15.9 us
    ppermute x8, waiting for transfers between devices, dense_body(): move = lambda a, by: lax.ppermute(a, axes, hop(by, 0))  12.9 us
    pallas_call x6, Pallas kernels, run_kernel(): pl.pallas_call(kernel, out_shape=[pltpu.VMEM(shape, dtype) for shape, dty...  7.48 us
    pallas_call x1, Pallas kernels, load_weights(): pl.pallas_call(functools.partial(load_kernel, n), out_shape=[pltpu.VMEM(w...  4.48 us
    ppermute x1, waiting for transfers between devices, dense_body(): cross = lambda a, by: lax.ppermute(a, axes, hop(by, 1))  2.66 us
    ppermute x9, waiting for transfers between devices, dense_body(): swap = lambda a: lax.ppermute(a, axes, swap_pairs)  2.37 us
    ppermute x9, starting transfers between devices, dense_body(): swap = lambda a: lax.ppermute(a, axes, swap_pairs)  1.93 us
    pallas_call x1, Pallas kernels, make_message(): pl.pallas_call(message_kernel, out_shape=[pltpu.VMEM((rows, width + LANES...  1.11 us
  transfers between devices with their start and end apart: 18, of which 10 were waited for; matrix products, arithmetic and copies ran while one was open for 1% of the time, Pallas kernels for 18%

profile of v8, /device:TPU:0, one launch (start us, length us, event | category | flops | bytes accessed | tf_op | source)
XLA Modules:
  0.0 50.0 jit_solution(13674174627382577822)
XLA Ops:
  0.0 1.1 %shard_map.82 = (bf16[32,2176]{1,0:T(8,128)(2,1)S(1)}, f32[8,128]{1,0:T(8,128)S(1)}) custom-call(s32[4]{0:T(128)} %hot_list_ref.1, s32[16]{0:T(128)} %slot_ref.1, bf16[32,2048]{1,0:T(8,128)(2,1)} %tok_ref.1, s32[8,32]{1,0:T(8,128)} %bitcast.4, f32[8,32]{1,0:T(8,128)} %bitcast.5), custom_call_target="tpu_custom_call" | custom-call | tf_op jit(solution)/shard_map/pallas_call | solution.py:337
  1.1 0.5 collective-permute-start
  1.6 1.0 %collective-permute-done.other_ref = bf16[32,2176]{1,0:T(8,128)(2,1)S(1)} collective-permute-done((bf16[32,2176]{1,0:T(8,128)(2,1)S(1)}, bf16[32,2176]{1,0:T(8,128)(2,1)S(1)}, u32[]{:S(2)}, u32[]{:S(2)}) %collective-permute-start) | collective-permute-done | bytes 139296 | tf_op jit(solution)/shard_map/ppermute | solution.py:380
  2.6 4.0 %collective-permute-start.1 = (bf16[64,2176]{1,0:T(8,128)(2,1)S(1)}, bf16[64,2176]{1,0:T(8,128)(2,1)S(1)}, u32[]{:S(2)}, u32[]{:S(2)}) collective-permute-start(bf16[64,2176]{1,0:T(8,128)(2,1)S(1)} %shard_map.83.refs_3_.refs_1_), channel_id=1, source_target_pairs={{0,2},{4,13},{1,3},{5,12},{2,11},{6,4},{3,10},{7,5},{11,9},{15,6},... | collective-permute-start | bytes 835592 | tf_op jit(solution)/shard_map/ppermute | solution.py:378
  6.6 4.5 %shard_map.84 = (bf16[1,2048,1536]{2,1,0:T(8,128)(2,1)S(1)}, bf16[1,768,2048]{2,1,0:T(8,128)(2,1)S(1)}, bf16[1,3,192,2048]{3,2,1,0:T(8,128)(2,1)S(1)}) custom-call(bf16[1,2048,1536]{2,1,0:T(8,128)(2,1)} %refs_0_.1, bf16[1,768,2048]{2,1,0:T(8,128)(2,1)} %refs_1_.1, bf16[1,3,192,2048]{3,2,1,0:T(8,128)(2,1)} %bitcast.3, ...), custom_call_target="tpu_custom_call" | custom-call | bytes 11796480 | tf_op jit(solution)/shard_map/pallas_call | solution.py:320
  11.1 1.6 %collective-permute-start.4 = (bf16[64,2176]{1,0:T(8,128)(2,1)S(1)}, bf16[64,2176]{1,0:T(8,128)(2,1)S(1)}, u32[]{:S(2)}, u32[]{:S(2)}) collective-permute-start(bf16[64,2176]{1,0:T(8,128)(2,1)S(1)} %shard_map.83.refs_3_.refs_1_), channel_id=1, source_target_pairs={{0,1},{4,12},{1,2},{5,4},{2,3},{6,5},{3,11},{7,6},{11,10},{15,7},{... | collective-permute-start | bytes 835592 | tf_op jit(solution)/shard_map/ppermute | solution.py:378
  12.7 0.9 %collective-permute-done.1.refs_0_ = bf16[64,2176]{1,0:T(8,128)(2,1)S(1)} collective-permute-done((bf16[64,2176]{1,0:T(8,128)(2,1)S(1)}, bf16[64,2176]{1,0:T(8,128)(2,1)S(1)}, u32[]{:S(2)}, u32[]{:S(2)}) %collective-permute-start.1) | collective-permute-done | bytes 278560 | tf_op jit(solution)/shard_map/ppermute | solution.py:378
  13.6 0.1 collective-permute-start.5
  13.7 2.1 %collective-permute-start.3 = (bf16[64,2176]{1,0:T(8,128)(2,1)S(1)}, bf16[64,2176]{1,0:T(8,128)(2,1)S(1)}, u32[]{:S(2)}, u32[]{:S(2)}) collective-permute-start(bf16[64,2176]{1,0:T(8,128)(2,1)S(1)} %collective-permute-done.1.refs_0_), channel_id=1, source_target_pairs={{0,1},{4,12},{1,2},{5,4},{2,3},{6,5},{3,11},{7,6},{11,10},{15,7},{... | collective-permute-start | bytes 835592 | tf_op jit(solution)/shard_map/ppermute | solution.py:378
  15.8 2.9 %collective-permute-start.2 = (bf16[32,2176]{1,0:T(8,128)(2,1)S(1)}, bf16[32,2176]{1,0:T(8,128)(2,1)S(1)}, u32[]{:S(2)}, u32[]{:S(2)}) collective-permute-start(bf16[32,2176]{1,0:T(8,128)(2,1)S(1)} %slice.48), channel_id=1, source_target_pairs={{0,2},{4,13},{1,3},{5,12},{2,11},{6,4},{3,10},{7,5},{11,9},{15,6},... | collective-permute-start | bytes 417800 | tf_op jit(solution)/shard_map/ppermute | solution.py:378
  18.7 2.6 %shard_map.85 = (bf16[256,192]{1,0:T(8,128)(2,1)S(1)}, bf16[96,2048]{1,0:T(8,128)(2,1)S(1)}, bf16[256,128]{1,0:T(8,128)(2,1)S(1)}, f32[256,128]{1,0:T(8,128)S(1)}) custom-call(f32[8,128]{1,0:T(8,128)S(1)} %get-tuple-element.46.key_ref, bf16[64,2176]{1,0:T(8,128)(2,1)S(1)} %collective-permute-done.1.refs_0_, bf16[64,2176]{1,0:T(8,128)(2,1)S(1)} %shard_map.83.refs_3_.refs_1_, ...), custom_call_target="tpu_custom_call" | custom-call | flops 905969664 | bytes 2097152 | tf_op jit(solution)/shard_map/pallas_call | solution.py:306
  21.3 0.9 %shard_map.86 = (bf16[96,2048]{1,0:T(8,128)(2,1)S(1)}, f32[160,2048]{1,0:T(8,128)S(1)}) custom-call(bf16[1,3,192,2048]{3,2,1,0:T(8,128)(2,1)S(1)} %get-tuple-element.45.refs_7_.hot_ref.refs_2_.refs_6_, bf16[256,192]{1,0:T(8,128)(2,1)S(1)} %get-tuple-element.49.refs_0_, bf16[96,2048]{1,0:T(8,128)(2,1)S(1)} %get-tuple-element.50.refs_1_, ...), custom_call_target="tpu_custom_call" | custom-call | flops 301989888 | bytes 2097152 | tf_op jit(solution)/shard_map/pallas_call | solution.py:306
  22.1 1.9 %collective-permute-done.2.refs_0_ = bf16[32,2176]{1,0:T(8,128)(2,1)S(1)} collective-permute-done((bf16[32,2176]{1,0:T(8,128)(2,1)S(1)}, bf16[32,2176]{1,0:T(8,128)(2,1)S(1)}, u32[]{:S(2)}, u32[]{:S(2)}) %collective-permute-start.2) | collective-permute-done | bytes 139296 | tf_op jit(solution)/shard_map/ppermute | solution.py:378
  24.0 0.5 %collective-permute-start.9 = (bf16[64,2176]{1,0:T(8,128)(2,1)S(1)}, bf16[64,2176]{1,0:T(8,128)(2,1)S(1)}, u32[]{:S(2)}, u32[]{:S(2)}) collective-permute-start(bf16[64,2176]{1,0:T(8,128)(2,1)S(1)} %collective-permute-done.3.refs_1_), channel_id=1, source_target_pairs={{0,4},{4,0},{1,5},{5,1},{2,6},{6,2},{3,7},{7,3},{11,15},{15,11},{1... | collective-permute-start | bytes 835592 | tf_op jit(solution)/shard_map/ppermute | solution.py:380
  24.5 0.8 %shard_map.87 = (bf16[96,192]{1,0:T(8,128)(2,1)S(1)}, bf16[48,2048]{1,0:T(8,128)(2,1)S(1)}, bf16[96,128]{1,0:T(8,128)(2,1)S(1)}, f32[96,128]{1,0:T(8,128)S(1)}) custom-call(f32[8,128]{1,0:T(8,128)S(1)} %get-tuple-element.46.key_ref, bf16[32,2176]{1,0:T(8,128)(2,1)S(1)} %collective-permute-done.2.refs_0_, ...), custom_call_target="tpu_custom_call" | custom-call | flops 169869312 | bytes 786432 | tf_op jit(solution)/shard_map/pallas_call | solution.py:306
  25.3 0.9 %collective-permute-done.8.refs_1_ = bf16[32,2176]{1,0:T(8,128)(2,1)S(1)} collective-permute-done((bf16[32,2176]{1,0:T(8,128)(2,1)S(1)}, bf16[32,2176]{1,0:T(8,128)(2,1)S(1)}, u32[]{:S(2)}, u32[]{:S(2)}) %collective-permute-start.8) | collective-permute-done | bytes 139296 | tf_op jit(solution)/shard_map/ppermute | solution.py:380
  26.2 2.7 %shard_map.88 = (bf16[96,2048]{1,0:T(8,128)(2,1)S(1)}, bf16[160,192]{1,0:T(8,128)(2,1)S(1)}, bf16[48,2048]{1,0:T(8,128)(2,1)S(1)}, bf16[64,2048]{1,0:T(8,128)(2,...) custom-call(f32[8,128]{1,0:T(8,128)S(1)} %get-tuple-element.46.key_ref, ...), custom_call_target="tpu_custom_call" | custom-call | flops 1056964608 | bytes 1310720 | tf_op jit(solution)/shard_map/pallas_call | solution.py:306
  28.9 0.2 collective-permute-start.10
  29.1 0.4 collective-permute-start.6
  29.5 0.5 %shard_map.89 = (bf16[64,2048]{1,0:T(8,128)(2,1)S(1)}, f32[96,2048]{1,0:T(8,128)S(1)}) custom-call(bf16[1,3,192,2048]{3,2,1,0:T(8,128)(2,1)S(1)} %get-tuple-element.45.refs_7_.hot_ref.refs_2_.refs_6_, bf16[96,192]{1,0:T(8,128)(2,1)S(1)} %get-tuple-element.58.refs_0_, bf16[48,2048]{1,0:T(8,128)(2,1)S(1)} %get-tuple-element.61.refs_1_, ...), custom_call_target="tpu_custom_call" | custom-call | flops 188743680 | bytes 1310720 | tf_op jit(solution)/shard_map/pallas_call | solution.py:306
  30.0 0.2 collective-permute-start.12
  30.2 0.5 collective-permute-done.10
  30.7 3.0 %collective-permute-start.11 = (bf16[32,2048]{1,0:T(8,128)(2,1)S(1)}, bf16[32,2048]{1,0:T(8,128)(2,1)S(1)}, u32[]{:S(2)}, u32[]{:S(2)}) collective-permute-start(bf16[32,2048]{1,0:T(8,128)(2,1)S(1)} %add_convert_fusion.3), channel_id=1, source_target_pairs={{0,9},{4,6},{1,8},{5,7},{2,0},{6,15},{3,1},{7,14},{11,2},{15,13},{... | collective-permute-start | bytes 393224 | tf_op jit(solution)/shard_map/ppermute | solution.py:378
  33.9 0.1 add_convert_fusion.1
  34.0 4.1 %collective-permute-done.11 = bf16[32,2048]{1,0:T(8,128)(2,1)S(1)} collective-permute-done((bf16[32,2048]{1,0:T(8,128)(2,1)S(1)}, bf16[32,2048]{1,0:T(8,128)(2,1)S(1)}, u32[]{:S(2)}, u32[]{:S(2)}) %collective-permute-start.11) | collective-permute-done | bytes 131104 | tf_op jit(solution)/shard_map/ppermute | solution.py:378
  38.2 0.2 collective-permute-start.13
  38.3 2.1 %collective-permute-done.15 = bf16[64,2048]{1,0:T(8,128)(2,1)S(1)} collective-permute-done((bf16[64,2048]{1,0:T(8,128)(2,1)S(1)}, bf16[64,2048]{1,0:T(8,128)(2,1)S(1)}, u32[]{:S(2)}, u32[]{:S(2)}) %collective-permute-start.15) | collective-permute-done | bytes 262176 | tf_op jit(solution)/shard_map/ppermute | solution.py:378
  40.5 2.0 %collective-permute-start.16 = (bf16[32,2048]{1,0:T(8,128)(2,1)S(1)}, bf16[32,2048]{1,0:T(8,128)(2,1)S(1)}, u32[]{:S(2)}, u32[]{:S(2)}) collective-permute-start(bf16[32,2048]{1,0:T(8,128)(2,1)S(1)} %get-tuple-element.73), channel_id=1, source_target_pairs={{0,9},{4,6},{1,8},{5,7},{2,0},{6,15},{3,1},{7,14},{11,2},{15,13},{... | collective-permute-start | bytes 393224 | tf_op jit(solution)/shard_map/ppermute | solution.py:378
  42.5 2.0 %collective-permute-done.13 = bf16[64,2048]{1,0:T(8,128)(2,1)S(1)} collective-permute-done((bf16[64,2048]{1,0:T(8,128)(2,1)S(1)}, bf16[64,2048]{1,0:T(8,128)(2,1)S(1)}, u32[]{:S(2)}, u32[]{:S(2)}) %collective-permute-start.13) | collective-permute-done | bytes 262176 | tf_op jit(solution)/shard_map/ppermute | solution.py:378
  44.6 1.9 %collective-permute-done.16 = bf16[32,2048]{1,0:T(8,128)(2,1)S(1)} collective-permute-done((bf16[32,2048]{1,0:T(8,128)(2,1)S(1)}, bf16[32,2048]{1,0:T(8,128)(2,1)S(1)}, u32[]{:S(2)}, u32[]{:S(2)}) %collective-permute-start.16) | collective-permute-done | bytes 131104 | tf_op jit(solution)/shard_map/ppermute | solution.py:378
  46.5 2.7 %collective-permute-done.17 = bf16[32,2048]{1,0:T(8,128)(2,1)S(1)} collective-permute-done((bf16[32,2048]{1,0:T(8,128)(2,1)S(1)}, bf16[32,2048]{1,0:T(8,128)(2,1)S(1)}, u32[]{:S(2)}, u32[]{:S(2)}) %collective-permute-start.17) | collective-permute-done | bytes 131104 | tf_op jit(solution)/shard_map/ppermute | solution.py:379
  49.2 0.8 %add_convert_fusion.2 = bf16[32,2048]{1,0:T(8,128)(2,1)} fusion(bf16[32,2048]{1,0:T(8,128)(2,1)S(1)} %collective-permute-done.17, bf16[32,2048]{1,0:T(8,128)(2,1)S(1)} %collective-permute-done.16, bf16[32,2048]{1,0:T(8,128)(2,1)S(1)} %collective-permute-done.14, f32[160,2048]{1,0:T(8,128)S(1)} %get-tuple-element.54, ...), kind=kLoop, calls=%fused_computation.8 | loop fusion | flops 720896 | bytes 1048576 | tf_op jit(solution)/shard_map/convert_element_type | solution.py:472
  (19 shorter events, 0.4 us)
Async XLA Ops:
  1.1 1.4 %collective-permute-start = (bf16[32,2176]{1,0:T(8,128)(2,1)S(1)}, bf16[32,2176]{1,0:T(8,128)(2,1)S(1)}, u32[]{:S(2)}, u32[]{:S(2)}) collective-permute-start(bf16[32,2176]{1,0:T(8,128)(2,1)S(1)} %get-tuple-element.40.mine_ref), channel_id=1, source_target_pairs={{0,4},{4,0},{1,5},{5,1},{2,6},{6,2},{3,7},{7,3},{11,15},{15,11},{1... | collective-permute-start | bytes 417800 | tf_op jit(solution)/shard_map/ppermute | solution.py:380
  2.6 11.0 %collective-permute-start.1 = (bf16[64,2176]{1,0:T(8,128)(2,1)S(1)}, bf16[64,2176]{1,0:T(8,128)(2,1)S(1)}, u32[]{:S(2)}, u32[]{:S(2)}) collective-permute-start(bf16[64,2176]{1,0:T(8,128)(2,1)S(1)} %shard_map.83.refs_3_.refs_1_), channel_id=1, source_target_pairs={{0,2},{4,13},{1,3},{5,12},{2,11},{6,4},{3,10},{7,5},{11,9},{15,6},... | collective-permute-start | bytes 835592 | tf_op jit(solution)/shard_map/ppermute | solution.py:378
  11.1 7.6 %collective-permute-start.4 = (bf16[64,2176]{1,0:T(8,128)(2,1)S(1)}, bf16[64,2176]{1,0:T(8,128)(2,1)S(1)}, u32[]{:S(2)}, u32[]{:S(2)}) collective-permute-start(bf16[64,2176]{1,0:T(8,128)(2,1)S(1)} %shard_map.83.refs_3_.refs_1_), channel_id=1, source_target_pairs={{0,1},{4,12},{1,2},{5,4},{2,3},{6,5},{3,11},{7,6},{11,10},{15,7},{... | collective-permute-start | bytes 835592 | tf_op jit(solution)/shard_map/ppermute | solution.py:378
  13.6 5.2 %collective-permute-start.5 = (bf16[64,2176]{1,0:T(8,128)(2,1)S(1)}, bf16[64,2176]{1,0:T(8,128)(2,1)S(1)}, u32[]{:S(2)}, u32[]{:S(2)}) collective-permute-start(bf16[64,2176]{1,0:T(8,128)(2,1)S(1)} %collective-permute-done.1.refs_0_), channel_id=1, source_target_pairs={{0,4},{4,0},{1,5},{5,1},{2,6},{6,2},{3,7},{7,3},{11,15},{15,11},{1... | collective-permute-start | bytes 835592 | tf_op jit(solution)/shard_map/ppermute | solution.py:380
  13.7 10.3 %collective-permute-start.3 = (bf16[64,2176]{1,0:T(8,128)(2,1)S(1)}, bf16[64,2176]{1,0:T(8,128)(2,1)S(1)}, u32[]{:S(2)}, u32[]{:S(2)}) collective-permute-start(bf16[64,2176]{1,0:T(8,128)(2,1)S(1)} %collective-permute-done.1.refs_0_), channel_id=1, source_target_pairs={{0,1},{4,12},{1,2},{5,4},{2,3},{6,5},{3,11},{7,6},{11,10},{15,7},{... | collective-permute-start | bytes 835592 | tf_op jit(solution)/shard_map/ppermute | solution.py:378
  15.8 8.2 %collective-permute-start.2 = (bf16[32,2176]{1,0:T(8,128)(2,1)S(1)}, bf16[32,2176]{1,0:T(8,128)(2,1)S(1)}, u32[]{:S(2)}, u32[]{:S(2)}) collective-permute-start(bf16[32,2176]{1,0:T(8,128)(2,1)S(1)} %slice.48), channel_id=1, source_target_pairs={{0,2},{4,13},{1,3},{5,12},{2,11},{6,4},{3,10},{7,5},{11,9},{15,6},... | collective-permute-start | bytes 417800 | tf_op jit(solution)/shard_map/ppermute | solution.py:378
  24.0 2.2 %collective-permute-start.7 = (bf16[64,2176]{1,0:T(8,128)(2,1)S(1)}, bf16[64,2176]{1,0:T(8,128)(2,1)S(1)}, u32[]{:S(2)}, u32[]{:S(2)}) collective-permute-start(bf16[64,2176]{1,0:T(8,128)(2,1)S(1)} %collective-permute-done.4.refs_4_), channel_id=1, source_target_pairs={{0,4},{4,0},{1,5},{5,1},{2,6},{6,2},{3,7},{7,3},{11,15},{15,11},{1... | collective-permute-start | bytes 835592 | tf_op jit(solution)/shard_map/ppermute | solution.py:380
  24.0 2.2 %collective-permute-start.9 = (bf16[64,2176]{1,0:T(8,128)(2,1)S(1)}, bf16[64,2176]{1,0:T(8,128)(2,1)S(1)}, u32[]{:S(2)}, u32[]{:S(2)}) collective-permute-start(bf16[64,2176]{1,0:T(8,128)(2,1)S(1)} %collective-permute-done.3.refs_1_), channel_id=1, source_target_pairs={{0,4},{4,0},{1,5},{5,1},{2,6},{6,2},{3,7},{7,3},{11,15},{15,11},{1... | collective-permute-start | bytes 835592 | tf_op jit(solution)/shard_map/ppermute | solution.py:380
  24.5 1.6 %collective-permute-start.8 = (bf16[32,2176]{1,0:T(8,128)(2,1)S(1)}, bf16[32,2176]{1,0:T(8,128)(2,1)S(1)}, u32[]{:S(2)}, u32[]{:S(2)}) collective-permute-start(bf16[32,2176]{1,0:T(8,128)(2,1)S(1)} %collective-permute-done.2.refs_0_), channel_id=1, source_target_pairs={{0,4},{4,0},{1,5},{5,1},{2,6},{6,2},{3,7},{7,3},{11,15},{15,11},{1... | collective-permute-start | bytes 417800 | tf_op jit(solution)/shard_map/ppermute | solution.py:380
  28.9 1.8 %collective-permute-start.10 = (bf16[96,2048]{1,0:T(8,128)(2,1)S(1)}, bf16[96,2048]{1,0:T(8,128)(2,1)S(1)}, u32[]{:S(2)}, u32[]{:S(2)}) collective-permute-start(bf16[96,2048]{1,0:T(8,128)(2,1)S(1)} %get-tuple-element.69), channel_id=1, source_target_pairs={{0,4},{4,0},{1,5},{5,1},{2,6},{6,2},{3,7},{7,3},{11,15},{15,11},{1... | collective-permute-start | bytes 1179656 | tf_op jit(solution)/shard_map/ppermute | solution.py:380
  29.1 4.8 %collective-permute-start.6 = (bf16[96,2048]{1,0:T(8,128)(2,1)S(1)}, bf16[96,2048]{1,0:T(8,128)(2,1)S(1)}, u32[]{:S(2)}, u32[]{:S(2)}) collective-permute-start(bf16[96,2048]{1,0:T(8,128)(2,1)S(1)} %get-tuple-element.55), channel_id=1, source_target_pairs={{0,4},{4,0},{1,5},{5,1},{2,6},{6,2},{3,7},{7,3},{11,15},{15,11},{1... | collective-permute-start | bytes 1179656 | tf_op jit(solution)/shard_map/ppermute | solution.py:380
  30.0 3.9 %collective-permute-start.12 = (bf16[64,2048]{1,0:T(8,128)(2,1)S(1)}, bf16[64,2048]{1,0:T(8,128)(2,1)S(1)}, u32[]{:S(2)}, u32[]{:S(2)}) collective-permute-start(bf16[64,2048]{1,0:T(8,128)(2,1)S(1)} %get-tuple-element.70), channel_id=1, source_target_pairs={{0,4},{4,0},{1,5},{5,1},{2,6},{6,2},{3,7},{7,3},{11,15},{15,11},{1... | collective-permute-start | bytes 786440 | tf_op jit(solution)/shard_map/ppermute | solution.py:380
  30.7 7.4 %collective-permute-start.11 = (bf16[32,2048]{1,0:T(8,128)(2,1)S(1)}, bf16[32,2048]{1,0:T(8,128)(2,1)S(1)}, u32[]{:S(2)}, u32[]{:S(2)}) collective-permute-start(bf16[32,2048]{1,0:T(8,128)(2,1)S(1)} %add_convert_fusion.3), channel_id=1, source_target_pairs={{0,9},{4,6},{1,8},{5,7},{2,0},{6,15},{3,1},{7,14},{11,2},{15,13},{... | collective-permute-start | bytes 393224 | tf_op jit(solution)/shard_map/ppermute | solution.py:378
  33.8 6.6 %collective-permute-start.15 = (bf16[64,2048]{1,0:T(8,128)(2,1)S(1)}, bf16[64,2048]{1,0:T(8,128)(2,1)S(1)}, u32[]{:S(2)}, u32[]{:S(2)}) collective-permute-start(bf16[64,2048]{1,0:T(8,128)(2,1)S(1)} %add_convert_fusion), channel_id=1, source_target_pairs={{0,8},{4,5},{1,0},{5,6},{2,1},{6,7},{3,2},{7,15},{11,3},{15,14},{1... | collective-permute-start | bytes 786440 | tf_op jit(solution)/shard_map/ppermute | solution.py:378
  38.2 6.4 %collective-permute-start.13 = (bf16[64,2048]{1,0:T(8,128)(2,1)S(1)}, bf16[64,2048]{1,0:T(8,128)(2,1)S(1)}, u32[]{:S(2)}, u32[]{:S(2)}) collective-permute-start(bf16[64,2048]{1,0:T(8,128)(2,1)S(1)} %get-tuple-element.71), channel_id=1, source_target_pairs={{0,8},{4,5},{1,0},{5,6},{2,1},{6,7},{3,2},{7,15},{11,3},{15,14},{1... | collective-permute-start | bytes 786440 | tf_op jit(solution)/shard_map/ppermute | solution.py:378
  40.5 6.0 %collective-permute-start.16 = (bf16[32,2048]{1,0:T(8,128)(2,1)S(1)}, bf16[32,2048]{1,0:T(8,128)(2,1)S(1)}, u32[]{:S(2)}, u32[]{:S(2)}) collective-permute-start(bf16[32,2048]{1,0:T(8,128)(2,1)S(1)} %get-tuple-element.73), channel_id=1, source_target_pairs={{0,9},{4,6},{1,8},{5,7},{2,0},{6,15},{3,1},{7,14},{11,2},{15,13},{... | collective-permute-start | bytes 393224 | tf_op jit(solution)/shard_map/ppermute | solution.py:378
  42.5 6.7 %collective-permute-start.17 = (bf16[32,2048]{1,0:T(8,128)(2,1)S(1)}, bf16[32,2048]{1,0:T(8,128)(2,1)S(1)}, u32[]{:S(2)}, u32[]{:S(2)}) collective-permute-start(bf16[32,2048]{1,0:T(8,128)(2,1)S(1)} %get-tuple-element.74), channel_id=1, source_target_pairs={{0,13},{4,2},{1,12},{5,3},{2,4},{6,11},{3,5},{7,10},{11,6},{15,9},... | collective-permute-start | bytes 393224 | tf_op jit(solution)/shard_map/ppermute | solution.py:379
  44.6 4.6 %collective-permute-start.14 = (bf16[32,2048]{1,0:T(8,128)(2,1)S(1)}, bf16[32,2048]{1,0:T(8,128)(2,1)S(1)}, u32[]{:S(2)}, u32[]{:S(2)}) collective-permute-start(bf16[32,2048]{1,0:T(8,128)(2,1)S(1)} %slice.67), channel_id=1, source_target_pairs={{0,4},{4,0},{1,5},{5,1},{2,6},{6,2},{3,7},{7,3},{11,15},{15,11},{1... | collective-permute-start | bytes 393224 | tf_op jit(solution)/shard_map/ppermute | solution.py:380
